TPU v7x, 256 devices: a whole 4x4x8 slice. The times are simulated.
256 devices in a mesh: dp: 32 (over z, x), mp: 8 (over y, core).
Axes of the slice: x: 4, y: 4, z: 8, core: 2. Of those that a mesh axis runs over, the one named last changes fastest.
Arguments:
- activations: bfloat16 [32, 1024, 3072], P('dp', 'mp'), may hold values from -6 to 6
- cotangent: bfloat16 [32, 1024, 3072], P('dp', None, 'mp'), may hold values from -0.19921875 to 0.19921875
- weight: bfloat16 [3072, 3072], P(None, 'mp'), may hold values from -3 to 3
- feedback: bfloat16 [32, 3072, 3072], P('dp', None, 'mp'), may hold values from -3 to 3
- q_previous: float32 [3072, 64], P('mp'), may hold values from -6 to 6
Outputs:
- input_grad: bfloat16 [32, 1024, 3072], P('dp', 'mp')
- p_basis: float32 [3072, 64], replicated
- q_factor: float32 [3072, 64], P('mp')
- feedback_new: bfloat16 [32, 3072, 3072], P('dp', None, 'mp')
All inputs are finite; a program needn't handle non-finite values.
Results may differ from a plain program's by a relative error of at most 0.02.
Values may be sent and summed in bfloat16 or wider, within the bound.
No kernel may reach another device: no remote copies, remote signals or barrier semaphores. Data moves between devices by JAX's collectives and lax.ppermute only.
A program may use at most 128 MiB of HBM per device.

v0:
```python
import jax
import jax.numpy as jnp
from jax import lax
from jax.sharding import PartitionSpec as P


def orthonormal(factor, gram_matrix):
    lower_factor = jnp.linalg.cholesky(gram_matrix)
    return lax.linalg.triangular_solve(
        lower_factor, factor, left_side=False, lower=True, transpose_a=True
    )


def local(activations, cotangent, weight, feedback, q_previous):
    act_shard = activations[0]
    cot_rows = cotangent[0]
    old_feedback = feedback[0]
    cot_block = cot_rows
    gradient = lax.dot_general(
        lax.all_gather(act_shard, "mp", axis=0, tiled=True),
        cot_block,
        (((0,), (0,)), ((), ())),
        preferred_element_type=jnp.float32,
    )
    merged = (gradient + old_feedback.astype(jnp.float32)).astype(jnp.bfloat16)
    q_low = q_previous.astype(jnp.bfloat16)
    p_summed = lax.psum(jnp.dot(merged, q_low, preferred_element_type=jnp.float32), ("dp", "mp"))
    gram_matrix = jnp.dot(
        p_summed.T, p_summed, precision=lax.Precision.HIGHEST, preferred_element_type=jnp.float32
    )
    p_basis = orthonormal(p_summed, gram_matrix)
    basis_low = p_basis.astype(jnp.bfloat16)
    q_part = lax.dot_general(
        merged, basis_low, (((0,), (0,)), ((), ())), preferred_element_type=jnp.float32
    )
    q_factor = lax.psum(q_part.astype(jnp.bfloat16), "dp").astype(jnp.float32) / lax.axis_size("dp")
    approx = jnp.dot(
        p_basis, q_factor.T, precision=lax.Precision.HIGHEST, preferred_element_type=jnp.float32
    )
    feedback_new = (merged.astype(jnp.float32) - approx).astype(jnp.bfloat16)
    cot_block = cot_rows
    input_grad = lax.psum_scatter(
        lax.dot_general(
            cot_block, weight, (((1,), (1,)), ((), ())), preferred_element_type=jnp.float32
        ),
        "mp",
        scatter_dimension=0,
        tiled=True,
    ).astype(jnp.bfloat16)
    return (input_grad[None], p_basis, q_factor, feedback_new[None])


def solution(mesh):
    placed = (
        P("dp", "mp", None),
        P("dp", None, "mp"),
        P(None, "mp"),
        P("dp", None, "mp"),
        P("mp", None),
    )
    return jax.shard_map(
        local,
        mesh=mesh,
        in_specs=placed,
        out_specs=(P("dp", "mp", None), P(), P("mp", None), P("dp", None, "mp")),
        check_vma=False,
    )
```

profile of v0, /device:TPU:8, one launch (start us, length us, event | category | flops | bytes accessed | tf_op | source)
XLA Modules:
  0.0 496.6 jit_solution(1968175758639679522)
XLA Ops:
  7.2 0.0 all-gather.3.cloned.1.call-start
  7.2 0.7 all-gather.3.cloned.1.call-update
  7.9 0.0 all-reduce.2.cloned.1.call-start
  8.0 47.4 %all-gather.3.cloned.1.call-done = bf16[1,1024,3072]{2,1,0:T(8,128)(2,1)} async-done(((bf16[1,128,3072]{2,1,0:T(8,128)(2,1)}), bf16[1,1024,3072]{2,1,0:T(8,128)(2,1)}) %all-gather.3.cloned.1.call-update) | async-done | bytes 6291472 | tf_op jit(solution)/shard_map/all_gather | solution.py:20
  55.3 7.2 %fusion.2 = bf16[3072,384]{1,0:T(8,128)(2,1)S(1)} fusion(bf16[1,1024,3072]{2,1,0:T(8,128)(2,1)} %all-gather.3.cloned.1.call-done, bf16[1,3072,384]{2,1,0:T(8,128)(2,1)} %param.8, bf16[1,1024,384]{2,1,0:T(8,128)(2,1)} %param.6), kind=kOutput, calls=%fused_computation.3 | convolution fusion | flops 2419458048 | bytes 11796480 | tf_op jit(solution)/shard_map/dot_general | solution.py:19
  62.5 1.4 copy-done.1
  63.9 1.7 fusion.10
  65.7 0.0 all-reduce.2.cloned.1.call-update
  65.7 0.0 reduce-scatter.2.cloned.1.call-start
  65.8 6.4 %fusion.7 = f32[1024,3072]{1,0:T(8,128)} fusion(bf16[3072,384]{1,0:T(8,128)(2,1)S(1)} %copy-done, bf16[1,1024,384]{2,1,0:T(8,128)(2,1)S(1)} %copy-done.4), kind=kOutput, calls=%fused_computation.8 | convolution fusion | flops 2415919104 | bytes 15728640 | tf_op jit(solution)/shard_map/dot_general | solution.py:43
  72.2 0.0 reduce-scatter.2.cloned.1.call-update
  72.2 248.8 %all-reduce.2.cloned.1.call-done = f32[3072,64]{0,1:T(8,128)} async-done(((f32[3072,64]{0,1:T(8,128)}), f32[3072,64]{0,1:T(8,128)}) %all-reduce.2.cloned.1.call-update) | async-done | bytes 786448 | tf_op jit(solution)/shard_map/psum | solution.py:27
  321.0 2.2 fusion.16
  323.2 0.1 copy.9
  323.3 5.8 %cholesky.16 = f32[64,64]{1,0:T(8,128)S(1)} custom-call(f32[64,64]{1,0:T(8,128)S(1)} %fusion.15), custom_call_target="Cholesky" | custom-call | tf_op jit(solution)/shard_map/jit(cholesky)/cholesky | solution.py:8
  329.2 0.6 compare_reduce_fusion
  329.8 0.7 fusion.12
  330.5 4.9 custom-call.6
  335.4 0.8 fusion.13
  336.2 0.9 copy-done.3
  337.1 2.2 convolution_convert_fusion
  339.3 140.5 %psum.15 = bf16[384,64]{0,1:T(8,128)(2,1)S(1)} all-reduce(bf16[384,64]{0,1:T(8,128)(2,1)S(1)} %convolution_convert_fusion), channel_id=1, replica_groups=mesh['dp'=32,'mp'=8] {'dp'}, use_global_device_ids=true, to_apply=%region_4.5 | all-reduce | flops 24576 | bytes 98304 | tf_op jit(solution)/shard_map/psum | solution.py:36
  479.8 7.9 %fusion.5 = bf16[1,3072,384]{2,1,0:T(8,128)(2,1)} fusion(f32[3072,64]{0,1:T(8,128)} %copy-done.3, f32[384,64]{0,1:T(8,128)S(1)} %convert_multiply_fusion, bf16[3072,384]{1,0:T(8,128)(2,1)} %copy-done.1), kind=kOutput, calls=%fused_computation.5 | convolution fusion | flops 909508608 | bytes 5603328 | tf_op jit(solution)/shard_map/dot_general | solution.py:37
  487.7 2.4 convert_bitcast_fusion
  (16 shorter events, 0.1 us)
Async XLA Ops:
  7.2 58.6 %copy-start = (bf16[3072,384]{1,0:T(8,128)(2,1)S(1)}, bf16[3072,384]{1,0:T(8,128)(2,1)}, u32[]{:S(2)}) copy-start(bf16[3072,384]{1,0:T(8,128)(2,1)} %param.7) | copy-start | bytes 7077892
  7.2 48.1 %all-gather.3.cloned.1.call-start = ((), (), s32[]{:S(2)}) async-start(), calls=%async_computation.3 | async-start | bytes 7077888 | tf_op jit(solution)/shard_map/all_gather | solution.py:20
  7.9 56.0 %copy-start.6 = (f32[384,64]{0,1:T(8,128)S(1)}, f32[384,64]{0,1:T(8,128)}, u32[]{:S(2)}) copy-start(f32[384,64]{0,1:T(8,128)} %param.9) | copy-start | bytes 294916
  7.9 313.1 %all-reduce.2.cloned.1.call-start = ((), (), s32[]{:S(2)}) async-start(), calls=%async_computation.2 | async-start | bytes 1572864 | tf_op jit(solution)/shard_map/psum | solution.py:27
  62.5 1.4 copy-start.1
  63.9 1.8 copy-start.4
  65.7 422.0 %reduce-scatter.2.cloned.1.call-start = ((), (), s32[]{:S(2)}) async-start(), calls=%async_computation.1 | async-start | bytes 14155776 | tf_op jit(solution)/shard_map/reduce_scatter | solution.py:42
  321.0 14.4 %copy-start.2 = (f32[3072,64]{0,1:T(8,128)S(1)}, f32[3072,64]{0,1:T(8,128)}, u32[]{:S(2)}) copy-start(f32[3072,64]{0,1:T(8,128)} %all-reduce.2.cloned.1.call-done) | copy-start | bytes 2359300
  336.2 0.9 copy-start.3
  479.8 7.9 %copy-start.5 = (f32[384,64]{0,1:T(8,128)}, f32[384,64]{0,1:T(8,128)S(1)}, u32[]{:S(2)}) copy-start(f32[384,64]{0,1:T(8,128)S(1)} %convert_multiply_fusion) | copy-start | bytes 294916
Sparse Core Ops, SparseCore 0:
  9.8 45.4 all-gather.2
  65.8 255.1 all-reduce.1
  323.7 71.3 reduce-scatter.1
where the time goes:
time: 497 us
  waiting for transfers between devices  297 us (60%)
  blocking collectives  140 us (28%)
  matrix products  28.5 us (6%)
  other arithmetic  14.5 us (3%)
  between operations  13.9 us (3%)
    psum x1, waiting for transfers between devices, local(): lax.psum(jnp.dot(merged, q_low, preferred_element_type=jnp.float32), ('dp...  249 us
    psum x1, blocking collectives, local(): lax.psum(q_part.astype(jnp.bfloat16), 'dp').astype(jnp.float32)  140 us
    all_gather x1, waiting for transfers between devices, local(): lax.all_gather(act_shard, 'mp', axis=0, tiled=True)  47.4 us
  transfers between devices with their start and end apart: 3, of which 2 were waited for; matrix products, arithmetic and copies ran while one was open for 6% of the time, Pallas kernels for 0%

commit v1 on v0

v1 whole, which is shorter than its diff:
```python
import functools

import jax
import jax.numpy as jnp
from jax import lax
from jax.experimental import pallas as pl
from jax.experimental.pallas import tpu as pltpu
from jax.sharding import Mesh, PartitionSpec as P

F32 = jnp.float32
BF16 = jnp.bfloat16
NX, NY, NZ, NC = 4, 4, 8, 2
MP = ("y", "c")
XYC = ("x", "y", "c")


def ring(value, axis, size, shift):
    return lax.ppermute(value, axis, [(i, (i + shift) % size) for i in range(size)])


def exchange(value, axes):
    return lax.all_to_all(value, axes, 0, 0, tiled=True)


def spread(value, axes, count):
    return exchange(jnp.broadcast_to(value[None], (count,) + value.shape), axes)


def split(value):
    high = lax.reduce_precision(value, 8, 7)
    return high.astype(BF16), (value - high).astype(BF16)


def merge_kernel(*refs):
    acts, cot_ref, old_ref, out_ref = refs[:8], refs[8], refs[9], refs[10]
    rows = jnp.concatenate([ref[...] for ref in acts], axis=0)
    gradient = lax.dot_general(
        rows, cot_ref[...], (((0,), (0,)), ((), ())), preferred_element_type=F32
    )
    out_ref[...] = (gradient + old_ref[...].astype(F32)).astype(BF16)


def merge(acts, cot_rel, old_feedback):
    d, cols = old_feedback.shape
    rows = acts[0].shape[0]
    tile = 512
    return pl.pallas_call(
        merge_kernel,
        grid=(d // tile,),
        in_specs=[pl.BlockSpec((rows, tile), lambda i: (0, i))] * 8
        + [
            pl.BlockSpec(cot_rel.shape, lambda i: (0, 0)),
            pl.BlockSpec((tile, cols), lambda i: (i, 0)),
        ],
        out_specs=pl.BlockSpec((tile, cols), lambda i: (i, 0)),
        out_shape=jax.ShapeDtypeStruct((d, cols), BF16),
        compiler_params=pltpu.CompilerParams(vmem_limit_bytes=32 * 2**20),
        cost_estimate=pl.CostEstimate(
            flops=2 * d * cols * rows * 8, bytes_accessed=12 * 2**20, transcendentals=0
        ),
    )(*acts, cot_rel, old_feedback)


def local(activations, cotangent, weight, feedback, q_previous):
    act, cot, old = activations[0], cotangent[0], feedback[0]
    y, c = lax.axis_index("y"), lax.axis_index("c")
    cot_blocks = cot.reshape(NY, NC, 128, 384)

    same = [act] + [ring(act, "y", NY, k) for k in (1, 3, 2)]
    other = [ring(value, "c", NC, 1) for value in same]
    acts = [value for pair in zip(same, other) for value in pair]
    from_y = [(y - k) % NY for k in (0, 1, 3, 2)]
    cot_rel = jnp.concatenate(
        [cot_blocks[yy, cc] for yy in from_y for cc in (c, 1 - c)], axis=0
    )

    q_low = q_previous.astype(BF16)
    t_part = jnp.dot(cot, q_low, preferred_element_type=F32)
    t_send = t_part.reshape(8, 2, 64, 64).transpose(0, 2, 1, 3).reshape(8, 64, 128)
    t_sum = exchange(t_send, MP).sum(0)
    t_rows = jnp.concatenate([t_sum[:, :64], t_sum[:, 64:]], axis=0)
    t_high, t_low = split(t_rows)
    contract = (((0,), (0,)), ((), ()))
    p_part = (
        lax.dot_general(act, t_high, contract, preferred_element_type=F32)
        + lax.dot_general(act, t_low, contract, preferred_element_type=F32)
        + jnp.dot(old, q_low, preferred_element_type=F32)
    )
    p_send = jnp.concatenate([p_part[:1536], p_part[1536:]], axis=1).reshape(32, 48, 128)
    p_chunk = exchange(p_send, XYC).sum(0)
    p_chunk = exchange(jnp.broadcast_to(p_chunk[None], (NZ, 48, 128)), "z").sum(0)
    p_all = spread(p_chunk, XYC, 32).reshape(1536, 128)
    p_summed = jnp.concatenate([p_all[:, :64], p_all[:, 64:]], axis=0)

    merged = merge(acts, cot_rel, old)

    p_high, p_low = split(p_summed)
    s_part = lax.dot_general(p_high, merged, contract, preferred_element_type=F32)
    s_part += lax.dot_general(p_low, merged, contract, preferred_element_type=F32)
    s_send = s_part.reshape(64, 3, 128).transpose(1, 0, 2).reshape(NX, 48, 128)
    s_chunk = exchange(s_send, "x").sum(0)
    s_chunk = spread(s_chunk, "z", NZ).sum(0)
    s_all = spread(s_chunk, "x", NX).reshape(3, 64, 128).transpose(1, 0, 2).reshape(64, 384)

    gram_matrix = jnp.dot(
        p_summed.T, p_summed, precision=lax.Precision.HIGHEST, preferred_element_type=F32
    )
    lower_factor = jnp.linalg.cholesky(gram_matrix)
    p_basis = lax.linalg.triangular_solve(
        lower_factor, p_summed, left_side=False, lower=True, transpose_a=True
    )
    q_t = lax.linalg.triangular_solve(lower_factor, s_all, left_side=True, lower=True) / 32
    approx = jnp.dot(p_basis, q_t, precision=lax.Precision.HIGHEST, preferred_element_type=F32)
    feedback_new = (merged.astype(F32) - approx).astype(BF16)

    to_t = (((1,), (1,)), ((), ()))
    for_other = lax.dot_general(
        cot_blocks[:, 1 - c].reshape(512, 384), weight, to_t, preferred_element_type=F32
    ).astype(BF16)
    got = ring(for_other, "c", NC, 1)
    mine = lax.dot_general(
        cot_blocks[:, c].reshape(512, 384), weight, to_t, preferred_element_type=F32
    )
    chip = (mine + got.astype(F32)).astype(BF16).reshape(NY, 128, 3072)
    chip, *_ = lax.optimization_barrier((chip, *same))
    total = chip[y].astype(F32)
    for k in (1, 3, 2):
        total += ring(chip[(y + k) % NY], "y", NY, k).astype(F32)
    input_grad = total.astype(BF16)
    return input_grad[None], p_basis, q_t.T, feedback_new[None]


def solution(mesh):
    fine = Mesh(mesh.devices.reshape(NZ, NX, NY, NC), ("z", "x", "y", "c"))
    dp = ("z", "x")
    placed = (P(dp, MP, None), P(dp, None, MP), P(None, MP), P(dp, None, MP), P(MP, None))
    return jax.shard_map(
        local,
        mesh=fine,
        in_specs=placed,
        out_specs=(P(dp, MP, None), P(), P(MP, None), P(dp, None, MP)),
        check_vma=False,
    )
```

time: 497 us -> 206 us (0.41)
  the two profiles are of different devices: /device:TPU:8 before, /device:TPU:1 now
where the time goes in v1:
time: 206 us; the launch traced here: 204 us
  waiting for transfers between devices  51.9 us (25%)
  starting transfers between devices  48.2 us (23%)
  local copies, waits for them, and re-layouts  37.2 us (18%)
  matrix products  33.1 us (16%)
  other arithmetic  25.5 us (12%)
  Pallas kernels  7.12 us (3%)
    all_to_all x7, waiting for transfers between devices, exchange(): return lax.all_to_all(value, axes, 0, 0, tiled=True)  41.6 us
    all_to_all x7, starting transfers between devices, exchange(): return lax.all_to_all(value, axes, 0, 0, tiled=True)  37.6 us
    unnamed x29, local copies, waits for them, and re-layouts  15.8 us
    ppermute x11, starting transfers between devices, ring(): lax.ppermute(value, axis, [(i, (i + shift) % size) for i in range(size)])  10.6 us
    ppermute x11, waiting for transfers between devices, ring(): lax.ppermute(value, axis, [(i, (i + shift) % size) for i in range(size)])  10.3 us
    another operation x3, other arithmetic, local(): lower_factor = jnp.linalg.cholesky(gram_matrix)  8.66 us
    dot_general x1, matrix products, local(): jnp.dot(p_basis, q_t, precision=lax.Precision.HIGHEST, preferred_element_...  7.86 us
    pallas_call x1, Pallas kernels, merge(): pl.pallas_call(merge_kernel, grid=(d // tile,), in_specs=[pl.BlockSpec((r...  7.12 us
  transfers between devices with their start and end apart: 18, of which 7 were waited for; matrix products, arithmetic and copies ran while one was open for 43% of the time, Pallas kernels for 3%

profile of v1, /device:TPU:1, one launch (start us, length us, event | category | flops | bytes accessed | tf_op | source)
XLA Modules:
  0.0 204.0 jit_solution(3131296191673945150)
XLA Ops:
  10.8 6.1 %all-to-all-start = ((f32[8,64,128]{2,1,0:T(8,128)}), f32[8,64,128]{2,1,0:T(8,128)S(1)}, u32[]{:S(2)}, u32[]{:S(2)}) async-start(f32[8,64,128]{2,1,0:T(8,128)} %reshape.53), calls=%async_computation | async-start | bytes 524288 | tf_op jit(solution)/shard_map/all_to_all | solution.py:22
  16.8 3.4 %fusion.22 = f32[3072,64]{0,1:T(8,128)} fusion(f32[384,64]{0,1:T(8,128)S(1)} %copy-done.8, bf16[1,3072,384]{2,1,0:T(8,128)(2,1)} %param.8), kind=kOutput, calls=%fused_computation.51 | convolution fusion | flops 151019520 | bytes 3244032 | tf_op jit(solution)/shard_map/dot_general | solution.py:87
  20.2 22.6 %all-to-all-done = f32[8,64,128]{2,1,0:T(8,128)S(1)} async-done(((f32[8,64,128]{2,1,0:T(8,128)}), f32[8,64,128]{2,1,0:T(8,128)S(1)}, u32[]{:S(2)}, u32[]{:S(2)}) %all-to-all-start) | async-done | bytes 262176 | tf_op jit(solution)/shard_map/all_to_all | solution.py:22
  48.0 6.8 %all-to-all-start.1 = ((f32[32,48,128]{2,1,0:T(8,128)}), f32[32,48,128]{2,1,0:T(8,128)}, u32[]{:S(2)}, u32[]{:S(2)}) async-start(f32[32,48,128]{2,1,0:T(8,128)} %bitcast.103), calls=%async_computation.1 | async-start | bytes 1572864 | tf_op jit(solution)/shard_map/all_to_all | solution.py:22
  56.0 3.5 %convolution_convert_fusion = bf16[512,3072]{1,0:T(8,128)(2,1)} fusion(bf16[512,384]{1,0:T(8,128)(2,1)S(1)} %bitcast.108, bf16[3072,384]{1,0:T(8,128)(2,1)S(1)} %copy-done), kind=kOutput, calls=%fused_computation.2 | convolution fusion | flops 1209532416 | bytes 5898240 | tf_op jit(solution)/shard_map/dot_general | solution.py:117
  60.0 9.0 %all-to-all-done.1 = f32[32,48,128]{2,1,0:T(8,128)} async-done(((f32[32,48,128]{2,1,0:T(8,128)}), f32[32,48,128]{2,1,0:T(8,128)}, u32[]{:S(2)}, u32[]{:S(2)}) %all-to-all-start.1) | async-done | bytes 786464 | tf_op jit(solution)/shard_map/all_to_all | solution.py:22
  72.3 8.2 %all-to-all-start.2 = ((f32[8,48,128]{2,1,0:T(8,128)}), f32[8,48,128]{2,1,0:T(8,128)}, u32[]{:S(2)}, u32[]{:S(2)}) async-start(f32[8,48,128]{2,1,0:T(8,128)} %broadcast_in_dim.14), calls=%async_computation.2 | async-start | bytes 393216 | tf_op jit(solution)/shard_map/all_to_all | solution.py:22
  85.8 5.8 %all-to-all-done.2 = f32[8,48,128]{2,1,0:T(8,128)} async-done(((f32[8,48,128]{2,1,0:T(8,128)}), f32[8,48,128]{2,1,0:T(8,128)}, u32[]{:S(2)}, u32[]{:S(2)}) %all-to-all-start.2) | async-done | bytes 196640 | tf_op jit(solution)/shard_map/all_to_all | solution.py:22
  94.7 4.7 %all-to-all-start.3 = ((f32[32,48,128]{2,1,0:T(8,128)}), f32[32,48,128]{2,1,0:T(8,128)}, u32[]{:S(2)}, u32[]{:S(2)}) async-start(f32[32,48,128]{2,1,0:T(8,128)} %broadcast_in_dim.15), calls=%async_computation.3 | async-start | bytes 1572864 | tf_op jit(solution)/shard_map/all_to_all | solution.py:22
  108.9 7.1 %shard_map.84 = bf16[3072,384]{1,0:T(8,128)(2,1)S(1)} custom-call(bf16[128,3072]{1,0:T(8,128)(2,1)S(1)} %bitcast.90, bf16[128,3072]{1,0:T(8,128)(2,1)} %collective-permute-done.7.refs_1_, bf16[128,3072]{1,0:T(8,128)(2,1)} %collective-permute-done.1.refs_2_, bf16[128,3072]{1,0:T(8,128)(2,1)} %collective-permute-done.8.refs_3_, ...), custom_call_target="tpu_custom_call" | custom-call | flops 2415919104 | bytes 12582912 | tf_op jit(solution)/shard_map/pallas_call | solution.py:47
  120.0 3.4 %fusion.11 = f32[64,64]{1,0:T(8,128)} fusion(f32[1536,64]{1,0:T(8,128)S(1)} %get-tuple-element.10, f32[1536,64]{1,0:T(8,128)S(1)} %get-tuple-element.9), kind=kOutput, calls=%fused_computation.25 | convolution fusion | flops 151191552 | bytes 802816 | tf_op jit(solution)/shard_map/dot_general | solution.py:105
  126.2 7.2 %cholesky.16 = f32[64,64]{1,0:T(8,128)} custom-call(f32[64,64]{1,0:T(8,128)} %fusion.21), custom_call_target="Cholesky" | custom-call | tf_op jit(solution)/shard_map/jit(cholesky)/cholesky | solution.py:108
  133.4 2.6 %fusion.8 = f32[64,384]{1,0:T(8,128)S(1)} fusion(bf16[3072,384]{1,0:T(8,128)(2,1)} %copy-done.1, f32[1536,64]{1,0:T(8,128)} %copy-done.5, f32[1536,64]{1,0:T(8,128)S(1)} %get-tuple-element.9), kind=kOutput, calls=%fused_computation.19 | convolution fusion | flops 151781376 | bytes 3244032 | tf_op jit(solution)/shard_map/dot_general | solution.py:99
  140.5 4.3 %all-to-all-start.4 = ((f32[4,48,128]{2,1,0:T(8,128)}), f32[4,48,128]{2,1,0:T(8,128)}, u32[]{:S(2)}, u32[]{:S(2)}) async-start(f32[4,48,128]{2,1,0:T(8,128)} %bitcast.107), calls=%async_computation.4 | async-start | bytes 196608 | tf_op jit(solution)/shard_map/all_to_all | solution.py:22
  146.2 3.3 %all-to-all-done.4 = f32[4,48,128]{2,1,0:T(8,128)} async-done(((f32[4,48,128]{2,1,0:T(8,128)}), f32[4,48,128]{2,1,0:T(8,128)}, u32[]{:S(2)}, u32[]{:S(2)}) %all-to-all-start.4) | async-done | bytes 98336 | tf_op jit(solution)/shard_map/all_to_all | solution.py:22
  152.5 4.0 %all-to-all-start.5 = ((f32[8,48,128]{2,1,0:T(8,128)}), f32[8,48,128]{2,1,0:T(8,128)}, u32[]{:S(2)}, u32[]{:S(2)}) async-start(f32[8,48,128]{2,1,0:T(8,128)} %broadcast_in_dim.16), calls=%async_computation.5 | async-start | bytes 393216 | tf_op jit(solution)/shard_map/all_to_all | solution.py:22
  156.5 3.7 %add_convert_fusion = bf16[512,3072]{1,0:T(8,128)(2,1)S(1)} fusion(bf16[512,3072]{1,0:T(8,128)(2,1)} %collective-permute-done, bf16[512,384]{1,0:T(8,128)(2,1)S(1)} %bitcast.104, bf16[3072,384]{1,0:T(8,128)(2,1)S(1)} %copy-done), kind=kOutput, calls=%fused_computation | convolution fusion | flops 1212678144 | bytes 9043968 | tf_op jit(solution)/shard_map/dot_general | solution.py:121
  162.6 2.7 %collective-permute-start.6 = (bf16[128,3072]{1,0:T(8,128)(2,1)}, bf16[128,3072]{1,0:T(8,128)(2,1)}, u32[]{:S(2)}, u32[]{:S(2)}) collective-permute-start(bf16[128,3072]{1,0:T(8,128)(2,1)} %get-tuple-element.7), channel_id=1, source_target_pairs={{0,4},{2,6},{4,0},{6,2},{1,5},{3,7},{5,1},{7,3},{8,12},{10,14},{12... | collective-permute-start | bytes 2359304 | tf_op jit(solution)/shard_map/ppermute | solution.py:18
  167.5 4.9 %custom-call.8 = f32[1,64,64]{1,2,0:T(8,128)S(1)} custom-call(f32[1,64,64]{2,1,0:T(8,128)S(1)} %fusion.16), custom_call_target="InvertDiagBlocksLowerTriangular" | custom-call | tf_op jit(solution)/shard_map/triangular_solve | solution.py:109
  174.0 3.5 %all-to-all-start.6 = ((f32[4,48,128]{2,1,0:T(8,128)}), f32[4,48,128]{2,1,0:T(8,128)S(1)}, u32[]{:S(2)}, u32[]{:S(2)}) async-start(f32[4,48,128]{2,1,0:T(8,128)} %broadcast_in_dim.18), calls=%async_computation.6 | async-start | bytes 196608 | tf_op jit(solution)/shard_map/all_to_all | solution.py:22
  177.5 3.9 %fusion.10 = f32[3072,64]{0,1:T(8,128)} fusion(f32[1536,64]{1,0:T(8,128)} %copy-done.5, f32[1536,64]{1,0:T(8,128)S(1)} %get-tuple-element.9, f32[1,64,64]{1,2,0:T(8,128)S(1)} %custom-call.8), kind=kOutput, calls=%fused_computation.24 | convolution fusion | flops 151191552 | bytes 1589248 | tf_op jit(solution)/shard_map/triangular_solve | solution.py:109
  182.6 7.9 %fusion.2 = bf16[1,3072,384]{2,1,0:T(8,128)(2,1)} fusion(bf16[3072,384]{1,0:T(8,128)(2,1)} %copy-done.1, f32[3072,64]{0,1:T(8,128)} %fusion.10, f32[64,384]{1,0:T(8,128)S(1)} %convolution_multiply_fusion), kind=kOutput, calls=%fused_computation.6 | convolution fusion | flops 909508608 | bytes 5603328 | tf_op jit(solution)/shard_map/dot_general | solution.py:113
  190.5 9.3 %collective-permute-done.5 = bf16[128,3072]{1,0:T(8,128)(2,1)} collective-permute-done((bf16[128,3072]{1,0:T(8,128)(2,1)}, bf16[128,3072]{1,0:T(8,128)(2,1)}, u32[]{:S(2)}, u32[]{:S(2)}) %collective-permute-start.5) | collective-permute-done | bytes 786464 | tf_op jit(solution)/shard_map/ppermute | solution.py:18
  200.8 3.2 %fusion.7 = bf16[1,128,3072]{2,1,0:T(8,128)(2,1)} fusion(bf16[128,3072]{1,0:T(8,128)(2,1)} %collective-permute-done.6, bf16[128,3072]{1,0:T(8,128)(2,1)} %collective-permute-done.5, bf16[128,3072]{1,0:T(8,128)(2,1)} %collective-permute-done.4, bf16[4,128,3072]{2,1,0:T(8,128)(2,1)} %bitcast.92, s32[]{:T(128)S(6)} %select_n.79), kind=kLoop, calls=%fused_computation.18 | loop fusion | flops 3145728 | bytes 3932164 | tf_op jit(solution)/shard_map/broadcast_in_dim | solution.py:130
  (83 shorter events, 61.9 us)
Async XLA Ops:
  0.6 55.4 %copy-start = (bf16[3072,384]{1,0:T(8,128)(2,1)S(1)}, bf16[3072,384]{1,0:T(8,128)(2,1)}, u32[]{:S(2)}) copy-start(bf16[3072,384]{1,0:T(8,128)(2,1)} %param.7) | copy-start | bytes 7077892
  0.6 16.2 %copy-start.8 = (f32[384,64]{0,1:T(8,128)S(1)}, f32[384,64]{0,1:T(8,128)}, u32[]{:S(2)}) copy-start(f32[384,64]{0,1:T(8,128)} %param.9) | copy-start | bytes 294916
  0.7 81.4 %collective-permute-start.1 = (bf16[128,3072]{1,0:T(8,128)(2,1)}, bf16[128,3072]{1,0:T(8,128)(2,1)}, u32[]{:S(2)}, u32[]{:S(2)}) collective-permute-start(bf16[128,3072]{1,0:T(8,128)(2,1)} %bitcast.86), channel_id=1, source_target_pairs={{0,2},{2,4},{4,6},{6,0},{1,3},{3,5},{5,7},{7,1},{8,10},{10,12},{12... | collective-permute-start | bytes 2359304 | tf_op jit(solution)/shard_map/ppermute | solution.py:18
  2.9 79.3 %collective-permute-start.2 = (bf16[128,3072]{1,0:T(8,128)(2,1)}, bf16[128,3072]{1,0:T(8,128)(2,1)}, u32[]{:S(2)}, u32[]{:S(2)}) collective-permute-start(bf16[128,3072]{1,0:T(8,128)(2,1)} %bitcast.87), channel_id=1, source_target_pairs={{0,6},{2,0},{4,2},{6,4},{1,7},{3,1},{5,3},{7,5},{8,14},{10,8},{12,... | collective-permute-start | bytes 2359304 | tf_op jit(solution)/shard_map/ppermute | solution.py:18
  4.4 78.2 %collective-permute-start.3 = (bf16[128,3072]{1,0:T(8,128)(2,1)}, bf16[128,3072]{1,0:T(8,128)(2,1)}, u32[]{:S(2)}, u32[]{:S(2)}) collective-permute-start(bf16[128,3072]{1,0:T(8,128)(2,1)} %bitcast.88), channel_id=1, source_target_pairs={{0,4},{2,6},{4,0},{6,2},{1,5},{3,7},{5,1},{7,3},{8,12},{10,14},{12... | collective-permute-start | bytes 2359304 | tf_op jit(solution)/shard_map/ppermute | solution.py:18
  8.6 34.3 %copy-start.4 = (bf16[1,128,3072]{2,1,0:T(8,128)(2,1)S(1)}, bf16[1,128,3072]{2,1,0:T(8,128)(2,1)}, u32[]{:S(2)}) copy-start(bf16[1,128,3072]{2,1,0:T(8,128)(2,1)} %param.5) | copy-start | bytes 2359300
  10.8 32.1 %all-to-all-start = ((f32[8,64,128]{2,1,0:T(8,128)}), f32[8,64,128]{2,1,0:T(8,128)S(1)}, u32[]{:S(2)}, u32[]{:S(2)}) async-start(f32[8,64,128]{2,1,0:T(8,128)} %reshape.53), calls=%async_computation | async-start | bytes 524288 | tf_op jit(solution)/shard_map/all_to_all | solution.py:22
  48.0 21.1 %all-to-all-start.1 = ((f32[32,48,128]{2,1,0:T(8,128)}), f32[32,48,128]{2,1,0:T(8,128)}, u32[]{:S(2)}, u32[]{:S(2)}) async-start(f32[32,48,128]{2,1,0:T(8,128)} %bitcast.103), calls=%async_computation.1 | async-start | bytes 1572864 | tf_op jit(solution)/shard_map/all_to_all | solution.py:22
  59.5 97.0 %collective-permute-start = (bf16[512,3072]{1,0:T(8,128)(2,1)}, bf16[512,3072]{1,0:T(8,128)(2,1)}, u32[]{:S(2)}, u32[]{:S(2)}) collective-permute-start(bf16[512,3072]{1,0:T(8,128)(2,1)} %convolution_convert_fusion), channel_id=1, source_target_pairs={{0,1},{1,0},{2,3},{3,2},{4,5},{5,4},{6,7},{7,6},{8,9},{9,8},{10,11... | collective-permute-start | bytes 9437192 | tf_op jit(solution)/shard_map/ppermute | solution.py:18
  59.8 47.4 %collective-permute-start.7 = (bf16[128,3072]{1,0:T(8,128)(2,1)S(1)}, bf16[128,3072]{1,0:T(8,128)(2,1)}, u32[]{:S(2)}, u32[]{:S(2)}) collective-permute-start(bf16[128,3072]{1,0:T(8,128)(2,1)S(1)} %bitcast.89), channel_id=1, source_target_pairs={{0,1},{1,0},{2,3},{3,2},{4,5},{5,4},{6,7},{7,6},{8,9},{9,8},{10,11... | collective-permute-start | bytes 2359304 | tf_op jit(solution)/shard_map/ppermute | solution.py:18
  72.3 19.2 %all-to-all-start.2 = ((f32[8,48,128]{2,1,0:T(8,128)}), f32[8,48,128]{2,1,0:T(8,128)}, u32[]{:S(2)}, u32[]{:S(2)}) async-start(f32[8,48,128]{2,1,0:T(8,128)} %broadcast_in_dim.14), calls=%async_computation.2 | async-start | bytes 393216 | tf_op jit(solution)/shard_map/all_to_all | solution.py:22
  82.0 25.2 %collective-permute-start.8 = (bf16[128,3072]{1,0:T(8,128)(2,1)}, bf16[128,3072]{1,0:T(8,128)(2,1)}, u32[]{:S(2)}, u32[]{:S(2)}) collective-permute-start(bf16[128,3072]{1,0:T(8,128)(2,1)} %collective-permute-done.1.refs_2_), channel_id=1, source_target_pairs={{0,1},{1,0},{2,3},{3,2},{4,5},{5,4},{6,7},{7,6},{8,9},{9,8},{10,11... | collective-permute-start | bytes 2359304 | tf_op jit(solution)/shard_map/ppermute | solution.py:18
  82.2 25.0 %collective-permute-start.9 = (bf16[128,3072]{1,0:T(8,128)(2,1)}, bf16[128,3072]{1,0:T(8,128)(2,1)}, u32[]{:S(2)}, u32[]{:S(2)}) collective-permute-start(bf16[128,3072]{1,0:T(8,128)(2,1)} %collective-permute-done.2.refs_4_), channel_id=1, source_target_pairs={{0,1},{1,0},{2,3},{3,2},{4,5},{5,4},{6,7},{7,6},{8,9},{9,8},{10,11... | collective-permute-start | bytes 2359304 | tf_op jit(solution)/shard_map/ppermute | solution.py:18
  82.5 24.7 %collective-permute-start.10 = (bf16[128,3072]{1,0:T(8,128)(2,1)}, bf16[128,3072]{1,0:T(8,128)(2,1)}, u32[]{:S(2)}, u32[]{:S(2)}) collective-permute-start(bf16[128,3072]{1,0:T(8,128)(2,1)} %collective-permute-done.3.refs_6_), channel_id=1, source_target_pairs={{0,1},{1,0},{2,3},{3,2},{4,5},{5,4},{6,7},{7,6},{8,9},{9,8},{10,11... | collective-permute-start | bytes 2359304 | tf_op jit(solution)/shard_map/ppermute | solution.py:18
  94.7 22.7 %all-to-all-start.3 = ((f32[32,48,128]{2,1,0:T(8,128)}), f32[32,48,128]{2,1,0:T(8,128)}, u32[]{:S(2)}, u32[]{:S(2)}) async-start(f32[32,48,128]{2,1,0:T(8,128)} %broadcast_in_dim.15), calls=%async_computation.3 | async-start | bytes 1572864 | tf_op jit(solution)/shard_map/all_to_all | solution.py:22
  133.4 2.8 %copy-start.6 = (f32[1536,64]{1,0:T(8,128)S(1)}, f32[1536,64]{1,0:T(8,128)}, u32[]{:S(2)}) copy-start(f32[1536,64]{1,0:T(8,128)} %copy-done.5) | copy-start | bytes 1179652
  140.5 9.0 %all-to-all-start.4 = ((f32[4,48,128]{2,1,0:T(8,128)}), f32[4,48,128]{2,1,0:T(8,128)}, u32[]{:S(2)}, u32[]{:S(2)}) async-start(f32[4,48,128]{2,1,0:T(8,128)} %bitcast.107), calls=%async_computation.4 | async-start | bytes 196608 | tf_op jit(solution)/shard_map/all_to_all | solution.py:22
  152.5 19.9 %all-to-all-start.5 = ((f32[8,48,128]{2,1,0:T(8,128)}), f32[8,48,128]{2,1,0:T(8,128)}, u32[]{:S(2)}, u32[]{:S(2)}) async-start(f32[8,48,128]{2,1,0:T(8,128)} %broadcast_in_dim.16), calls=%async_computation.5 | async-start | bytes 393216 | tf_op jit(solution)/shard_map/all_to_all | solution.py:22
  160.3 6.6 %copy-start.10 = (f32[64,64]{1,0:T(8,128)S(1)}, f32[64,64]{1,0:T(8,128)}, u32[]{:S(2)}) copy-start(f32[64,64]{1,0:T(8,128)} %cholesky.16) | copy-start | bytes 49156
  162.6 27.8 %collective-permute-start.6 = (bf16[128,3072]{1,0:T(8,128)(2,1)}, bf16[128,3072]{1,0:T(8,128)(2,1)}, u32[]{:S(2)}, u32[]{:S(2)}) collective-permute-start(bf16[128,3072]{1,0:T(8,128)(2,1)} %get-tuple-element.7), channel_id=1, source_target_pairs={{0,4},{2,6},{4,0},{6,2},{1,5},{3,7},{5,1},{7,3},{8,12},{10,14},{12... | collective-permute-start | bytes 2359304 | tf_op jit(solution)/shard_map/ppermute | solution.py:18
  165.4 34.4 %collective-permute-start.5 = (bf16[128,3072]{1,0:T(8,128)(2,1)}, bf16[128,3072]{1,0:T(8,128)(2,1)}, u32[]{:S(2)}, u32[]{:S(2)}) collective-permute-start(bf16[128,3072]{1,0:T(8,128)(2,1)} %get-tuple-element.8), channel_id=1, source_target_pairs={{0,6},{2,0},{4,2},{6,4},{1,7},{3,1},{5,3},{7,5},{8,14},{10,8},{12,... | collective-permute-start | bytes 2359304 | tf_op jit(solution)/shard_map/ppermute | solution.py:18
  166.2 34.5 %collective-permute-start.4 = (bf16[128,3072]{1,0:T(8,128)(2,1)}, bf16[128,3072]{1,0:T(8,128)(2,1)}, u32[]{:S(2)}, u32[]{:S(2)}) collective-permute-start(bf16[128,3072]{1,0:T(8,128)(2,1)} %get-tuple-element.6), channel_id=1, source_target_pairs={{0,2},{2,4},{4,6},{6,0},{1,3},{3,5},{5,7},{7,1},{8,10},{10,12},{12... | collective-permute-start | bytes 2359304 | tf_op jit(solution)/shard_map/ppermute | solution.py:18
  174.0 8.3 %all-to-all-start.6 = ((f32[4,48,128]{2,1,0:T(8,128)}), f32[4,48,128]{2,1,0:T(8,128)S(1)}, u32[]{:S(2)}, u32[]{:S(2)}) async-start(f32[4,48,128]{2,1,0:T(8,128)} %broadcast_in_dim.18), calls=%async_computation.6 | async-start | bytes 196608 | tf_op jit(solution)/shard_map/all_to_all | solution.py:22
  182.6 7.9 %copy-start.9 = (f32[64,384]{1,0:T(8,128)}, f32[64,384]{1,0:T(8,128)S(1)}, u32[]{:S(2)}) copy-start(f32[64,384]{1,0:T(8,128)S(1)} %convolution_multiply_fusion) | copy-start | bytes 294916
  (5 other events, 9.0 us)

commit v2 on v0

v2 whole, which is shorter than its diff:
```python
import functools

import jax
import jax.numpy as jnp
from jax import lax
from jax.experimental import pallas as pl
from jax.experimental.pallas import tpu as pltpu
from jax.sharding import Mesh, PartitionSpec as P

F32 = jnp.float32
BF16 = jnp.bfloat16
NX, NY, NZ, NC = 4, 4, 8, 2
DP, MP = ("z", "x"), ("y", "c")
N_DP = NZ * NX
HALF, COLS, RANK, BLOCK, D = 1536, 384, 64, 128, 3072
TILE = 512
STEPS = HALF // TILE
HIGHEST = lax.Precision.HIGHEST


def ring(value, axis, size, shift):
    return lax.ppermute(value, axis, [(i, (i + shift) % size) for i in range(size)])


def exchange(value, axes):
    return lax.all_to_all(value, axes, 0, 0, tiled=True)


def call(kernel, outs, flops, grid=None, **kwargs):
    return pl.pallas_call(
        kernel,
        out_shape=outs,
        compiler_params=pltpu.CompilerParams(vmem_limit_bytes=40 * 2**20),
        cost_estimate=pl.CostEstimate(
            flops=int(flops), bytes_accessed=4 * 2**20, transcendentals=0
        ),
        **({} if grid is None else {"grid": grid}),
        **kwargs,
    )


def out(shape, dtype=F32):
    return jax.ShapeDtypeStruct(shape, dtype)


def dot(a, b, dims=((1,), (0,)), precision=None):
    return lax.dot_general(a, b, (dims, ((), ())), precision=precision, preferred_element_type=F32)


def two(value):
    high = value.astype(BF16)
    return high, (value - high.astype(F32)).astype(BF16)


def lanes(shape):
    return lax.broadcasted_iota(jnp.int32, shape, 1)


def sides(q):
    zero = jnp.zeros_like(q)
    return jnp.concatenate([q, zero], axis=1), jnp.concatenate([zero, q], axis=1)


def t_kernel(cot_ref, q_ref, out_ref):
    left, right = sides(q_ref[...].astype(BF16))
    cot = cot_ref[...].reshape(8, 2, 64, COLS)
    first, second = cot[:, 0].reshape(512, COLS), cot[:, 1].reshape(512, COLS)
    out_ref[...] = (dot(first, left) + dot(second, right)).reshape(8, 64, 128)


def t_rows(cot, q):
    return call(t_kernel, out((8, 64, 128)), 2e8)(cot, q)


def f_kernel(old_ref, q_ref, first_ref, second_ref, fq_ref, act_ref):
    left, right = sides(q_ref[...].astype(BF16))
    fq_ref[...] = dot(old_ref[0], left) + dot(old_ref[1], right)
    act_ref[0] = first_ref[...].T
    act_ref[1] = second_ref[...].T


def f_rows(old, q, act):
    return call(
        f_kernel,
        [out((HALF, 128)), out((2, HALF, BLOCK), BF16)],
        3e8,
        grid=(STEPS,),
        in_specs=[
            pl.BlockSpec((2, TILE, COLS), lambda i: (0, i, 0)),
            pl.BlockSpec((COLS, RANK), lambda i: (0, 0)),
            pl.BlockSpec((BLOCK, TILE), lambda i: (0, i)),
            pl.BlockSpec((BLOCK, TILE), lambda i: (0, i + STEPS)),
        ],
        out_specs=[
            pl.BlockSpec((TILE, 128), lambda i: (i, 0)),
            pl.BlockSpec((2, TILE, BLOCK), lambda i: (0, i, 0)),
        ],
    )(old, q, act, act)


def p_kernel(t_ref, act_ref, fq_ref, out_ref):
    t = jnp.sum(t_ref[...], axis=0)
    low_lane = lanes(t.shape) < 64
    turned = pltpu.roll(t, 64, 1)
    rhs = jnp.concatenate(
        [
            jnp.where(low_lane, t, 0.0),
            jnp.where(low_lane, turned, 0.0),
            jnp.where(low_lane, 0.0, turned),
            jnp.where(low_lane, 0.0, t),
        ],
        axis=0,
    )
    lhs = jnp.concatenate([act_ref[0], act_ref[1]], axis=1)
    both = dot(lhs, jnp.concatenate(two(rhs), axis=1))
    out_ref[...] = both[:, :128] + both[:, 128:] + fq_ref[...]


def p_rows(t, act, fq):
    return call(p_kernel, out((HALF, 128)), 2e8)(t, act, fq)


def sum_kernel(in_ref, out_ref):
    out_ref[...] = jnp.broadcast_to(jnp.sum(in_ref[...], axis=0)[None], out_ref.shape)


def sum_spread(value, count):
    return call(sum_kernel, out((count,) + value.shape[1:]), 1e6)(value)


def merge_kernel(place_ref, cot_ref, old_ref, *refs):
    acts, (out_ref, cot_rel) = refs[:-2], refs[-2:]
    y, c = place_ref[0], place_ref[1]

    @pl.when(pl.program_id(0) == 0)
    def _():
        for n, k in enumerate((0, 3, 1, 2)):
            for m in range(2):
                block = lax.rem(y + k, NY) * 2 + (c if m == 0 else 1 - c)
                cot_rel[pl.ds((2 * n + m) * BLOCK, BLOCK), :] = cot_ref[
                    pl.ds(pl.multiple_of(block * BLOCK, BLOCK), BLOCK), :
                ]

    for h in range(2):
        near = [ref[h] for ref in acts[:6]]
        far = [ref[...] for ref in acts[6 + 2 * h : 8 + 2 * h]]
        gradient = dot(jnp.concatenate(near + far, axis=1), cot_rel[...])
        out_ref[h] = (gradient + old_ref[h].astype(F32)).astype(BF16)


def merge(place, cot, old, near, far):
    return call(
        merge_kernel,
        out((2, HALF, COLS), BF16),
        2.4e9,
        grid=(STEPS,),
        in_specs=[
            pl.BlockSpec(memory_space=pltpu.SMEM),
            pl.BlockSpec(cot.shape, lambda i: (0, 0)),
            pl.BlockSpec((2, TILE, COLS), lambda i: (0, i, 0)),
        ]
        + [pl.BlockSpec((2, TILE, BLOCK), lambda i: (0, i, 0))] * 6
        + [pl.BlockSpec((TILE, BLOCK), lambda i: (i, 0))] * 4,
        out_specs=pl.BlockSpec((2, TILE, COLS), lambda i: (0, i, 0)),
        scratch_shapes=[pltpu.VMEM((8 * BLOCK, COLS), BF16)],
    )(place, cot, old, *near, *far)


def s_kernel(p_ref, merged_ref, out_ref):
    p = jnp.concatenate(two(p_ref[...]), axis=1)
    first = dot(p, merged_ref[0], ((0,), (0,)))
    second = dot(p, merged_ref[1], ((0,), (0,)))
    s = first[:64] + first[128:192] + second[64:128] + second[192:]
    for n in range(3):
        out_ref[pl.ds(64 * n, 64), :] = s[:, 128 * n : 128 * n + 128]
    out_ref[pl.ds(192, 64), :] = jnp.zeros((64, 128), F32)


def s_rows(p, merged):
    return call(s_kernel, out((256, 128)), 1.2e9)(p, merged)


def basis_kernel(p_ref, basis_ref, packed_ref, inverse_ref):
    p = p_ref[...]
    pair = dot(p, p, ((0,), (0,)), HIGHEST)
    gram = pair[:64, :64] + pair[64:, 64:]
    row = lax.broadcasted_iota(jnp.int32, (64, 64), 0)
    unit = jnp.where(row == lanes((64, 64)), 1.0, 0.0)
    table = jnp.concatenate([gram, unit], axis=1)
    tiles = [table[8 * i : 8 * i + 8] for i in range(8)]
    sub = lax.broadcasted_iota(jnp.int32, (8, 128), 0)
    for j in range(64):
        at, inner = j // 8, j % 8
        pivot = tiles[at][inner : inner + 1]
        scaled = pivot * (1.0 / pivot[:, j : j + 1])
        for i in range(at, 8):
            factor = jnp.broadcast_to(tiles[i][:, j : j + 1], (8, 128))
            if i == at:
                factor = jnp.where(sub > inner, factor, 0.0)
            tiles[i] = tiles[i] - factor * scaled
    table = jnp.concatenate(tiles, axis=0)
    lane = lanes((64, 128))
    here = lax.broadcasted_iota(jnp.int32, (64, 128), 0) == lane
    diagonal = jnp.sum(jnp.where(here, table, 0.0), axis=1, keepdims=True)
    right = jnp.where(lane >= 64, table, 0.0) / jnp.sqrt(diagonal)
    inverse = jnp.concatenate([pltpu.roll(right, 64, 1), right], axis=0)
    basis = dot(p, inverse, ((1,), (1,)), HIGHEST)
    inverse_ref[...] = inverse
    packed_ref[...] = basis
    basis_ref[0] = basis[:, :64]
    basis_ref[1] = basis[:, 64:]


def basis_rows(p):
    return call(
        basis_kernel, [out((2, HALF, 64)), out((HALF, 128)), out((128, 128))], 5e9
    )(p)


def last_kernel(s_ref, inverse_ref, packed_ref, merged_ref, q_ref, new_ref, rhs):
    @pl.when(pl.program_id(0) == 0)
    def _():
        s = jnp.concatenate([s_ref[pl.ds(64 * n, 64), :] for n in range(3)], axis=1)
        q = dot(inverse_ref[0:64, 0:64], s, precision=HIGHEST) * (1.0 / N_DP)
        q_ref[...] = q.T
        high, low = two(q)
        zero = jnp.zeros_like(high)
        for h in range(2):
            pair = lambda v: [zero, v] if h else [v, zero]
            rhs[h] = jnp.concatenate(pair(high) + pair(high) + pair(low), axis=0)

    high, low = two(packed_ref[...])
    lhs = jnp.concatenate([high, low, high], axis=1)
    for h in range(2):
        new_ref[h] = (merged_ref[h].astype(F32) - dot(lhs, rhs[h])).astype(BF16)


def last(s, inverse, packed, merged):
    return call(
        last_kernel,
        [out((COLS, RANK)), out((2, HALF, COLS), BF16)],
        1e9,
        grid=(STEPS,),
        in_specs=[
            pl.BlockSpec((256, 128), lambda i: (0, 0)),
            pl.BlockSpec((128, 128), lambda i: (0, 0)),
            pl.BlockSpec((TILE, 128), lambda i: (i, 0)),
            pl.BlockSpec((2, TILE, COLS), lambda i: (0, i, 0)),
        ],
        out_specs=[
            pl.BlockSpec((COLS, RANK), lambda i: (0, 0)),
            pl.BlockSpec((2, TILE, COLS), lambda i: (0, i, 0)),
        ],
        scratch_shapes=[pltpu.VMEM((2, 384, COLS), BF16)],
    )(s, inverse, packed, merged)


def pick(place_ref, cot_ref, own):
    y, c = place_ref[0], place_ref[1]
    core = c if own else 1 - c
    rows = [
        cot_ref[
            pl.ds(pl.multiple_of((lax.rem(y + k, NY) * 2 + core) * BLOCK, BLOCK), BLOCK), :
        ]
        for k in range(NY)
    ]
    return jnp.concatenate(rows, axis=0)


def other_kernel(place_ref, cot_ref, weight_ref, out_ref):
    part = dot(pick(place_ref, cot_ref, False), weight_ref[...], ((1,), (1,)))
    out_ref[...] = part.astype(BF16)


def own_kernel(place_ref, cot_ref, weight_ref, got_ref, *out_refs):
    part = dot(pick(place_ref, cot_ref, True), weight_ref[...], ((1,), (1,)))
    part = (part + got_ref[...].astype(F32)).astype(BF16)
    for k, ref in enumerate(out_refs):
        ref[...] = part[k * BLOCK : (k + 1) * BLOCK]


def grad_specs(cot):
    return [
        pl.BlockSpec(memory_space=pltpu.SMEM),
        pl.BlockSpec(cot.shape, lambda i: (0, 0)),
        pl.BlockSpec((TILE, COLS), lambda i: (i, 0)),
    ]


def grad_other(place, cot, weight):
    return call(
        other_kernel,
        out((NY * BLOCK, D), BF16),
        1.2e9,
        grid=(D // TILE,),
        in_specs=grad_specs(cot),
        out_specs=pl.BlockSpec((NY * BLOCK, TILE), lambda i: (0, i)),
    )(place, cot, weight)


def grad_own(place, cot, weight, got):
    return call(
        own_kernel,
        [out((BLOCK, D), BF16)] * NY,
        1.2e9,
        grid=(D // TILE,),
        in_specs=grad_specs(cot) + [pl.BlockSpec((NY * BLOCK, TILE), lambda i: (0, i))],
        out_specs=[pl.BlockSpec((BLOCK, TILE), lambda i: (0, i))] * NY,
    )(place, cot, weight, got)


def add_kernel(a_ref, b_ref, c_ref, d_ref, out_ref):
    total = a_ref[...].astype(F32) + b_ref[...].astype(F32)
    out_ref[...] = (total + c_ref[...].astype(F32) + d_ref[...].astype(F32)).astype(BF16)


def add_four(parts):
    return call(add_kernel, out((BLOCK, D), BF16), 2e6)(*parts)


def after(values, *earlier):
    held = lax.optimization_barrier((tuple(values), earlier))
    return list(held[0])


def local(activations, cotangent, weight, feedback, q_previous):
    act, cot = activations[0], cotangent[0]
    old = feedback[0].reshape(2, HALF, COLS)
    place = jnp.stack([lax.axis_index("y"), lax.axis_index("c")]).astype(jnp.int32)

    t = exchange(t_rows(cot, q_previous), MP)
    fq, act_t = f_rows(old, q_previous, act)
    p_send = p_rows(t, act_t, fq).reshape(N_DP, 48, 128)

    (near,) = after([act_t], t)
    low, high = ring(near, "y", NY, 1), ring(near, "y", NY, 3)

    p_mp = exchange(sum_spread(exchange(p_send, DP), 8), MP)
    from_low, from_high = after([low[1], high[0]], p_mp)
    far_second, far_first = ring(from_low, "y", NY, 1), ring(from_high, "y", NY, 3)
    p = exchange(sum_spread(p_mp, N_DP), DP).reshape(HALF, 128)

    side = lambda value: ring(value, "c", NC, 1)
    near_all = [near, side(near), low, side(low), high, side(high)]
    far_all = [far_first, side(far_first), far_second, side(far_second)]
    merged = merge(place, cot, old, near_all, far_all)

    got = side(grad_other(place, cot, weight))
    mine, *rest = grad_own(place, cot, weight, got)
    rest = after(rest, far_first, far_second)
    parts = [ring(value, "y", NY, k) for k, value in zip((1, 2, 3), rest)]
    input_grad = add_four([mine] + parts)

    s = exchange(s_rows(p, merged).reshape(N_DP, 8, 128), DP)
    basis, packed, inverse = basis_rows(p)
    s = exchange(sum_spread(s, N_DP), DP).reshape(256, 128)
    q_factor, feedback_new = last(s, inverse, packed, merged)
    return (
        input_grad[None],
        basis.reshape(D, RANK),
        q_factor,
        feedback_new.reshape(1, D, COLS),
    )


def solution(mesh):
    fine = Mesh(mesh.devices.reshape(NZ, NX, NY, NC), ("z", "x", "y", "c"))
    placed = (P(DP, MP, None), P(DP, None, MP), P(None, MP), P(DP, None, MP), P(MP, None))
    return jax.shard_map(
        local,
        mesh=fine,
        in_specs=placed,
        out_specs=(P(DP, MP, None), P(), P(MP, None), P(DP, None, MP)),
        check_vma=False,
    )
```

time: 497 us -> 158 us (0.32)
  the two profiles are of different devices: /device:TPU:8 before, /device:TPU:1 now
where the time goes in v2:
time: 158 us; the launch traced here: 155 us
  starting transfers between devices  44.7 us (28%)
  Pallas kernels  41.9 us (27%)
  waiting for transfers between devices  26.2 us (17%)
  local copies, waits for them, and re-layouts  23.5 us (15%)
  blocking collectives  18.3 us (12%)
    all_to_all x5, starting transfers between devices, exchange(): return lax.all_to_all(value, axes, 0, 0, tiled=True)  32.7 us
    unnamed x39, local copies, waits for them, and re-layouts  20.7 us
    all_to_all x1, blocking collectives, exchange(): return lax.all_to_all(value, axes, 0, 0, tiled=True)  18.3 us
    all_to_all x5, waiting for transfers between devices, exchange(): return lax.all_to_all(value, axes, 0, 0, tiled=True)  16.8 us
    ppermute x13, starting transfers between devices, ring(): lax.ppermute(value, axis, [(i, (i + shift) % size) for i in range(size)])  12 us
    ppermute x13, waiting for transfers between devices, ring(): lax.ppermute(value, axis, [(i, (i + shift) % size) for i in range(size)])  9.38 us
    pallas_call x1, Pallas kernels, basis_rows(): call(basis_kernel, [out((2, HALF, 64)), out((HALF, 128)), out((128, 128))...  8.36 us
    pallas_call x1, Pallas kernels, grad_own(): call(own_kernel, [out((BLOCK, D), BF16)] * NY, 1200000000.0, grid=(D // T...  6.3 us
  transfers between devices with their start and end apart: 18, of which 5 were waited for; matrix products, arithmetic and copies ran while one was open for 3% of the time, Pallas kernels for 23%

profile of v2, /device:TPU:1, one launch (start us, length us, event | category | flops | bytes accessed | tf_op | source)
XLA Modules:
  0.0 155.5 jit_solution(14693457217119213482)
XLA Ops:
  3.9 7.2 %all-to-all-start = ((f32[8,64,128]{2,1,0:T(8,128)}), f32[8,64,128]{2,1,0:T(8,128)}, u32[]{:S(2)}, u32[]{:S(2)}) async-start(f32[8,64,128]{2,1,0:T(8,128)} %shard_map.87), calls=%async_computation | async-start | bytes 524288 | tf_op jit(solution)/shard_map/all_to_all | solution.py:26
  13.9 2.5 %shard_map.86 = (f32[1536,128]{1,0:T(8,128)S(1)}, bf16[2,1536,128]{2,1,0:T(8,128)(2,1)}) custom-call(bf16[2,1536,384]{2,1,0:T(8,128)(2,1)S(1)} %bitcast.20, f32[384,64]{1,0:T(8,128)S(1)} %copy.9.q_ref, bf16[128,3072]{1,0:T(8,128)(2,1)S(1)} %bitcast.23, bf16[128,3072]{1,0:T(8,128)(2,1)S(1)} %bitcast.24), custom_call_target="tpu_custom_call" | custom-call | flops 300000000 | bytes 4194304 | tf_op jit(solution)/shard_map/pallas_call | solution.py:83
  21.6 9.9 %all-to-all-start.1 = ((f32[32,48,128]{2,1,0:T(8,128)}), f32[32,48,128]{2,1,0:T(8,128)}, u32[]{:S(2)}, u32[]{:S(2)}) async-start(f32[32,48,128]{2,1,0:T(8,128)} %bitcast.22), calls=%async_computation.1 | async-start | bytes 1572864 | tf_op jit(solution)/shard_map/all_to_all | solution.py:26
  31.6 5.1 %shard_map.84 = bf16[512,3072]{1,0:T(8,128)(2,1)} custom-call(s32[2]{0:T(128)S(1)} %pad_add_fusion.place_ref, bf16[1024,384]{1,0:T(8,128)(2,1)S(1)} %bitcast.17, bf16[3072,384]{1,0:T(8,128)(2,1)S(1)} %copy-done.2), custom_call_target="tpu_custom_call" | custom-call | flops 1200000000 | bytes 4194304 | tf_op jit(solution)/shard_map/pallas_call | solution.py:291
  39.8 12.8 %all-to-all-done.1.in_ref = f32[32,48,128]{2,1,0:T(8,128)} async-done(((f32[32,48,128]{2,1,0:T(8,128)}), f32[32,48,128]{2,1,0:T(8,128)}, u32[]{:S(2)}, u32[]{:S(2)}) %all-to-all-start.1) | async-done | bytes 786464 | tf_op jit(solution)/shard_map/all_to_all | solution.py:26
  52.6 1.9 %shard_map.89 = f32[8,48,128]{2,1,0:T(8,128)} custom-call(f32[32,48,128]{2,1,0:T(8,128)} %all-to-all-done.1.in_ref), custom_call_target="tpu_custom_call" | custom-call | flops 1000000 | bytes 4194304 | tf_op jit(solution)/shard_map/pallas_call | solution.py:128
  54.5 6.9 %all-to-all-start.2 = ((f32[8,48,128]{2,1,0:T(8,128)}), f32[8,48,128]{2,1,0:T(8,128)S(1)}, u32[]{:S(2)}, u32[]{:S(2)}) async-start(f32[8,48,128]{2,1,0:T(8,128)} %shard_map.89), calls=%async_computation.2 | async-start | bytes 393216 | tf_op jit(solution)/shard_map/all_to_all | solution.py:26
  61.4 1.8 %slice_bitcast_fusion = bf16[1536,128]{1,0:T(8,128)(2,1)} fusion(bf16[2,1536,128]{2,1,0:T(8,128)(2,1)} %collective-permute-done.2.refs_4_), kind=kLoop, calls=%fused_computation | loop fusion | bytes 786432 | tf_op jit(solution)/shard_map/squeeze | solution.py:339
  63.7 3.6 %all-to-all-done.2.in_ref = f32[8,48,128]{2,1,0:T(8,128)S(1)} async-done(((f32[8,48,128]{2,1,0:T(8,128)}), f32[8,48,128]{2,1,0:T(8,128)S(1)}, u32[]{:S(2)}, u32[]{:S(2)}) %all-to-all-start.2) | async-done | bytes 196640 | tf_op jit(solution)/shard_map/all_to_all | solution.py:26
  68.3 4.9 %all-to-all-start.3 = ((f32[32,48,128]{2,1,0:T(8,128)}), f32[32,48,128]{2,1,0:T(8,128)}, u32[]{:S(2)}, u32[]{:S(2)}) async-start(f32[32,48,128]{2,1,0:T(8,128)} %copy-done.5), calls=%async_computation.3 | async-start | bytes 1572864 | tf_op jit(solution)/shard_map/all_to_all | solution.py:26
  75.7 8.0 %collective-permute-done.3.refs_6_ = bf16[1536,128]{1,0:T(8,128)(2,1)S(1)} collective-permute-done((bf16[1536,128]{1,0:T(8,128)(2,1)S(1)}, bf16[1536,128]{1,0:T(8,128)(2,1)S(1)}, u32[]{:S(2)}, u32[]{:S(2)}) %collective-permute-start.3) | collective-permute-done | bytes 393248 | tf_op jit(solution)/shard_map/ppermute | solution.py:22
  83.8 2.1 %collective-permute-start.11 = (bf16[1536,128]{1,0:T(8,128)(2,1)S(1)}, bf16[1536,128]{1,0:T(8,128)(2,1)S(1)}, u32[]{:S(2)}, u32[]{:S(2)}) collective-permute-start(bf16[1536,128]{1,0:T(8,128)(2,1)S(1)} %collective-permute-done.3.refs_6_), channel_id=1, source_target_pairs={{0,1},{1,0},{2,3},{3,2},{4,5},{5,4},{6,7},{7,6},{8,9},{9,8},{10,11... | collective-permute-start | bytes 1179656 | tf_op jit(solution)/shard_map/ppermute | solution.py:22
  85.8 2.1 %collective-permute-start.12 = (bf16[1536,128]{1,0:T(8,128)(2,1)S(1)}, bf16[1536,128]{1,0:T(8,128)(2,1)S(1)}, u32[]{:S(2)}, u32[]{:S(2)}) collective-permute-start(bf16[1536,128]{1,0:T(8,128)(2,1)S(1)} %collective-permute-done.4.refs_8_), channel_id=1, source_target_pairs={{0,1},{1,0},{2,3},{3,2},{4,5},{5,4},{6,7},{7,6},{8,9},{9,8},{10,11... | collective-permute-start | bytes 1179656 | tf_op jit(solution)/shard_map/ppermute | solution.py:22
  90.9 5.7 %shard_map.93.merged_ref = bf16[2,1536,384]{2,1,0:T(8,128)(2,1)S(1)} custom-call(s32[2]{0:T(128)S(1)} %pad_add_fusion.place_ref, bf16[1024,384]{1,0:T(8,128)(2,1)S(1)} %bitcast.18, bf16[2,1536,384]{2,1,0:T(8,128)(2,1)S(1)} %bitcast.21, bf16[2,1536,128]{2,1,0:T(8,128)(2,1)} %get-tuple-element.26.act_ref.refs_0_, ...), custom_call_target="tpu_custom_call" | custom-call | flops 2400000000 | bytes 4194304 | tf_op jit(solution)/shard_map/pallas_call | solution.py:152
  98.0 6.3 %shard_map.85 = (bf16[128,3072]{1,0:T(8,128)(2,1)S(1)}, bf16[128,3072]{1,0:T(8,128)(2,1)}, bf16[128,3072]{1,0:T(8,128)(2,1)}, bf16[128,3072]{1,0:T(8,128)(2,1)}) custom-call(s32[2]{0:T(128)S(1)} %pad_add_fusion.place_ref, bf16[1024,384]{1,0:T(8,128)(2,1)S(1)} %bitcast.19, bf16[3072,384]{1,0:T(8,128)(2,1)S(1)} %copy-done.2, ...), custom_call_target="tpu_custom_call" | custom-call | flops 1200000000 | bytes 4194304 | tf_op jit(solution)/shard_map/pallas_call | solution.py:302
  105.3 1.7 %collective-permute-start.6 = (bf16[128,3072]{1,0:T(8,128)(2,1)}, bf16[128,3072]{1,0:T(8,128)(2,1)}, u32[]{:S(2)}, u32[]{:S(2)}) collective-permute-start(bf16[128,3072]{1,0:T(8,128)(2,1)} %get-tuple-element.31), channel_id=1, source_target_pairs={{0,4},{2,6},{4,0},{6,2},{1,5},{3,7},{5,1},{7,3},{8,12},{10,14},{12... | collective-permute-start | bytes 2359304 | tf_op jit(solution)/shard_map/ppermute | solution.py:22
  108.0 1.7 %copy-done.9 = bf16[2,1536,384]{2,1,0:T(8,128)(2,1)S(1)} copy-done((bf16[2,1536,384]{2,1,0:T(8,128)(2,1)S(1)}, bf16[2,1536,384]{2,1,0:T(8,128)(2,1)}, u32[]{:S(2)}) %copy-start.9) | copy-done | bytes 2359320
  109.6 2.1 %shard_map.94 = f32[256,128]{1,0:T(8,128)S(1)} custom-call(f32[1536,128]{1,0:T(8,128)} %bitcast.9.p_ref, bf16[2,1536,384]{2,1,0:T(8,128)(2,1)S(1)} %copy-done.9), custom_call_target="tpu_custom_call" | custom-call | flops 1200000000 | bytes 4194304 | tf_op jit(solution)/shard_map/pallas_call | solution.py:180
  111.8 18.3 %all_to_all.30.in_ref = f32[32,8,128]{2,1,0:T(8,128)S(1)} all-to-all(f32[32,8,128]{2,1,0:T(8,128)S(1)} %bitcast.27), channel_id=1, replica_groups=mesh['z'=8,'x'=4,'y'=4,'c'=2] {'z','x'}, dimensions={0} | all-to-all | bytes 262144 | tf_op jit(solution)/shard_map/all_to_all | solution.py:26
  130.8 3.8 %all-to-all-start.5 = ((f32[32,8,128]{2,1,0:T(8,128)}), f32[32,8,128]{2,1,0:T(8,128)S(1)}, u32[]{:S(2)}, u32[]{:S(2)}) async-start(f32[32,8,128]{2,1,0:T(8,128)} %shard_map.95), calls=%async_computation.5 | async-start | bytes 262144 | tf_op jit(solution)/shard_map/all_to_all | solution.py:26
  134.6 8.4 %shard_map.92 = (f32[2,1536,64]{2,1,0:T(8,128)S(1)}, f32[1536,128]{1,0:T(8,128)S(1)}, f32[128,128]{1,0:T(8,128)S(1)}) custom-call(f32[1536,128]{1,0:T(8,128)} %bitcast.9.p_ref), custom_call_target="tpu_custom_call" | custom-call | flops 5000000000 | bytes 4194304 | tf_op jit(solution)/shard_map/pallas_call | solution.py:215
  145.5 2.9 %shard_map.90 = bf16[128,3072]{1,0:T(8,128)(2,1)} custom-call(bf16[128,3072]{1,0:T(8,128)(2,1)S(1)} %copy-done.14, bf16[128,3072]{1,0:T(8,128)(2,1)} %collective-permute-done.5.b_ref, bf16[128,3072]{1,0:T(8,128)(2,1)} %collective-permute-done.6.c_ref, bf16[128,3072]{1,0:T(8,128)(2,1)} %collective-permute-done.7.d_ref), custom_call_target="tpu_custom_call" | custom-call | flops 2000000 | bytes 4194304 | tf_op jit(solution)/shard_map/pallas_call | solution.py:318
  148.4 1.7 %copy-done.10 = bf16[2,1536,384]{2,1,0:T(8,128)(2,1)S(1)} copy-done((bf16[2,1536,384]{2,1,0:T(8,128)(2,1)S(1)}, bf16[2,1536,384]{2,1,0:T(8,128)(2,1)}, u32[]{:S(2)}) %copy-start.10) | copy-done | bytes 2359320
  151.2 3.6 %shard_map.96 = (f32[384,64]{1,0:T(8,128)S(1)}, bf16[2,1536,384]{2,1,0:T(8,128)(2,1)}) custom-call(f32[256,128]{1,0:T(8,128)S(1)} %bitcast.26, f32[128,128]{1,0:T(8,128)S(1)} %get-tuple-element.34.inverse_ref, f32[1536,128]{1,0:T(8,128)S(1)} %copy-done.16, bf16[2,1536,384]{2,1,0:T(8,128)(2,1)S(1)} %copy-done.10), custom_call_target="tpu_custom_call" | custom-call | flops 1000000000 | bytes 4194304 | tf_op jit(solution)/shard_map/pallas_call | solution.py:239
  (68 shorter events, 30.0 us)
Async XLA Ops:
  3.9 13.8 %all-to-all-start = ((f32[8,64,128]{2,1,0:T(8,128)}), f32[8,64,128]{2,1,0:T(8,128)}, u32[]{:S(2)}, u32[]{:S(2)}) async-start(f32[8,64,128]{2,1,0:T(8,128)} %shard_map.87), calls=%async_computation | async-start | bytes 524288 | tf_op jit(solution)/shard_map/all_to_all | solution.py:26
  11.1 1.7 %copy-start.3 = (bf16[1,3072,384]{2,1,0:T(8,128)(2,1)S(1)}, bf16[1,3072,384]{2,1,0:T(8,128)(2,1)}, u32[]{:S(2)}) copy-start(bf16[1,3072,384]{2,1,0:T(8,128)(2,1)} %param.8) | copy-start | bytes 7077892
  17.2 14.4 %copy-start.1 = (bf16[1,1024,384]{2,1,0:T(8,128)(2,1)S(1)}, bf16[1,1024,384]{2,1,0:T(8,128)(2,1)}, u32[]{:S(2)}) copy-start(bf16[1,1024,384]{2,1,0:T(8,128)(2,1)} %param.6) | copy-start | bytes 2359300
  17.2 14.4 %copy-start.2 = (bf16[3072,384]{1,0:T(8,128)(2,1)S(1)}, bf16[3072,384]{1,0:T(8,128)(2,1)}, u32[]{:S(2)}) copy-start(bf16[3072,384]{1,0:T(8,128)(2,1)} %weight_ref.3) | copy-start | bytes 7077892
  21.6 31.0 %all-to-all-start.1 = ((f32[32,48,128]{2,1,0:T(8,128)}), f32[32,48,128]{2,1,0:T(8,128)}, u32[]{:S(2)}, u32[]{:S(2)}) async-start(f32[32,48,128]{2,1,0:T(8,128)} %bitcast.22), calls=%async_computation.1 | async-start | bytes 1572864 | tf_op jit(solution)/shard_map/all_to_all | solution.py:26
  36.7 61.3 %collective-permute-start = (bf16[512,3072]{1,0:T(8,128)(2,1)}, bf16[512,3072]{1,0:T(8,128)(2,1)}, u32[]{:S(2)}, u32[]{:S(2)}) collective-permute-start(bf16[512,3072]{1,0:T(8,128)(2,1)} %shard_map.84), channel_id=1, source_target_pairs={{0,1},{1,0},{2,3},{3,2},{4,5},{5,4},{6,7},{7,6},{8,9},{9,8},{10,11... | collective-permute-start | bytes 9437192 | tf_op jit(solution)/shard_map/ppermute | solution.py:22
  37.8 23.6 %collective-permute-start.2 = (bf16[2,1536,128]{2,1,0:T(8,128)(2,1)}, bf16[2,1536,128]{2,1,0:T(8,128)(2,1)}, u32[]{:S(2)}, u32[]{:S(2)}) collective-permute-start(bf16[2,1536,128]{2,1,0:T(8,128)(2,1)} %get-tuple-element.26.act_ref.refs_0_), channel_id=1, source_target_pairs={{0,6},{2,0},{4,2},{6,4},{1,7},{3,1},{5,3},{7,5},{8,14},{10,8},{12,... | collective-permute-start | bytes 2359304 | tf_op jit(solution)/shard_map/ppermute | solution.py:22
  39.4 23.8 %collective-permute-start.1 = (bf16[2,1536,128]{2,1,0:T(8,128)(2,1)}, bf16[2,1536,128]{2,1,0:T(8,128)(2,1)}, u32[]{:S(2)}, u32[]{:S(2)}) collective-permute-start(bf16[2,1536,128]{2,1,0:T(8,128)(2,1)} %get-tuple-element.26.act_ref.refs_0_), channel_id=1, source_target_pairs={{0,2},{2,4},{4,6},{6,0},{1,3},{3,5},{5,7},{7,1},{8,10},{10,12},{12... | collective-permute-start | bytes 2359304 | tf_op jit(solution)/shard_map/ppermute | solution.py:22
  39.4 35.7 %collective-permute-start.8 = (bf16[2,1536,128]{2,1,0:T(8,128)(2,1)}, bf16[2,1536,128]{2,1,0:T(8,128)(2,1)}, u32[]{:S(2)}, u32[]{:S(2)}) collective-permute-start(bf16[2,1536,128]{2,1,0:T(8,128)(2,1)} %get-tuple-element.26.act_ref.refs_0_), channel_id=1, source_target_pairs={{0,1},{1,0},{2,3},{3,2},{4,5},{5,4},{6,7},{7,6},{8,9},{9,8},{10,11... | collective-permute-start | bytes 2359304 | tf_op jit(solution)/shard_map/ppermute | solution.py:22
  54.5 12.8 %all-to-all-start.2 = ((f32[8,48,128]{2,1,0:T(8,128)}), f32[8,48,128]{2,1,0:T(8,128)S(1)}, u32[]{:S(2)}, u32[]{:S(2)}) async-start(f32[8,48,128]{2,1,0:T(8,128)} %shard_map.89), calls=%async_computation.2 | async-start | bytes 393216 | tf_op jit(solution)/shard_map/all_to_all | solution.py:26
  63.2 24.8 %collective-permute-start.10 = (bf16[2,1536,128]{2,1,0:T(8,128)(2,1)}, bf16[2,1536,128]{2,1,0:T(8,128)(2,1)}, u32[]{:S(2)}, u32[]{:S(2)}) collective-permute-start(bf16[2,1536,128]{2,1,0:T(8,128)(2,1)} %collective-permute-done.2.refs_4_), channel_id=1, source_target_pairs={{0,1},{1,0},{2,3},{3,2},{4,5},{5,4},{6,7},{7,6},{8,9},{9,8},{10,11... | collective-permute-start | bytes 2359304 | tf_op jit(solution)/shard_map/ppermute | solution.py:22
  63.2 24.7 %collective-permute-start.9 = (bf16[2,1536,128]{2,1,0:T(8,128)(2,1)}, bf16[2,1536,128]{2,1,0:T(8,128)(2,1)}, u32[]{:S(2)}, u32[]{:S(2)}) collective-permute-start(bf16[2,1536,128]{2,1,0:T(8,128)(2,1)} %collective-permute-done.1.refs_2_), channel_id=1, source_target_pairs={{0,1},{1,0},{2,3},{3,2},{4,5},{5,4},{6,7},{7,6},{8,9},{9,8},{10,11... | collective-permute-start | bytes 2359304 | tf_op jit(solution)/shard_map/ppermute | solution.py:22
  68.3 5.9 %copy-start.17 = (bf16[1536,128]{1,0:T(8,128)(2,1)S(1)}, bf16[1536,128]{1,0:T(8,128)(2,1)}, u32[]{:S(2)}) copy-start(bf16[1536,128]{1,0:T(8,128)(2,1)} %slice_bitcast_fusion) | copy-start | bytes 1179652
  68.3 39.7 %all-to-all-start.3 = ((f32[32,48,128]{2,1,0:T(8,128)}), f32[32,48,128]{2,1,0:T(8,128)}, u32[]{:S(2)}, u32[]{:S(2)}) async-start(f32[32,48,128]{2,1,0:T(8,128)} %copy-done.5), calls=%async_computation.3 | async-start | bytes 1572864 | tf_op jit(solution)/shard_map/all_to_all | solution.py:26
  74.2 9.6 %collective-permute-start.3 = (bf16[1536,128]{1,0:T(8,128)(2,1)S(1)}, bf16[1536,128]{1,0:T(8,128)(2,1)S(1)}, u32[]{:S(2)}, u32[]{:S(2)}) collective-permute-start(bf16[1536,128]{1,0:T(8,128)(2,1)S(1)} %copy-done.17), channel_id=1, source_target_pairs={{0,6},{2,0},{4,2},{6,4},{1,7},{3,1},{5,3},{7,5},{8,14},{10,8},{12,... | collective-permute-start | bytes 1179656 | tf_op jit(solution)/shard_map/ppermute | solution.py:22
  75.2 10.6 %collective-permute-start.4 = (bf16[1536,128]{1,0:T(8,128)(2,1)S(1)}, bf16[1536,128]{1,0:T(8,128)(2,1)S(1)}, u32[]{:S(2)}, u32[]{:S(2)}) collective-permute-start(bf16[1536,128]{1,0:T(8,128)(2,1)S(1)} %slice_bitcast_fusion.1), channel_id=1, source_target_pairs={{0,2},{2,4},{4,6},{6,0},{1,3},{3,5},{5,7},{7,1},{8,10},{10,12},{12... | collective-permute-start | bytes 1179656 | tf_op jit(solution)/shard_map/ppermute | solution.py:22
  83.8 4.2 %collective-permute-start.11 = (bf16[1536,128]{1,0:T(8,128)(2,1)S(1)}, bf16[1536,128]{1,0:T(8,128)(2,1)S(1)}, u32[]{:S(2)}, u32[]{:S(2)}) collective-permute-start(bf16[1536,128]{1,0:T(8,128)(2,1)S(1)} %collective-permute-done.3.refs_6_), channel_id=1, source_target_pairs={{0,1},{1,0},{2,3},{3,2},{4,5},{5,4},{6,7},{7,6},{8,9},{9,8},{10,11... | collective-permute-start | bytes 1179656 | tf_op jit(solution)/shard_map/ppermute | solution.py:22
  85.8 3.4 %collective-permute-start.12 = (bf16[1536,128]{1,0:T(8,128)(2,1)S(1)}, bf16[1536,128]{1,0:T(8,128)(2,1)S(1)}, u32[]{:S(2)}, u32[]{:S(2)}) collective-permute-start(bf16[1536,128]{1,0:T(8,128)(2,1)S(1)} %collective-permute-done.4.refs_8_), channel_id=1, source_target_pairs={{0,1},{1,0},{2,3},{3,2},{4,5},{5,4},{6,7},{7,6},{8,9},{9,8},{10,11... | collective-permute-start | bytes 1179656 | tf_op jit(solution)/shard_map/ppermute | solution.py:22
  105.3 39.1 %collective-permute-start.5 = (bf16[128,3072]{1,0:T(8,128)(2,1)}, bf16[128,3072]{1,0:T(8,128)(2,1)}, u32[]{:S(2)}, u32[]{:S(2)}) collective-permute-start(bf16[128,3072]{1,0:T(8,128)(2,1)} %get-tuple-element.30), channel_id=1, source_target_pairs={{0,2},{2,4},{4,6},{6,0},{1,3},{3,5},{5,7},{7,1},{8,10},{10,12},{12... | collective-permute-start | bytes 2359304 | tf_op jit(solution)/shard_map/ppermute | solution.py:22
  105.3 39.1 %collective-permute-start.6 = (bf16[128,3072]{1,0:T(8,128)(2,1)}, bf16[128,3072]{1,0:T(8,128)(2,1)}, u32[]{:S(2)}, u32[]{:S(2)}) collective-permute-start(bf16[128,3072]{1,0:T(8,128)(2,1)} %get-tuple-element.31), channel_id=1, source_target_pairs={{0,4},{2,6},{4,0},{6,2},{1,5},{3,7},{5,1},{7,3},{8,12},{10,14},{12... | collective-permute-start | bytes 2359304 | tf_op jit(solution)/shard_map/ppermute | solution.py:22
  107.0 37.3 %collective-permute-start.7 = (bf16[128,3072]{1,0:T(8,128)(2,1)}, bf16[128,3072]{1,0:T(8,128)(2,1)}, u32[]{:S(2)}, u32[]{:S(2)}) collective-permute-start(bf16[128,3072]{1,0:T(8,128)(2,1)} %get-tuple-element.32), channel_id=1, source_target_pairs={{0,6},{2,0},{4,2},{6,4},{1,7},{3,1},{5,3},{7,5},{8,14},{10,8},{12,... | collective-permute-start | bytes 2359304 | tf_op jit(solution)/shard_map/ppermute | solution.py:22
  108.0 1.7 %copy-start.9 = (bf16[2,1536,384]{2,1,0:T(8,128)(2,1)S(1)}, bf16[2,1536,384]{2,1,0:T(8,128)(2,1)}, u32[]{:S(2)}) copy-start(bf16[2,1536,384]{2,1,0:T(8,128)(2,1)} %copy-done.8) | copy-start | bytes 7077892
  130.8 17.6 %all-to-all-start.5 = ((f32[32,8,128]{2,1,0:T(8,128)}), f32[32,8,128]{2,1,0:T(8,128)S(1)}, u32[]{:S(2)}, u32[]{:S(2)}) async-start(f32[32,8,128]{2,1,0:T(8,128)} %shard_map.95), calls=%async_computation.5 | async-start | bytes 262144 | tf_op jit(solution)/shard_map/all_to_all | solution.py:26
  148.4 1.7 %copy-start.10 = (bf16[2,1536,384]{2,1,0:T(8,128)(2,1)S(1)}, bf16[2,1536,384]{2,1,0:T(8,128)(2,1)}, u32[]{:S(2)}) copy-start(bf16[2,1536,384]{2,1,0:T(8,128)(2,1)} %copy-done.8) | copy-start | bytes 7077892
  (12 other events, 14.0 us)

commit v3 on v2

v3 whole, which is shorter than its diff:
```python
import functools

import jax
import jax.numpy as jnp
from jax import lax
from jax.experimental import pallas as pl
from jax.experimental.pallas import tpu as pltpu
from jax.sharding import Mesh, PartitionSpec as P

F32 = jnp.float32
BF16 = jnp.bfloat16
NX, NY, NZ, NC = 4, 4, 8, 2
DP, MP, PLANE = ("z", "x"), ("y", "c"), ("x", "y")
N_DP = NZ * NX
HALF, COLS, RANK, BLOCK, D = 1536, 384, 64, 128, 3072
PART = HALF // 2
TILE = 512
STEPS = HALF // TILE
HIGHEST = lax.Precision.HIGHEST


def ring(value, axis, size, shift):
    return lax.ppermute(value, axis, [(i, (i + shift) % size) for i in range(size)])


def exchange(value, axes):
    return lax.all_to_all(value, axes, 0, 0, tiled=True)


def call(kernel, outs, flops, grid=None, pins=(), near=(), prefetch=False, **kwargs):
    if prefetch:
        names = ("in_specs", "out_specs", "scratch_shapes")
        spec = {name: kwargs.pop(name) for name in names if name in kwargs}
        kwargs["grid_spec"] = pltpu.PrefetchScalarGridSpec(
            num_scalar_prefetch=1, grid=grid, **spec
        )
        grid = None
    made = pl.pallas_call(
        kernel,
        out_shape=outs,
        compiler_params=pltpu.CompilerParams(vmem_limit_bytes=16 * 2**20),
        cost_estimate=pl.CostEstimate(
            flops=int(flops), bytes_accessed=1000, transcendentals=0
        ),
        **({} if grid is None else {"grid": grid}),
        **kwargs,
    )
    held = pltpu.with_memory_space_constraint
    where = {n: pltpu.HBM for n in pins} | {n: pltpu.VMEM for n in near}
    return lambda *args: made(
        *(held(v, where[n]) if n in where else v for n, v in enumerate(args))
    )


def out(shape, dtype=F32):
    return jax.ShapeDtypeStruct(shape, dtype)


def far_out(shape, dtype=F32):
    return pltpu.HBM(shape, dtype)


def dot(a, b, dims=((1,), (0,)), precision=None):
    return lax.dot_general(a, b, (dims, ((), ())), precision=precision, preferred_element_type=F32)


def two(value):
    high = value.astype(BF16)
    return high, (value - high.astype(F32)).astype(BF16)


def lanes(shape):
    return lax.broadcasted_iota(jnp.int32, shape, 1)


def sides(q):
    zero = jnp.zeros_like(q)
    return jnp.concatenate([q, zero], axis=0), jnp.concatenate([zero, q], axis=0)


ROWS = ((1,), (1,))


def t_kernel(cot_ref, q_ref, out_ref):
    left, right = sides(q_ref[...].astype(BF16))
    cot = cot_ref[...].reshape(4, 2, 64, COLS)
    first, second = cot[:, 0].reshape(256, COLS), cot[:, 1].reshape(256, COLS)
    both = dot(first, left, ROWS) + dot(second, right, ROWS)
    out_ref[...] = both.reshape(4, 64, 128)


def t_rows(cot, q):
    return call(
        t_kernel,
        out((8, 64, 128)),
        1e3,
        grid=(2,),
        pins=(0, 1),
        in_specs=[
            pl.BlockSpec((512, COLS), lambda i: (i, 0)),
            pl.BlockSpec((RANK, COLS), lambda i: (0, 0)),
        ],
        out_specs=pl.BlockSpec((4, 64, 128), lambda i: (i, 0, 0)),
    )(cot, q)


def f_kernel(old_ref, q_ref, first_ref, second_ref, fq_ref, act0_ref, act1_ref):
    left, right = sides(q_ref[...].astype(BF16))
    fq_ref[...] = dot(old_ref[0], left, ROWS) + dot(old_ref[1], right, ROWS)
    act0_ref[...] = first_ref[...].T
    act1_ref[...] = second_ref[...].T


def f_rows(old, q, act):
    return call(
        f_kernel,
        [far_out((HALF, 128))] + [out((HALF, BLOCK), BF16)] * 2,
        1e3,
        grid=(STEPS,),
        pins=(0, 1, 2, 3),
        in_specs=[
            pl.BlockSpec((2, TILE, COLS), lambda i: (0, i, 0)),
            pl.BlockSpec((RANK, COLS), lambda i: (0, 0)),
            pl.BlockSpec((BLOCK, TILE), lambda i: (0, i)),
            pl.BlockSpec((BLOCK, TILE), lambda i: (0, i + STEPS)),
        ],
        out_specs=[
            pl.BlockSpec((TILE, 128), lambda i: (i, 0)),
            pl.BlockSpec((TILE, BLOCK), lambda i: (i, 0)),
            pl.BlockSpec((TILE, BLOCK), lambda i: (i, 0)),
        ],
    )(old, q, act, act)


def p_kernel(place_ref, t_ref, act0_ref, act1_ref, fq_ref, keep_ref, send_ref):
    t = jnp.sum(t_ref[...], axis=0)
    low_lane = lanes(t.shape) < 64
    turned = pltpu.roll(t, 64, 1)
    rhs = jnp.concatenate(
        [
            jnp.where(low_lane, t, 0.0),
            jnp.where(low_lane, turned, 0.0),
            jnp.where(low_lane, 0.0, turned),
            jnp.where(low_lane, 0.0, t),
        ],
        axis=0,
    )
    lhs = jnp.concatenate([act0_ref[...], act1_ref[...]], axis=1)
    both = dot(lhs, jnp.concatenate(two(rhs), axis=1))
    total = both[:, :128] + both[:, 128:] + fq_ref[...]
    for n, ref in enumerate((keep_ref, send_ref)):

        @pl.when(pl.program_id(0) == n)
        def _():
            ref[...] = total


def half_of(i, place):
    return lax.rem(place[1] + i, 2)


def p_rows(place, t, act0, act1, fq):
    return call(
        p_kernel,
        [out((PART, 128))] * 2,
        1e3,
        grid=(2,),
        pins=(4,),
        prefetch=True,
        in_specs=[
            pl.BlockSpec((8, 64, 128), lambda i, place: (0, 0, 0)),
            pl.BlockSpec((PART, BLOCK), lambda i, place: (half_of(i, place), 0)),
            pl.BlockSpec((PART, BLOCK), lambda i, place: (half_of(i, place), 0)),
            pl.BlockSpec((PART, 128), lambda i, place: (half_of(i, place), 0)),
        ],
        out_specs=[pl.BlockSpec((PART, 128), lambda i, place: (0, 0))] * 2,
    )(place, t, act0, act1, fq)


def pair_kernel(a_ref, b_ref, out_ref):
    out_ref[...] = a_ref[...] + b_ref[...]


def pair_sum(a, b):
    return call(pair_kernel, far_out(a.shape), 1e3)(a, b)


def sum_kernel(in_ref, out_ref):
    total = jnp.sum(in_ref[...].astype(F32), axis=0)
    out_ref[...] = jnp.broadcast_to(total[None], out_ref.shape)


def sum_spread(value, count):
    return call(sum_kernel, out((count,) + value.shape[1:]), 1e3)(value)


def merge_kernel(place_ref, cot_ref, old_ref, *refs):
    acts, (out_ref, cot_rel) = refs[:-2], refs[-2:]
    y, c = place_ref[0], place_ref[1]

    @pl.when(pl.program_id(0) == 0)
    def _():
        for n, k in enumerate((0, 3, 1, 2)):
            for m in range(2):
                block = lax.rem(y + k, NY) * 2 + (c if m == 0 else 1 - c)
                cot_rel[pl.ds((2 * n + m) * BLOCK, BLOCK), :] = cot_ref[
                    pl.ds(pl.multiple_of(block * BLOCK, BLOCK), BLOCK), :
                ]

    for h in range(2):
        rows = jnp.concatenate([ref[...] for ref in acts[8 * h : 8 * h + 8]], axis=1)
        gradient = dot(rows, cot_rel[...])
        out_ref[h] = (gradient + old_ref[h].astype(F32)).astype(BF16)


def merge(place, cot, old, acts):
    return call(
        merge_kernel,
        pltpu.VMEM((2, HALF, COLS), BF16),
        1.5e10,
        grid=(STEPS,),
        pins=tuple(range(1, 19)),
        in_specs=[
            pl.BlockSpec(memory_space=pltpu.SMEM),
            pl.BlockSpec(cot.shape, lambda i: (0, 0)),
            pl.BlockSpec((2, TILE, COLS), lambda i: (0, i, 0)),
        ]
        + [pl.BlockSpec((TILE, BLOCK), lambda i: (i, 0))] * 16,
        out_specs=pl.BlockSpec((2, TILE, COLS), lambda i: (0, i, 0)),
        scratch_shapes=[pltpu.VMEM((8 * BLOCK, COLS), BF16)],
    )(place, cot, old, *acts)


def s_kernel(place_ref, p_ref, merged_ref, before_ref, out_ref):
    p = jnp.concatenate(two(p_ref[...]), axis=1)
    first = dot(p, merged_ref[0], ((0,), (0,)))
    second = dot(p, merged_ref[1], ((0,), (0,)))
    s = first[:64] + first[128:192] + second[64:128] + second[192:]
    for n in range(3):
        at = pl.ds(64 * n, 64)
        out_ref[at, :] = before_ref[at, :] + s[:, 128 * n : 128 * n + 128]
    out_ref[pl.ds(192, 64), :] = before_ref[pl.ds(192, 64), :]


def s_rows(place, p, merged, before, flip):
    return call(
        s_kernel,
        out((256, 128)),
        1e3,
        grid=(1,),
        near=(2,),
        prefetch=True,
        in_specs=[
            pl.BlockSpec((PART, 128), lambda i, place: (0, 0)),
            pl.BlockSpec((2, PART, COLS), lambda i, place: (0, half_of(flip, place), 0)),
            pl.BlockSpec((256, 128), lambda i, place: (0, 0)),
        ],
        out_specs=pl.BlockSpec((256, 128), lambda i, place: (0, 0)),
    )(place, p, merged, before)


def gram_half(p):
    high, rest = p.astype(BF16), p - p.astype(BF16).astype(F32)
    split = jnp.concatenate([high, *two(rest)], axis=1)
    blocks = dot(split, split, ((0,), (0,)))
    part = lambda a, b: blocks[128 * a : 128 * a + 128, 128 * b : 128 * b + 128]
    small = part(0, 2) + part(2, 0) + part(1, 1)
    return part(0, 0) + (part(0, 1) + part(1, 0) + small)


def inverse_kernel(own_ref, other_ref, inverse_ref):
    pair = gram_half(own_ref[...]) + gram_half(other_ref[...])
    gram = pair[:64, :64] + pair[64:, 64:]
    row = lax.broadcasted_iota(jnp.int32, (64, 64), 0)
    unit = jnp.where(row == lanes((64, 64)), 1.0, 0.0)
    table = jnp.concatenate([gram, unit], axis=1)
    tiles = [table[8 * i : 8 * i + 8] for i in range(8)]
    sub = lax.broadcasted_iota(jnp.int32, (8, 128), 0)
    for j in range(0, 64, 4):
        at, inner = j // 8, j % 8
        columns = [
            {i: jnp.broadcast_to(tiles[i][:, j + k : j + k + 1], (8, 128)) for i in range(at, 8)}
            for k in range(4)
        ]
        for k in range(4):
            n = inner + k
            scale = 1.0 / columns[k][at][n : n + 1]
            heads = [columns[m][at][n : n + 1] for m in range(k + 1, 4)]
            pivot = tiles[at][n : n + 1]
            for i in range(at, 8):
                factor = columns[k][i] * scale
                if i == at:
                    factor = jnp.where(sub > n, factor, 0.0)
                for m, head in zip(range(k + 1, 4), heads):
                    columns[m][i] = columns[m][i] - factor * head
                tiles[i] = tiles[i] - factor * pivot
    table = jnp.concatenate(tiles, axis=0)
    lane = lanes((64, 128))
    here = lax.broadcasted_iota(jnp.int32, (64, 128), 0) == lane
    diagonal = jnp.sum(jnp.where(here, table, 0.0), axis=1, keepdims=True)
    right = jnp.where(lane >= 64, table, 0.0) / jnp.sqrt(diagonal)
    inverse_ref[...] = jnp.concatenate([pltpu.roll(right, 64, 1), right], axis=0)


def basis_kernel(place_ref, own_ref, other_ref, inverse_ref, basis_ref, packed_ref):
    inverse = inverse_ref[...]
    for n, ref in enumerate((own_ref, other_ref)):
        half = lax.rem(place_ref[1] + n, 2)
        start = pl.multiple_of(half * PART, PART)
        p = ref[...]
        packed_ref[pl.ds(start, PART), :] = dot(p, inverse, ROWS, HIGHEST)
        turned = dot(inverse, p, ROWS, HIGHEST)
        for h in range(2):
            at = pl.ds(pl.multiple_of(start + h * HALF, PART), PART)
            basis_ref[:, at] = turned[64 * h : 64 * h + 64]


def inverse_rows(own, other):
    return call(inverse_kernel, out((128, 128)), 1e3)(own, other)


def basis_rows(place, own, other, inverse):
    return call(
        basis_kernel,
        [out((RANK, D)), out((HALF, 128))],
        1e3,
        in_specs=[pl.BlockSpec(memory_space=pltpu.SMEM)] + [pl.BlockSpec()] * 3,
    )(place, own, other, inverse)


def last_kernel(s_ref, inverse_ref, packed_ref, merged_ref, q_ref, new_ref, rhs):
    @pl.when(pl.program_id(0) == 0)
    def _():
        s = jnp.concatenate([s_ref[pl.ds(64 * n, 64), :] for n in range(3)], axis=1)
        q = dot(inverse_ref[0:64, 0:64], s, precision=HIGHEST) * (1.0 / N_DP)
        q_ref[...] = q
        high, low = two(q)
        zero = jnp.zeros_like(high)
        for h in range(2):
            pair = lambda v: [zero, v] if h else [v, zero]
            rhs[h] = jnp.concatenate(pair(high) + pair(high) + pair(low), axis=0)

    high, low = two(packed_ref[...])
    lhs = jnp.concatenate([high, low, high], axis=1)
    for h in range(2):
        new_ref[h] = (merged_ref[h].astype(F32) - dot(lhs, rhs[h])).astype(BF16)


def last(s, inverse, packed, merged):
    return call(
        last_kernel,
        [far_out((RANK, COLS)), far_out((2, HALF, COLS), BF16)],
        1e3,
        grid=(STEPS,),
        near=(3,),
        in_specs=[
            pl.BlockSpec((256, 128), lambda i: (0, 0)),
            pl.BlockSpec((128, 128), lambda i: (0, 0)),
            pl.BlockSpec((TILE, 128), lambda i: (i, 0)),
            pl.BlockSpec((2, TILE, COLS), lambda i: (0, i, 0)),
        ],
        out_specs=[
            pl.BlockSpec((RANK, COLS), lambda i: (0, 0)),
            pl.BlockSpec((2, TILE, COLS), lambda i: (0, i, 0)),
        ],
        scratch_shapes=[pltpu.VMEM((2, 384, COLS), BF16)],
    )(s, inverse, packed, merged)


def grad_kernel(place_ref, cot_ref, weight_ref, cot_side_ref, weight_side_ref, *refs):
    out_refs, rows = refs[:-1], refs[-1]

    @pl.when(pl.program_id(0) == 0)
    def _():
        for k in range(NY):
            block = lax.rem(place_ref[0] + k, NY) * 2 + place_ref[1]
            start = pl.multiple_of(block * BLOCK, BLOCK)
            for n, ref in enumerate((cot_ref, cot_side_ref)):
                rows[n * COLS : (n + 1) * COLS, k * BLOCK : (k + 1) * BLOCK] = ref[
                    pl.ds(start, BLOCK), :
                ].T

    weight = jnp.concatenate([weight_ref[...], weight_side_ref[...]], axis=1)
    part = dot(weight, rows[...]).astype(BF16)
    for k, ref in enumerate(out_refs):
        ref[...] = part[:, k * BLOCK : (k + 1) * BLOCK]


def grad_parts(place, cot, cot_side, weight, weight_side):
    whole = pl.BlockSpec(cot.shape, lambda i: (0, 0))
    tile = pl.BlockSpec((TILE, COLS), lambda i: (i, 0))
    return call(
        grad_kernel,
        [far_out((D, BLOCK), BF16)] * NY,
        1e3,
        grid=(D // TILE,),
        pins=(1, 3),
        in_specs=[pl.BlockSpec(memory_space=pltpu.SMEM), whole, tile, whole, tile],
        out_specs=[pl.BlockSpec((TILE, BLOCK), lambda i: (i, 0))] * NY,
        scratch_shapes=[pltpu.VMEM((2 * COLS, NY * BLOCK), BF16)],
    )(place, cot, weight, cot_side, weight_side)


def add_kernel(*refs):
    total = refs[0][...].astype(F32)
    for ref in refs[1:NY]:
        total += ref[...].astype(F32)
    refs[NY][...] = total.astype(BF16).T


def add_four(*parts):
    return call(
        add_kernel,
        far_out((BLOCK, D), BF16),
        1e3,
        grid=(2,),
        pins=(0,),
        in_specs=[pl.BlockSpec((HALF, BLOCK), lambda i: (i, 0))] * NY,
        out_specs=pl.BlockSpec((BLOCK, HALF), lambda i: (0, i)),
    )(*parts)


def after(values, *earlier):
    held = lax.optimization_barrier((tuple(values), earlier))
    return list(held[0])


def local(activations, cotangent, weight, feedback, q_previous):
    act, cot = activations[0], cotangent[0]
    old = feedback[0].reshape(2, HALF, COLS)
    place = jnp.stack([lax.axis_index("y"), lax.axis_index("c")]).astype(jnp.int32)

    q = q_previous.T
    t_send = t_rows(cot, q)
    t = exchange(t_send, MP)
    side = lambda value: ring(value, "c", NC, 1)
    act, cot_later, weight = after([act, cot, weight], t_send)
    fq, own0, own1 = f_rows(old, q, act)
    cot_side, weight_side = side(cot_later), side(weight)
    keep, p_send = p_rows(place, t, own0, own1, fq)
    p_send = pair_sum(keep, side(p_send)).reshape(16, 48, 128)

    mine, *rest = grad_parts(place, cot_later, cot_side, weight, weight_side)

    go0, go1 = after([own0, own1], t)
    low1, high0 = ring(go1, "y", NY, 1), ring(go0, "y", NY, 3)
    (p_plane,) = after([exchange(p_send, PLANE)], mine)
    p_sum = sum_spread(p_plane, NZ)
    go0, go1, far_go0, far_go1 = after([own0, own1, high0, low1], p_sum)
    low0, high1 = ring(go0, "y", NY, 1), ring(go1, "y", NY, 3)
    far0, far1 = ring(far_go0, "y", NY, 3), ring(far_go1, "y", NY, 1)

    p_z = exchange(p_sum, "z")
    p_half = sum_spread(p_z, 16)
    p = exchange(p_half, PLANE).reshape(PART, 128)
    later = after([low0, high0, far0, low1, high1, far1], p_half)

    own_sides = [side(value) for value in after([own0, own1], p_send)]
    sides = [side(value) for value in later]
    pairs = [(own0, own_sides[0]), *zip(later[:3], sides[:3])]
    pairs += [(own1, own_sides[1]), *zip(later[3:], sides[3:])]
    acts = [value for pair in pairs for value in pair]
    merged = merge(place, cot, old, acts)
    (p,) = after([p], merged)
    p_other = side(p)

    rest = after(rest, merged)
    parts = [ring(value, "y", NY, k) for k, value in zip((1, 2, 3), rest)]
    input_grad = add_four(mine, *parts)

    s_send = s_rows(place, p, merged, jnp.zeros((256, 128), F32), 0)
    s_send = s_rows(place, p_other, merged, s_send, 1)
    s = exchange(s_send.reshape(N_DP, 8, 128), DP)
    p, p_other = after([p, p_other], s_send)
    inverse = inverse_rows(p, p_other)
    (s,) = after([s], inverse)
    basis, packed = basis_rows(place, p, p_other, inverse)
    s = exchange(sum_spread(s, N_DP), DP).reshape(256, 128)
    (inverse,) = after([inverse], input_grad, basis)
    q_factor, feedback_new = last(s, inverse, packed, merged)
    return (
        input_grad[None],
        basis.T,
        q_factor.T,
        feedback_new.reshape(1, D, COLS),
    )


def solution(mesh):
    fine = Mesh(mesh.devices.reshape(NZ, NX, NY, NC), ("z", "x", "y", "c"))
    placed = (P(DP, MP, None), P(DP, None, MP), P(None, MP), P(DP, None, MP), P(MP, None))
    return jax.shard_map(
        local,
        mesh=fine,
        in_specs=placed,
        out_specs=(P(DP, MP, None), P(), P(MP, None), P(DP, None, MP)),
        check_vma=False,
    )
```

time: 158 us -> 126 us (0.80); the launches traced: 155 us -> 125 us
  local copies, waits for them, and re-layouts: 23.5 us -> 3.14 us
  blocking collectives: 18.3 us -> 0 us
  starting transfers between devices: 44.7 us -> 57.5 us
  waiting for transfers between devices: 26.2 us -> 22.4 us
    all_to_all x1 -> x0, blocking collectives: 18.3 us -> none  [exchange(): return lax.all_to_all(value, axes, 0, 0, tiled=True)]
    unnamed x39 -> x28, local copies, waits for them, and re-layouts: 20.7 us -> 3.13 us
    ppermute x13 -> x21, starting transfers between devices: 12 us -> 25.7 us  [ring(): lax.ppermute(value, axis, [(i, (i + shift) % size) for i in range(size)])]
    squeeze x2 -> x0, local copies, waits for them, and re-layouts: 2.79 us -> none  [local(): from_low, from_high = after([low[1], high[0]], p_mp)]
    all_to_all x5 -> x6, waiting for transfers between devices: 16.8 us -> 14.7 us  [exchange(): return lax.all_to_all(value, axes, 0, 0, tiled=True)]
    ppermute x13 -> x21, waiting for transfers between devices: 9.38 us -> 7.71 us  [ring(): lax.ppermute(value, axis, [(i, (i + shift) % size) for i in range(size)])]
    all_to_all x5 -> x6, starting transfers between devices: 32.7 us -> 31.7 us  [exchange(): return lax.all_to_all(value, axes, 0, 0, tiled=True)]
    pallas_call x13 -> x15, Pallas kernels: 41.9 us -> 41.3 us  [call(): made(*(held(v, where[n]) if n in where else v for n, v in enumerate(args)))]
  transfers between devices with their start and end apart: 18 -> 27, of which waited for: 5 -> 9; matrix products, arithmetic and copies ran while one was open for 3% -> 0% of each run, Pallas kernels for 23% -> 28%
where the time goes in v3:
time: 126 us; the launch traced here: 125 us
  starting transfers between devices  57.5 us (46%)
  Pallas kernels  41.3 us (33%)
  waiting for transfers between devices  22.4 us (18%)
  local copies, waits for them, and re-layouts  3.14 us (2%)
    pallas_call x15, Pallas kernels, call(): made(*(held(v, where[n]) if n in where else v for n, v in enumerate(args)))  41.3 us
    all_to_all x6, starting transfers between devices, exchange(): return lax.all_to_all(value, axes, 0, 0, tiled=True)  31.7 us
    ppermute x21, starting transfers between devices, ring(): lax.ppermute(value, axis, [(i, (i + shift) % size) for i in range(size)])  25.7 us
    all_to_all x6, waiting for transfers between devices, exchange(): return lax.all_to_all(value, axes, 0, 0, tiled=True)  14.7 us
    ppermute x21, waiting for transfers between devices, ring(): lax.ppermute(value, axis, [(i, (i + shift) % size) for i in range(size)])  7.71 us
    unnamed x28, local copies, waits for them, and re-layouts  3.13 us
  transfers between devices with their start and end apart: 27, of which 9 were waited for; matrix products, arithmetic and copies ran while one was open for 0% of the time, Pallas kernels for 28%

profile of v3, /device:TPU:1, one launch (start us, length us, event | category | flops | bytes accessed | tf_op | source)
XLA Modules:
  0.0 125.2 jit_solution(12971101850336900460)
XLA Ops:
  0.6 2.2 %shard_map.84 = f32[8,64,128]{2,1,0:T(8,128)} custom-call(bf16[1024,384]{1,0:T(8,128)(2,1)} %bitcast.19, f32[64,384]{1,0:T(8,128)} %bitcast.29), custom_call_target="tpu_custom_call" | custom-call | flops 1000 | bytes 1000 | tf_op jit(solution)/shard_map/pallas_call | solution.py:50
  2.9 3.2 %collective-permute-start.1 = (bf16[3072,384]{1,0:T(8,128)(2,1)}, bf16[3072,384]{1,0:T(8,128)(2,1)}, u32[]{:S(2)}, u32[]{:S(2)}) collective-permute-start(bf16[3072,384]{1,0:T(8,128)(2,1)} %weight_ref), channel_id=1, source_target_pairs={{0,1},{1,0},{2,3},{3,2},{4,5},{5,4},{6,7},{7,6},{8,9},{9,8},{10,11... | collective-permute-start | bytes 7077896 | tf_op jit(solution)/shard_map/ppermute | solution.py:23
  6.1 3.4 %all-to-all-start = ((f32[8,64,128]{2,1,0:T(8,128)}), f32[8,64,128]{2,1,0:T(8,128)S(1)}, u32[]{:S(2)}, u32[]{:S(2)}) async-start(f32[8,64,128]{2,1,0:T(8,128)} %shard_map.84), calls=%async_computation | async-start | bytes 524288 | tf_op jit(solution)/shard_map/all_to_all | solution.py:27
  9.7 3.9 %shard_map.86 = (f32[1536,128]{1,0:T(8,128)}, bf16[1536,128]{1,0:T(8,128)(2,1)S(1)}, bf16[1536,128]{1,0:T(8,128)(2,1)S(1)}) custom-call(bf16[2,1536,384]{2,1,0:T(8,128)(2,1)} %bitcast.25, f32[64,384]{1,0:T(8,128)} %bitcast.30, bf16[128,3072]{1,0:T(8,128)(2,1)} %bitcast.23, bf16[128,3072]{1,0:T(8,128)(2,1)} %bitcast.24), custom_call_target="tpu_custom_call" | custom-call | flops 1000 | bytes 1000 | tf_op jit(solution)/shard_map/pallas_call | solution.py:50
  13.6 2.3 %all-to-all-done.t_ref = f32[8,64,128]{2,1,0:T(8,128)S(1)} async-done(((f32[8,64,128]{2,1,0:T(8,128)}), f32[8,64,128]{2,1,0:T(8,128)S(1)}, u32[]{:S(2)}, u32[]{:S(2)}) %all-to-all-start) | async-done | bytes 262176 | tf_op jit(solution)/shard_map/all_to_all | solution.py:27
  15.9 2.3 %shard_map.87 = (f32[768,128]{1,0:T(8,128)S(1)}, f32[768,128]{1,0:T(8,128)S(1)}) custom-call(s32[2]{0:T(128)S(1)} %pad_add_fusion.place_ref, f32[8,64,128]{2,1,0:T(8,128)S(1)} %all-to-all-done.t_ref, bf16[1536,128]{1,0:T(8,128)(2,1)S(1)} %get-tuple-element.59.act0_ref.refs_0_, bf16[1536,128]{1,0:T(8,128)(2,1)S(1)} %get-tuple-element.66.act1_ref.refs_8_, ...), custom_call_target="tpu_custom_call" | custom-call | flops 1000 | bytes 1000 | tf_op jit(solution)/shard_map/pallas_call | solution.py:50
  21.6 5.5 %all-to-all-start.1 = ((f32[16,48,128]{2,1,0:T(8,128)}), f32[16,48,128]{2,1,0:T(8,128)S(1)}, u32[]{:S(2)}, u32[]{:S(2)}) async-start(f32[16,48,128]{2,1,0:T(8,128)} %bitcast.27), calls=%async_computation.1 | async-start | bytes 786432 | tf_op jit(solution)/shard_map/all_to_all | solution.py:27
  27.1 7.4 %shard_map.85 = (bf16[3072,128]{1,0:T(8,128)(2,1)}, bf16[3072,128]{1,0:T(8,128)(2,1)}, bf16[3072,128]{1,0:T(8,128)(2,1)}, bf16[3072,128]{1,0:T(8,128)(2,1)}) custom-call(s32[2]{0:T(128)S(1)} %pad_add_fusion.place_ref, bf16[1024,384]{1,0:T(8,128)(2,1)} %bitcast.21, bf16[3072,384]{1,0:T(8,128)(2,1)S(1)} %copy-done, ...), custom_call_target="tpu_custom_call" | custom-call | flops 1000 | bytes 1000 | tf_op jit(solution)/shard_map/pallas_call | solution.py:50
  36.6 2.1 %collective-permute-start.7 = (bf16[1536,128]{1,0:T(8,128)(2,1)}, bf16[1536,128]{1,0:T(8,128)(2,1)S(1)}, u32[]{:S(2)}, u32[]{:S(2)}) collective-permute-start(bf16[1536,128]{1,0:T(8,128)(2,1)} %collective-permute-done.4.refs_4_), channel_id=1, source_target_pairs={{0,6},{2,0},{4,2},{6,4},{1,7},{3,1},{5,3},{7,5},{8,14},{10,8},{12,... | collective-permute-start | bytes 1179656 | tf_op jit(solution)/shard_map/ppermute | solution.py:23
  40.2 8.2 %all-to-all-start.2 = ((f32[8,48,128]{2,1,0:T(8,128)}), f32[8,48,128]{2,1,0:T(8,128)S(1)}, u32[]{:S(2)}, u32[]{:S(2)}) async-start(f32[8,48,128]{2,1,0:T(8,128)} %shard_map.89), calls=%async_computation.2 | async-start | bytes 393216 | tf_op jit(solution)/shard_map/all_to_all | solution.py:27
  48.4 4.0 %collective-permute-start.3 = (bf16[1536,128]{1,0:T(8,128)(2,1)S(1)}, bf16[1536,128]{1,0:T(8,128)(2,1)S(1)}, u32[]{:S(2)}, u32[]{:S(2)}) collective-permute-start(bf16[1536,128]{1,0:T(8,128)(2,1)S(1)} %get-tuple-element.59.act0_ref.refs_0_), channel_id=1, source_target_pairs={{0,1},{1,0},{2,3},{3,2},{4,5},{5,4},{6,7},{7,6},{8,9},{9,8},{10,11... | collective-permute-start | bytes 1179656 | tf_op jit(solution)/shard_map/ppermute | solution.py:23
  52.4 4.7 %all-to-all-done.2.in_ref = f32[8,48,128]{2,1,0:T(8,128)S(1)} async-done(((f32[8,48,128]{2,1,0:T(8,128)}), f32[8,48,128]{2,1,0:T(8,128)S(1)}, u32[]{:S(2)}, u32[]{:S(2)}) %all-to-all-start.2) | async-done | bytes 196640 | tf_op jit(solution)/shard_map/all_to_all | solution.py:27
  58.0 5.0 %collective-permute-start.13 = (bf16[1536,128]{1,0:T(8,128)(2,1)S(1)}, bf16[1536,128]{1,0:T(8,128)(2,1)S(1)}, u32[]{:S(2)}, u32[]{:S(2)}) collective-permute-start(bf16[1536,128]{1,0:T(8,128)(2,1)S(1)} %get-tuple-element.66.act1_ref.refs_8_), channel_id=1, source_target_pairs={{0,1},{1,0},{2,3},{3,2},{4,5},{5,4},{6,7},{7,6},{8,9},{9,8},{10,11... | collective-permute-start | bytes 1179656 | tf_op jit(solution)/shard_map/ppermute | solution.py:23
  66.0 4.2 %all-to-all-start.3 = ((f32[16,48,128]{2,1,0:T(8,128)}), f32[16,48,128]{2,1,0:T(8,128)S(1)}, u32[]{:S(2)}, u32[]{:S(2)}) async-start(f32[16,48,128]{2,1,0:T(8,128)} %shard_map.90), calls=%async_computation.3 | async-start | bytes 786432 | tf_op jit(solution)/shard_map/all_to_all | solution.py:27
  71.8 6.6 %shard_map.91.merged_ref = bf16[2,1536,384]{2,1,0:T(8,128)(2,1)S(1)} custom-call(s32[2]{0:T(128)S(1)} %pad_add_fusion.place_ref, bf16[1024,384]{1,0:T(8,128)(2,1)} %bitcast.22, bf16[2,1536,384]{2,1,0:T(8,128)(2,1)} %bitcast.26, bf16[1536,128]{1,0:T(8,128)(2,1)} %copy-done.3, bf16[1536,128]{1,0:T(8,128)(2,1)} %copy-done.9, bf16[1536,128]{1,0:T(8,128)(2,1)} %copy-done.5, ...), custom_call_target="tpu_custom_call" | custom-call | flops 15000000512 | bytes 1000 | tf_op jit(solution)/shard_map/pallas_call | solution.py:50
  81.1 1.9 %collective-permute-start.18 = (bf16[3072,128]{1,0:T(8,128)(2,1)}, bf16[3072,128]{1,0:T(8,128)(2,1)}, u32[]{:S(2)}, u32[]{:S(2)}) collective-permute-start(bf16[3072,128]{1,0:T(8,128)(2,1)} %get-tuple-element.71), channel_id=1, source_target_pairs={{0,4},{2,6},{4,0},{6,2},{1,5},{3,7},{5,1},{7,3},{8,12},{10,14},{12... | collective-permute-start | bytes 2359304 | tf_op jit(solution)/shard_map/ppermute | solution.py:23
  87.3 6.6 %all-to-all-start.4 = ((f32[32,8,128]{2,1,0:T(8,128)}), f32[32,8,128]{2,1,0:T(8,128)S(1)}, u32[]{:S(2)}, u32[]{:S(2)}) async-start(f32[32,8,128]{2,1,0:T(8,128)} %bitcast.10), calls=%async_computation.4 | async-start | bytes 262144 | tf_op jit(solution)/shard_map/all_to_all | solution.py:27
  94.0 3.6 %shard_map.95.inverse_ref = f32[128,128]{1,0:T(8,128)S(1)} custom-call(f32[768,128]{1,0:T(8,128)S(1)} %bitcast.16, f32[768,128]{1,0:T(8,128)S(1)} %collective-permute-done.20.p_ref.other_ref), custom_call_target="tpu_custom_call" | custom-call | flops 1000 | bytes 1000 | tf_op jit(solution)/shard_map/pallas_call | solution.py:50
  97.6 5.7 %all-to-all-done.4.in_ref = f32[32,8,128]{2,1,0:T(8,128)S(1)} async-done(((f32[32,8,128]{2,1,0:T(8,128)}), f32[32,8,128]{2,1,0:T(8,128)S(1)}, u32[]{:S(2)}, u32[]{:S(2)}) %all-to-all-start.4) | async-done | bytes 131104 | tf_op jit(solution)/shard_map/all_to_all | solution.py:27
  104.0 3.8 %all-to-all-start.5 = ((f32[32,8,128]{2,1,0:T(8,128)}), f32[32,8,128]{2,1,0:T(8,128)S(1)}, u32[]{:S(2)}, u32[]{:S(2)}) async-start(f32[32,8,128]{2,1,0:T(8,128)} %shard_map.97), calls=%async_computation.5 | async-start | bytes 262144 | tf_op jit(solution)/shard_map/all_to_all | solution.py:27
  107.9 2.8 %shard_map.96 = (f32[64,3072]{1,0:T(8,128)}, f32[1536,128]{1,0:T(8,128)S(1)}) custom-call(s32[2]{0:T(128)S(1)} %pad_add_fusion.place_ref, f32[768,128]{1,0:T(8,128)S(1)} %bitcast.17, f32[768,128]{1,0:T(8,128)S(1)} %collective-permute-done.20.p_ref.other_ref, f32[128,128]{1,0:T(8,128)S(1)} %shard_map.95.inverse_ref), custom_call_target="tpu_custom_call" | custom-call | flops 1000 | bytes 1000 | tf_op jit(solution)/shard_map/pallas_call | solution.py:50
  111.6 7.0 %collective-permute-done.17.refs_1_ = bf16[3072,128]{1,0:T(8,128)(2,1)} collective-permute-done((bf16[3072,128]{1,0:T(8,128)(2,1)}, bf16[3072,128]{1,0:T(8,128)(2,1)}, u32[]{:S(2)}, u32[]{:S(2)}) %collective-permute-start.17) | collective-permute-done | bytes 786464 | tf_op jit(solution)/shard_map/ppermute | solution.py:23
  118.9 2.8 %shard_map.92 = bf16[128,3072]{1,0:T(8,128)(2,1)} custom-call(bf16[3072,128]{1,0:T(8,128)(2,1)} %get-tuple-element.45.refs_0_, bf16[3072,128]{1,0:T(8,128)(2,1)} %collective-permute-done.17.refs_1_, bf16[3072,128]{1,0:T(8,128)(2,1)} %collective-permute-done.18.refs_2_, bf16[3072,128]{1,0:T(8,128)(2,1)} %collective-permute-done.19.refs_3_), custom_call_target="tpu_custom_call" | custom-call | flops 1000 | bytes 1000 | tf_op jit(solution)/shard_map/pallas_call | solution.py:50
  121.7 3.5 %shard_map.98 = (f32[64,384]{1,0:T(8,128)}, bf16[2,1536,384]{2,1,0:T(8,128)(2,1)}) custom-call(f32[256,128]{1,0:T(8,128)S(1)} %bitcast.18, f32[128,128]{1,0:T(8,128)S(1)} %shard_map.95.inverse_ref, f32[1536,128]{1,0:T(8,128)S(1)} %copy-done.2, bf16[2,1536,384]{2,1,0:T(8,128)(2,1)S(1)} %shard_map.91.merged_ref), custom_call_target="tpu_custom_call" | custom-call | flops 1000 | bytes 1000 | tf_op jit(solution)/shard_map/pallas_call | solution.py:50
  (75 shorter events, 21.4 us)
Async XLA Ops:
  2.9 24.3 %collective-permute-start.1 = (bf16[3072,384]{1,0:T(8,128)(2,1)}, bf16[3072,384]{1,0:T(8,128)(2,1)}, u32[]{:S(2)}, u32[]{:S(2)}) collective-permute-start(bf16[3072,384]{1,0:T(8,128)(2,1)} %weight_ref), channel_id=1, source_target_pairs={{0,1},{1,0},{2,3},{3,2},{4,5},{5,4},{6,7},{7,6},{8,9},{9,8},{10,11... | collective-permute-start | bytes 7077896 | tf_op jit(solution)/shard_map/ppermute | solution.py:23
  6.1 9.8 %all-to-all-start = ((f32[8,64,128]{2,1,0:T(8,128)}), f32[8,64,128]{2,1,0:T(8,128)S(1)}, u32[]{:S(2)}, u32[]{:S(2)}) async-start(f32[8,64,128]{2,1,0:T(8,128)} %shard_map.84), calls=%async_computation | async-start | bytes 524288 | tf_op jit(solution)/shard_map/all_to_all | solution.py:27
  9.5 17.6 %collective-permute-start = (bf16[1024,384]{1,0:T(8,128)(2,1)}, bf16[1024,384]{1,0:T(8,128)(2,1)}, u32[]{:S(2)}, u32[]{:S(2)}) collective-permute-start(bf16[1024,384]{1,0:T(8,128)(2,1)} %bitcast.20), channel_id=1, source_target_pairs={{0,1},{1,0},{2,3},{3,2},{4,5},{5,4},{6,7},{7,6},{8,9},{9,8},{10,11... | collective-permute-start | bytes 2359304 | tf_op jit(solution)/shard_map/ppermute | solution.py:23
  19.4 16.7 %collective-permute-start.4 = (bf16[1536,128]{1,0:T(8,128)(2,1)S(1)}, bf16[1536,128]{1,0:T(8,128)(2,1)}, u32[]{:S(2)}, u32[]{:S(2)}) collective-permute-start(bf16[1536,128]{1,0:T(8,128)(2,1)S(1)} %get-tuple-element.59.act0_ref.refs_0_), channel_id=1, source_target_pairs={{0,6},{2,0},{4,2},{6,4},{1,7},{3,1},{5,3},{7,5},{8,14},{10,8},{12,... | collective-permute-start | bytes 1179656 | tf_op jit(solution)/shard_map/ppermute | solution.py:23
  20.3 15.8 %collective-permute-start.5 = (bf16[1536,128]{1,0:T(8,128)(2,1)S(1)}, bf16[1536,128]{1,0:T(8,128)(2,1)}, u32[]{:S(2)}, u32[]{:S(2)}) collective-permute-start(bf16[1536,128]{1,0:T(8,128)(2,1)S(1)} %get-tuple-element.66.act1_ref.refs_8_), channel_id=1, source_target_pairs={{0,2},{2,4},{4,6},{6,0},{1,3},{3,5},{5,7},{7,1},{8,10},{10,12},{12... | collective-permute-start | bytes 1179656 | tf_op jit(solution)/shard_map/ppermute | solution.py:23
  21.6 13.7 %all-to-all-start.1 = ((f32[16,48,128]{2,1,0:T(8,128)}), f32[16,48,128]{2,1,0:T(8,128)S(1)}, u32[]{:S(2)}, u32[]{:S(2)}) async-start(f32[16,48,128]{2,1,0:T(8,128)} %bitcast.27), calls=%async_computation.1 | async-start | bytes 786432 | tf_op jit(solution)/shard_map/all_to_all | solution.py:27
  36.1 21.9 %collective-permute-start.6 = (bf16[1536,128]{1,0:T(8,128)(2,1)S(1)}, bf16[1536,128]{1,0:T(8,128)(2,1)S(1)}, u32[]{:S(2)}, u32[]{:S(2)}) collective-permute-start(bf16[1536,128]{1,0:T(8,128)(2,1)S(1)} %get-tuple-element.59.act0_ref.refs_0_), channel_id=1, source_target_pairs={{0,2},{2,4},{4,6},{6,0},{1,3},{3,5},{5,7},{7,1},{8,10},{10,12},{12... | collective-permute-start | bytes 1179656 | tf_op jit(solution)/shard_map/ppermute | solution.py:23
  36.6 26.4 %collective-permute-start.7 = (bf16[1536,128]{1,0:T(8,128)(2,1)}, bf16[1536,128]{1,0:T(8,128)(2,1)S(1)}, u32[]{:S(2)}, u32[]{:S(2)}) collective-permute-start(bf16[1536,128]{1,0:T(8,128)(2,1)} %collective-permute-done.4.refs_4_), channel_id=1, source_target_pairs={{0,6},{2,0},{4,2},{6,4},{1,7},{3,1},{5,3},{7,5},{8,14},{10,8},{12,... | collective-permute-start | bytes 1179656 | tf_op jit(solution)/shard_map/ppermute | solution.py:23
  38.8 24.2 %collective-permute-start.8 = (bf16[1536,128]{1,0:T(8,128)(2,1)S(1)}, bf16[1536,128]{1,0:T(8,128)(2,1)S(1)}, u32[]{:S(2)}, u32[]{:S(2)}) collective-permute-start(bf16[1536,128]{1,0:T(8,128)(2,1)S(1)} %get-tuple-element.66.act1_ref.refs_8_), channel_id=1, source_target_pairs={{0,6},{2,0},{4,2},{6,4},{1,7},{3,1},{5,3},{7,5},{8,14},{10,8},{12,... | collective-permute-start | bytes 1179656 | tf_op jit(solution)/shard_map/ppermute | solution.py:23
  39.3 23.7 %collective-permute-start.9 = (bf16[1536,128]{1,0:T(8,128)(2,1)}, bf16[1536,128]{1,0:T(8,128)(2,1)S(1)}, u32[]{:S(2)}, u32[]{:S(2)}) collective-permute-start(bf16[1536,128]{1,0:T(8,128)(2,1)} %collective-permute-done.5.refs_10_), channel_id=1, source_target_pairs={{0,2},{2,4},{4,6},{6,0},{1,3},{3,5},{5,7},{7,1},{8,10},{10,12},{12... | collective-permute-start | bytes 1179656 | tf_op jit(solution)/shard_map/ppermute | solution.py:23
  40.2 16.9 %all-to-all-start.2 = ((f32[8,48,128]{2,1,0:T(8,128)}), f32[8,48,128]{2,1,0:T(8,128)S(1)}, u32[]{:S(2)}, u32[]{:S(2)}) async-start(f32[8,48,128]{2,1,0:T(8,128)} %shard_map.89), calls=%async_computation.2 | async-start | bytes 393216 | tf_op jit(solution)/shard_map/all_to_all | solution.py:27
  48.4 15.3 %collective-permute-start.3 = (bf16[1536,128]{1,0:T(8,128)(2,1)S(1)}, bf16[1536,128]{1,0:T(8,128)(2,1)S(1)}, u32[]{:S(2)}, u32[]{:S(2)}) collective-permute-start(bf16[1536,128]{1,0:T(8,128)(2,1)S(1)} %get-tuple-element.59.act0_ref.refs_0_), channel_id=1, source_target_pairs={{0,1},{1,0},{2,3},{3,2},{4,5},{5,4},{6,7},{7,6},{8,9},{9,8},{10,11... | collective-permute-start | bytes 1179656 | tf_op jit(solution)/shard_map/ppermute | solution.py:23
  58.0 6.4 %collective-permute-start.13 = (bf16[1536,128]{1,0:T(8,128)(2,1)S(1)}, bf16[1536,128]{1,0:T(8,128)(2,1)S(1)}, u32[]{:S(2)}, u32[]{:S(2)}) collective-permute-start(bf16[1536,128]{1,0:T(8,128)(2,1)S(1)} %get-tuple-element.66.act1_ref.refs_8_), channel_id=1, source_target_pairs={{0,1},{1,0},{2,3},{3,2},{4,5},{5,4},{6,7},{7,6},{8,9},{9,8},{10,11... | collective-permute-start | bytes 1179656 | tf_op jit(solution)/shard_map/ppermute | solution.py:23
  63.2 7.1 %collective-permute-start.11 = (bf16[1536,128]{1,0:T(8,128)(2,1)}, bf16[1536,128]{1,0:T(8,128)(2,1)}, u32[]{:S(2)}, u32[]{:S(2)}) collective-permute-start(bf16[1536,128]{1,0:T(8,128)(2,1)} %collective-permute-done.4.refs_4_), channel_id=1, source_target_pairs={{0,1},{1,0},{2,3},{3,2},{4,5},{5,4},{6,7},{7,6},{8,9},{9,8},{10,11... | collective-permute-start | bytes 1179656 | tf_op jit(solution)/shard_map/ppermute | solution.py:23
  63.6 6.6 %collective-permute-start.12 = (bf16[1536,128]{1,0:T(8,128)(2,1)S(1)}, bf16[1536,128]{1,0:T(8,128)(2,1)}, u32[]{:S(2)}, u32[]{:S(2)}) collective-permute-start(bf16[1536,128]{1,0:T(8,128)(2,1)S(1)} %collective-permute-done.7.refs_6_), channel_id=1, source_target_pairs={{0,1},{1,0},{2,3},{3,2},{4,5},{5,4},{6,7},{7,6},{8,9},{9,8},{10,11... | collective-permute-start | bytes 1179656 | tf_op jit(solution)/shard_map/ppermute | solution.py:23
  63.7 6.6 %collective-permute-start.14 = (bf16[1536,128]{1,0:T(8,128)(2,1)}, bf16[1536,128]{1,0:T(8,128)(2,1)S(1)}, u32[]{:S(2)}, u32[]{:S(2)}) collective-permute-start(bf16[1536,128]{1,0:T(8,128)(2,1)} %collective-permute-done.5.refs_10_), channel_id=1, source_target_pairs={{0,1},{1,0},{2,3},{3,2},{4,5},{5,4},{6,7},{7,6},{8,9},{9,8},{10,11... | collective-permute-start | bytes 1179656 | tf_op jit(solution)/shard_map/ppermute | solution.py:23
  64.3 6.0 %collective-permute-start.15 = (bf16[1536,128]{1,0:T(8,128)(2,1)S(1)}, bf16[1536,128]{1,0:T(8,128)(2,1)S(1)}, u32[]{:S(2)}, u32[]{:S(2)}) collective-permute-start(bf16[1536,128]{1,0:T(8,128)(2,1)S(1)} %collective-permute-done.8.refs_12_), channel_id=1, source_target_pairs={{0,1},{1,0},{2,3},{3,2},{4,5},{5,4},{6,7},{7,6},{8,9},{9,8},{10,11... | collective-permute-start | bytes 1179656 | tf_op jit(solution)/shard_map/ppermute | solution.py:23
  65.6 6.2 %collective-permute-start.16 = (bf16[1536,128]{1,0:T(8,128)(2,1)S(1)}, bf16[1536,128]{1,0:T(8,128)(2,1)}, u32[]{:S(2)}, u32[]{:S(2)}) collective-permute-start(bf16[1536,128]{1,0:T(8,128)(2,1)S(1)} %collective-permute-done.9.refs_14_), channel_id=1, source_target_pairs={{0,1},{1,0},{2,3},{3,2},{4,5},{5,4},{6,7},{7,6},{8,9},{9,8},{10,11... | collective-permute-start | bytes 1179656 | tf_op jit(solution)/shard_map/ppermute | solution.py:23
  66.0 13.5 %all-to-all-start.3 = ((f32[16,48,128]{2,1,0:T(8,128)}), f32[16,48,128]{2,1,0:T(8,128)S(1)}, u32[]{:S(2)}, u32[]{:S(2)}) async-start(f32[16,48,128]{2,1,0:T(8,128)} %shard_map.90), calls=%async_computation.3 | async-start | bytes 786432 | tf_op jit(solution)/shard_map/all_to_all | solution.py:27
  81.0 37.6 %collective-permute-start.17 = (bf16[3072,128]{1,0:T(8,128)(2,1)}, bf16[3072,128]{1,0:T(8,128)(2,1)}, u32[]{:S(2)}, u32[]{:S(2)}) collective-permute-start(bf16[3072,128]{1,0:T(8,128)(2,1)} %get-tuple-element.70), channel_id=1, source_target_pairs={{0,2},{2,4},{4,6},{6,0},{1,3},{3,5},{5,7},{7,1},{8,10},{10,12},{12... | collective-permute-start | bytes 2359304 | tf_op jit(solution)/shard_map/ppermute | solution.py:23
  81.1 37.4 %collective-permute-start.18 = (bf16[3072,128]{1,0:T(8,128)(2,1)}, bf16[3072,128]{1,0:T(8,128)(2,1)}, u32[]{:S(2)}, u32[]{:S(2)}) collective-permute-start(bf16[3072,128]{1,0:T(8,128)(2,1)} %get-tuple-element.71), channel_id=1, source_target_pairs={{0,4},{2,6},{4,0},{6,2},{1,5},{3,7},{5,1},{7,3},{8,12},{10,14},{12... | collective-permute-start | bytes 2359304 | tf_op jit(solution)/shard_map/ppermute | solution.py:23
  83.0 35.9 %collective-permute-start.19 = (bf16[3072,128]{1,0:T(8,128)(2,1)}, bf16[3072,128]{1,0:T(8,128)(2,1)}, u32[]{:S(2)}, u32[]{:S(2)}) collective-permute-start(bf16[3072,128]{1,0:T(8,128)(2,1)} %get-tuple-element.72), channel_id=1, source_target_pairs={{0,6},{2,0},{4,2},{6,4},{1,7},{3,1},{5,3},{7,5},{8,14},{10,8},{12,... | collective-permute-start | bytes 2359304 | tf_op jit(solution)/shard_map/ppermute | solution.py:23
  87.3 16.0 %all-to-all-start.4 = ((f32[32,8,128]{2,1,0:T(8,128)}), f32[32,8,128]{2,1,0:T(8,128)S(1)}, u32[]{:S(2)}, u32[]{:S(2)}) async-start(f32[32,8,128]{2,1,0:T(8,128)} %bitcast.10), calls=%async_computation.4 | async-start | bytes 262144 | tf_op jit(solution)/shard_map/all_to_all | solution.py:27
  104.0 17.7 %all-to-all-start.5 = ((f32[32,8,128]{2,1,0:T(8,128)}), f32[32,8,128]{2,1,0:T(8,128)S(1)}, u32[]{:S(2)}, u32[]{:S(2)}) async-start(f32[32,8,128]{2,1,0:T(8,128)} %shard_map.97), calls=%async_computation.5 | async-start | bytes 262144 | tf_op jit(solution)/shard_map/all_to_all | solution.py:27
  (17 other events, 154.9 us)

commit v4 on v3

--- a/solution.py
+++ b/solution.py
@@ -322,7 +322,7 @@
 def basis_rows(place, own, other, inverse):
     return call(
         basis_kernel,
-        [out((RANK, D)), out((HALF, 128))],
+        [far_out((RANK, D)), out((HALF, 128))],
         1e3,
         in_specs=[pl.BlockSpec(memory_space=pltpu.SMEM)] + [pl.BlockSpec()] * 3,
     )(place, own, other, inverse)
@@ -367,8 +367,8 @@
     )(s, inverse, packed, merged)
 
 
-def grad_kernel(place_ref, cot_ref, weight_ref, cot_side_ref, weight_side_ref, *refs):
-    out_refs, rows = refs[:-1], refs[-1]
+def grad_kernel(half, place_ref, cot_ref, weight_ref, cot_side_ref, weight_side_ref, *refs):
+    out_refs, rows = refs[-1 - NY : -1], refs[-1]
 
     @pl.when(pl.program_id(0) == 0)
     def _():
@@ -382,42 +382,74 @@
 
     weight = jnp.concatenate([weight_ref[...], weight_side_ref[...]], axis=1)
     part = dot(weight, rows[...]).astype(BF16)
-    for k, ref in enumerate(out_refs):
-        ref[...] = part[:, k * BLOCK : (k + 1) * BLOCK]
-
-
-def grad_parts(place, cot, cot_side, weight, weight_side):
+    mine, up, far, down = (part[:, k * BLOCK : (k + 1) * BLOCK] for k in range(NY))
+    joined = (far, down, up) if half == 0 else (up, far, down)
+    for ref, value in zip(out_refs, (mine, *joined)):
+        ref[...] = value
+
+
+def grad_parts(place, cot, cot_side, weight, weight_side, half, before=()):
     whole = pl.BlockSpec(cot.shape, lambda i: (0, 0))
-    tile = pl.BlockSpec((TILE, COLS), lambda i: (i, 0))
-    return call(
-        grad_kernel,
-        [far_out((D, BLOCK), BF16)] * NY,
-        1e3,
-        grid=(D // TILE,),
-        pins=(1, 3),
-        in_specs=[pl.BlockSpec(memory_space=pltpu.SMEM), whole, tile, whole, tile],
-        out_specs=[pl.BlockSpec((TILE, BLOCK), lambda i: (i, 0))] * NY,
+    tile = pl.BlockSpec((PART, COLS), lambda i: (i + half * 2, 0))
+    return call(
+        functools.partial(grad_kernel, half),
+        [far_out((D, BLOCK), BF16)] * 3 + [far_out((HALF, BLOCK), BF16)],
+        1e3,
+        grid=(2,),
+        pins=(1, 3) + tuple(range(5, 5 + len(before))),
+        in_specs=[pl.BlockSpec(memory_space=pltpu.SMEM), whole, tile, whole, tile]
+        + [pl.BlockSpec(memory_space=pl.ANY)] * len(before),
+        out_specs=[pl.BlockSpec((PART, BLOCK), lambda i: (i + half * 2, 0))] * 3
+        + [pl.BlockSpec((PART, BLOCK), lambda i: (i, 0))],
         scratch_shapes=[pltpu.VMEM((2 * COLS, NY * BLOCK), BF16)],
-    )(place, cot, weight, cot_side, weight_side)
-
-
-def add_kernel(*refs):
-    total = refs[0][...].astype(F32)
-    for ref in refs[1:NY]:
-        total += ref[...].astype(F32)
-    refs[NY][...] = total.astype(BF16).T
-
-
-def add_four(*parts):
+        input_output_aliases={5 + n: n for n in range(len(before))},
+    )(place, cot, weight, cot_side, weight_side, *before)
+
+
+def join_kernel(a_ref, b_ref, c_ref, d_ref, up_ref, down_ref):
+    up_ref[...] = (a_ref[...].astype(F32) + b_ref[...].astype(F32)).astype(BF16)
+    down_ref[...] = (c_ref[...].astype(F32) + d_ref[...].astype(F32)).astype(BF16)
+
+
+def join(up, got_plus, down, got_minus):
+    first = pl.BlockSpec((HALF, BLOCK), lambda i: (0, 0))
+    second = pl.BlockSpec((HALF, BLOCK), lambda i: (1, 0))
+    return call(
+        join_kernel,
+        [far_out((HALF, BLOCK), BF16)] * 2,
+        1e3,
+        grid=(1,),
+        pins=(0, 2),
+        in_specs=[first, first, first, second],
+        out_specs=[first, first],
+    )(up, got_plus, down, got_minus)
+
+
+def add_kernel(mine_ref, plus_ref, minus_ref, up_ref, down_ref, out_ref):
+    step = pl.program_id(0)
+
+    def store(*refs):
+        total = refs[0][...].astype(F32)
+        for ref in refs[1:]:
+            total += ref[...].astype(F32)
+        out_ref[...] = total.astype(BF16).T
+
+    pl.when(step == 0)(lambda: store(mine_ref, minus_ref, up_ref))
+    pl.when(step == 1)(lambda: store(mine_ref, plus_ref, down_ref))
+
+
+def add_three(mine, got_plus, got_minus, got_up, got_down):
+    first = pl.BlockSpec((HALF, BLOCK), lambda i: (0, 0))
+    second = pl.BlockSpec((HALF, BLOCK), lambda i: (1, 0))
     return call(
         add_kernel,
         far_out((BLOCK, D), BF16),
         1e3,
         grid=(2,),
         pins=(0,),
-        in_specs=[pl.BlockSpec((HALF, BLOCK), lambda i: (i, 0))] * NY,
+        in_specs=[pl.BlockSpec((HALF, BLOCK), lambda i: (i, 0)), second, first, first, first],
         out_specs=pl.BlockSpec((BLOCK, HALF), lambda i: (0, i)),
-    )(*parts)
+    )(mine, got_plus, got_minus, got_up, got_down)
 
 
 def after(values, *earlier):
@@ -440,17 +472,22 @@
     keep, p_send = p_rows(place, t, own0, own1, fq)
     p_send = pair_sum(keep, side(p_send)).reshape(16, 48, 128)
 
-    mine, *rest = grad_parts(place, cot_later, cot_side, weight, weight_side)
+    inputs = (place, cot_later, cot_side, weight, weight_side)
+    *first, up = grad_parts(*inputs, 0)
+    mine = first[0]
 
     go0, go1 = after([own0, own1], t)
     low1, high0 = ring(go1, "y", NY, 1), ring(go0, "y", NY, 3)
     (p_plane,) = after([exchange(p_send, PLANE)], mine)
     p_sum = sum_spread(p_plane, NZ)
-    go0, go1, far_go0, far_go1 = after([own0, own1, high0, low1], p_sum)
     low0, high1 = ring(go0, "y", NY, 1), ring(go1, "y", NY, 3)
+    far_go0, far_go1 = after([high0, low1], p_sum)
     far0, far1 = ring(far_go0, "y", NY, 3), ring(far_go1, "y", NY, 1)
 
     p_z = exchange(p_sum, "z")
+    first = after(first, p_sum)
+    mine, plus, minus, down = grad_parts(*inputs, 1, first)
+    (p_z,) = after([p_z], mine)
     p_half = sum_spread(p_z, 16)
     p = exchange(p_half, PLANE).reshape(PART, 128)
     later = after([low0, high0, far0, low1, high1, far1], p_half)
@@ -464,19 +501,22 @@
     (p,) = after([p], merged)
     p_other = side(p)
 
-    rest = after(rest, merged)
-    parts = [ring(value, "y", NY, k) for k, value in zip((1, 2, 3), rest)]
-    input_grad = add_four(mine, *parts)
+    plus, minus = after([plus, minus], merged)
+    got_plus, got_minus = ring(plus, "y", NY, 1), ring(minus, "y", NY, 3)
 
     s_send = s_rows(place, p, merged, jnp.zeros((256, 128), F32), 0)
     s_send = s_rows(place, p_other, merged, s_send, 1)
     s = exchange(s_send.reshape(N_DP, 8, 128), DP)
     p, p_other = after([p, p_other], s_send)
     inverse = inverse_rows(p, p_other)
-    (s,) = after([s], inverse)
+    (up,) = after([up], inverse)
+    up, down = join(up, got_plus, down, got_minus)
+    (s,) = after([s], inverse, up)
+    got_up, got_down = ring(up, "y", NY, 1), ring(down, "y", NY, 3)
+    input_grad = add_three(mine, got_plus, got_minus, got_up, got_down)
     basis, packed = basis_rows(place, p, p_other, inverse)
     s = exchange(sum_spread(s, N_DP), DP).reshape(256, 128)
-    (inverse,) = after([inverse], input_grad, basis)
+    (inverse,) = after([inverse], basis, input_grad)
     q_factor, feedback_new = last(s, inverse, packed, merged)
     return (
         input_grad[None],

time: 126 us -> 120 us (0.952)
  waiting for transfers between devices: 22.4 us -> 12.5 us
  Pallas kernels: 41.3 us -> 44.7 us
    all_to_all x6, waiting for transfers between devices: 14.7 us -> 7.1 us  [exchange(): return lax.all_to_all(value, axes, 0, 0, tiled=True)]
    pallas_call x15 -> x17, Pallas kernels: 41.3 us -> 44.7 us  [call(): made(*(held(v, where[n]) if n in where else v for n, v in enumerate(args)))]
    ppermute x21 -> x22, waiting for transfers between devices: 7.71 us -> 5.44 us  [ring(): lax.ppermute(value, axis, [(i, (i + shift) % size) for i in range(size)])]
    ppermute x21 -> x22, starting transfers between devices: 25.7 us -> 26.3 us  [ring(): lax.ppermute(value, axis, [(i, (i + shift) % size) for i in range(size)])]
    unnamed x28 -> x22, local copies, waits for them, and re-layouts: 3.13 us -> 2.63 us
  transfers between devices with their start and end apart: 27 -> 28, of which waited for: 9 -> 8; matrix products, arithmetic and copies ran while one was open for 0% -> 0% of each run, Pallas kernels for 28% -> 33%
where the time goes in v4:
time: 120 us; the launch traced here: 119 us
  starting transfers between devices  57.9 us (48%)
  Pallas kernels  44.7 us (37%)
  waiting for transfers between devices  12.5 us (10%)
  local copies, waits for them, and re-layouts  2.64 us (2%)
    pallas_call x17, Pallas kernels, call(): made(*(held(v, where[n]) if n in where else v for n, v in enumerate(args)))  44.7 us
    all_to_all x6, starting transfers between devices, exchange(): return lax.all_to_all(value, axes, 0, 0, tiled=True)  31.6 us
    ppermute x22, starting transfers between devices, ring(): lax.ppermute(value, axis, [(i, (i + shift) % size) for i in range(size)])  26.3 us
    all_to_all x6, waiting for transfers between devices, exchange(): return lax.all_to_all(value, axes, 0, 0, tiled=True)  7.1 us
    ppermute x22, waiting for transfers between devices, ring(): lax.ppermute(value, axis, [(i, (i + shift) % size) for i in range(size)])  5.44 us
    unnamed x22, local copies, waits for them, and re-layouts  2.63 us
  transfers between devices with their start and end apart: 28, of which 8 were waited for; matrix products, arithmetic and copies ran while one was open for 0% of the time, Pallas kernels for 33%

profile of v4, /device:TPU:1, one launch (start us, length us, event | category | flops | bytes accessed | tf_op | source)
XLA Modules:
  0.0 118.7 jit_solution(23618669082625782)
XLA Ops:
  0.6 2.2 %shard_map.84 = f32[8,64,128]{2,1,0:T(8,128)} custom-call(bf16[1024,384]{1,0:T(8,128)(2,1)} %bitcast.19, f32[64,384]{1,0:T(8,128)} %bitcast.30), custom_call_target="tpu_custom_call" | custom-call | flops 1000 | bytes 1000 | tf_op jit(solution)/shard_map/pallas_call | solution.py:50
  2.9 3.2 %collective-permute-start.1 = (bf16[3072,384]{1,0:T(8,128)(2,1)}, bf16[3072,384]{1,0:T(8,128)(2,1)}, u32[]{:S(2)}, u32[]{:S(2)}) collective-permute-start(bf16[3072,384]{1,0:T(8,128)(2,1)} %weight_ref.1), channel_id=1, source_target_pairs={{0,1},{1,0},{2,3},{3,2},{4,5},{5,4},{6,7},{7,6},{8,9},{9,8},{10,11... | collective-permute-start | bytes 7077896 | tf_op jit(solution)/shard_map/ppermute | solution.py:23
  6.1 3.4 %all-to-all-start = ((f32[8,64,128]{2,1,0:T(8,128)}), f32[8,64,128]{2,1,0:T(8,128)S(1)}, u32[]{:S(2)}, u32[]{:S(2)}) async-start(f32[8,64,128]{2,1,0:T(8,128)} %shard_map.84), calls=%async_computation | async-start | bytes 524288 | tf_op jit(solution)/shard_map/all_to_all | solution.py:27
  9.7 3.9 %shard_map.86 = (f32[1536,128]{1,0:T(8,128)}, bf16[1536,128]{1,0:T(8,128)(2,1)S(1)}, bf16[1536,128]{1,0:T(8,128)(2,1)S(1)}) custom-call(bf16[2,1536,384]{2,1,0:T(8,128)(2,1)} %bitcast.26, f32[64,384]{1,0:T(8,128)} %bitcast.31, bf16[128,3072]{1,0:T(8,128)(2,1)} %bitcast.24, bf16[128,3072]{1,0:T(8,128)(2,1)} %bitcast.25), custom_call_target="tpu_custom_call" | custom-call | flops 1000 | bytes 1000 | tf_op jit(solution)/shard_map/pallas_call | solution.py:50
  13.6 2.3 %all-to-all-done.t_ref = f32[8,64,128]{2,1,0:T(8,128)S(1)} async-done(((f32[8,64,128]{2,1,0:T(8,128)}), f32[8,64,128]{2,1,0:T(8,128)S(1)}, u32[]{:S(2)}, u32[]{:S(2)}) %all-to-all-start) | async-done | bytes 262176 | tf_op jit(solution)/shard_map/all_to_all | solution.py:27
  15.9 2.3 %shard_map.87 = (f32[768,128]{1,0:T(8,128)S(1)}, f32[768,128]{1,0:T(8,128)S(1)}) custom-call(s32[2]{0:T(128)S(1)} %pad_add_fusion.place_ref, f32[8,64,128]{2,1,0:T(8,128)S(1)} %all-to-all-done.t_ref, bf16[1536,128]{1,0:T(8,128)(2,1)S(1)} %get-tuple-element.70.act0_ref.refs_0_, bf16[1536,128]{1,0:T(8,128)(2,1)S(1)} %get-tuple-element.78.act1_ref.refs_8_, ...), custom_call_target="tpu_custom_call" | custom-call | flops 1000 | bytes 1000 | tf_op jit(solution)/shard_map/pallas_call | solution.py:50
  21.7 5.5 %all-to-all-start.1 = ((f32[16,48,128]{2,1,0:T(8,128)}), f32[16,48,128]{2,1,0:T(8,128)S(1)}, u32[]{:S(2)}, u32[]{:S(2)}) async-start(f32[16,48,128]{2,1,0:T(8,128)} %bitcast.28), calls=%async_computation.1 | async-start | bytes 786432 | tf_op jit(solution)/shard_map/all_to_all | solution.py:27
  29.9 4.3 %shard_map.85 = (bf16[3072,128]{1,0:T(8,128)(2,1)}, bf16[3072,128]{1,0:T(8,128)(2,1)}, bf16[3072,128]{1,0:T(8,128)(2,1)}, bf16[1536,128]{1,0:T(8,128)(2,1)}) custom-call(s32[2]{0:T(128)S(1)} %pad_add_fusion.place_ref, bf16[1024,384]{1,0:T(8,128)(2,1)} %bitcast.21, bf16[3072,384]{1,0:T(8,128)(2,1)S(1)} %copy-done, ...), custom_call_target="tpu_custom_call" | custom-call | flops 1000 | bytes 1000 | tf_op jit(solution)/shard_map/pallas_call | solution.py:50
  37.6 8.2 %all-to-all-start.2 = ((f32[8,48,128]{2,1,0:T(8,128)}), f32[8,48,128]{2,1,0:T(8,128)S(1)}, u32[]{:S(2)}, u32[]{:S(2)}) async-start(f32[8,48,128]{2,1,0:T(8,128)} %shard_map.89), calls=%async_computation.2 | async-start | bytes 393216 | tf_op jit(solution)/shard_map/all_to_all | solution.py:27
  45.8 3.4 %collective-permute-start.13 = (bf16[1536,128]{1,0:T(8,128)(2,1)S(1)}, bf16[1536,128]{1,0:T(8,128)(2,1)}, u32[]{:S(2)}, u32[]{:S(2)}) collective-permute-start(bf16[1536,128]{1,0:T(8,128)(2,1)S(1)} %get-tuple-element.78.act1_ref.refs_8_), channel_id=1, source_target_pairs={{0,1},{1,0},{2,3},{3,2},{4,5},{5,4},{6,7},{7,6},{8,9},{9,8},{10,11... | collective-permute-start | bytes 1179656 | tf_op jit(solution)/shard_map/ppermute | solution.py:23
  49.2 4.3 %shard_map.90 = (bf16[3072,128]{1,0:T(8,128)(2,1)}, bf16[3072,128]{1,0:T(8,128)(2,1)}, bf16[3072,128]{1,0:T(8,128)(2,1)}, bf16[1536,128]{1,0:T(8,128)(2,1)}) custom-call(s32[2]{0:T(128)S(1)} %pad_add_fusion.place_ref, bf16[1024,384]{1,0:T(8,128)(2,1)} %bitcast.22, ...), custom_call_target="tpu_custom_call", output_to_operand_aliasing={{0}: (5, {}), {1}: (6, {}), {2}: (7, {})} | custom-call | flops 1000 | bytes 1000 | tf_op jit(solution)/shard_map/pallas_call | solution.py:50
  55.3 4.4 %collective-permute-start.3 = (bf16[1536,128]{1,0:T(8,128)(2,1)S(1)}, bf16[1536,128]{1,0:T(8,128)(2,1)S(1)}, u32[]{:S(2)}, u32[]{:S(2)}) collective-permute-start(bf16[1536,128]{1,0:T(8,128)(2,1)S(1)} %get-tuple-element.70.act0_ref.refs_0_), channel_id=1, source_target_pairs={{0,1},{1,0},{2,3},{3,2},{4,5},{5,4},{6,7},{7,6},{8,9},{9,8},{10,11... | collective-permute-start | bytes 1179656 | tf_op jit(solution)/shard_map/ppermute | solution.py:23
  62.2 4.7 %all-to-all-start.3 = ((f32[16,48,128]{2,1,0:T(8,128)}), f32[16,48,128]{2,1,0:T(8,128)S(1)}, u32[]{:S(2)}, u32[]{:S(2)}) async-start(f32[16,48,128]{2,1,0:T(8,128)} %shard_map.91), calls=%async_computation.3 | async-start | bytes 786432 | tf_op jit(solution)/shard_map/all_to_all | solution.py:27
  68.7 6.6 %shard_map.92.merged_ref = bf16[2,1536,384]{2,1,0:T(8,128)(2,1)S(1)} custom-call(s32[2]{0:T(128)S(1)} %pad_add_fusion.place_ref, bf16[1024,384]{1,0:T(8,128)(2,1)} %bitcast.23, bf16[2,1536,384]{2,1,0:T(8,128)(2,1)} %bitcast.27, bf16[1536,128]{1,0:T(8,128)(2,1)} %copy-done.3, bf16[1536,128]{1,0:T(8,128)(2,1)} %copy-done.5, ...), custom_call_target="tpu_custom_call" | custom-call | flops 15000000512 | bytes 1000 | tf_op jit(solution)/shard_map/pallas_call | solution.py:50
  82.2 5.1 %all-to-all-start.4 = ((f32[32,8,128]{2,1,0:T(8,128)}), f32[32,8,128]{2,1,0:T(8,128)S(1)}, u32[]{:S(2)}, u32[]{:S(2)}) async-start(f32[32,8,128]{2,1,0:T(8,128)} %bitcast.10), calls=%async_computation.4 | async-start | bytes 262144 | tf_op jit(solution)/shard_map/all_to_all | solution.py:27
  87.3 3.6 %shard_map.95.inverse_ref = f32[128,128]{1,0:T(8,128)S(1)} custom-call(f32[768,128]{1,0:T(8,128)S(1)} %bitcast.16, f32[768,128]{1,0:T(8,128)S(1)} %collective-permute-done.19.p_ref.other_ref), custom_call_target="tpu_custom_call" | custom-call | flops 1000 | bytes 1000 | tf_op jit(solution)/shard_map/pallas_call | solution.py:50
  91.0 4.6 %collective-permute-done.17.b_ref.plus_ref = bf16[3072,128]{1,0:T(8,128)(2,1)} collective-permute-done((bf16[3072,128]{1,0:T(8,128)(2,1)}, bf16[3072,128]{1,0:T(8,128)(2,1)}, u32[]{:S(2)}, u32[]{:S(2)}) %collective-permute-start.17) | collective-permute-done | bytes 786464 | tf_op jit(solution)/shard_map/ppermute | solution.py:23
  95.6 2.3 %shard_map.96 = (bf16[1536,128]{1,0:T(8,128)(2,1)}, bf16[1536,128]{1,0:T(8,128)(2,1)}) custom-call(bf16[1536,128]{1,0:T(8,128)(2,1)} %get-tuple-element.88.a_ref, bf16[3072,128]{1,0:T(8,128)(2,1)} %collective-permute-done.17.b_ref.plus_ref, bf16[1536,128]{1,0:T(8,128)(2,1)} %get-tuple-element.89.c_ref, bf16[3072,128]{1,0:T(8,128)(2,1)} %collective-permute-done.18.d_ref.minus_ref), custom_call_target="tpu_custom_call" | custom-call | flops 1000 | bytes 1000 | tf_op jit(solution)/shard_map/pallas_call | solution.py:50
  98.6 2.0 %collective-permute-start.21 = (bf16[1536,128]{1,0:T(8,128)(2,1)}, bf16[1536,128]{1,0:T(8,128)(2,1)}, u32[]{:S(2)}, u32[]{:S(2)}) collective-permute-start(bf16[1536,128]{1,0:T(8,128)(2,1)} %get-tuple-element.91), channel_id=1, source_target_pairs={{0,6},{2,0},{4,2},{6,4},{1,7},{3,1},{5,3},{7,5},{8,14},{10,8},{12,... | collective-permute-start | bytes 1179656 | tf_op jit(solution)/shard_map/ppermute | solution.py:23
  101.3 4.8 %all-to-all-start.5 = ((f32[32,8,128]{2,1,0:T(8,128)}), f32[32,8,128]{2,1,0:T(8,128)S(1)}, u32[]{:S(2)}, u32[]{:S(2)}) async-start(f32[32,8,128]{2,1,0:T(8,128)} %shard_map.99), calls=%async_computation.5 | async-start | bytes 262144 | tf_op jit(solution)/shard_map/all_to_all | solution.py:27
  106.1 2.8 %shard_map.98 = (f32[64,3072]{1,0:T(8,128)}, f32[1536,128]{1,0:T(8,128)S(1)}) custom-call(s32[2]{0:T(128)S(1)} %pad_add_fusion.place_ref, f32[768,128]{1,0:T(8,128)S(1)} %bitcast.17, f32[768,128]{1,0:T(8,128)S(1)} %collective-permute-done.19.p_ref.other_ref, f32[128,128]{1,0:T(8,128)S(1)} %shard_map.95.inverse_ref), custom_call_target="tpu_custom_call" | custom-call | flops 1000 | bytes 1000 | tf_op jit(solution)/shard_map/pallas_call | solution.py:50
  109.9 2.7 %shard_map.97 = bf16[128,3072]{1,0:T(8,128)(2,1)} custom-call(bf16[3072,128]{1,0:T(8,128)(2,1)} %get-tuple-element.66.mine_ref, bf16[3072,128]{1,0:T(8,128)(2,1)} %collective-permute-done.17.b_ref.plus_ref, bf16[3072,128]{1,0:T(8,128)(2,1)} %collective-permute-done.18.d_ref.minus_ref, bf16[1536,128]{1,0:T(8,128)(2,1)} %collective-permute-done.20.up_ref, ...), custom_call_target="tpu_custom_call" | custom-call | flops 1000 | bytes 1000 | tf_op jit(solution)/shard_map/pallas_call | solution.py:50
  112.6 2.6 %all-to-all-done.5 = f32[32,8,128]{2,1,0:T(8,128)S(1)} async-done(((f32[32,8,128]{2,1,0:T(8,128)}), f32[32,8,128]{2,1,0:T(8,128)S(1)}, u32[]{:S(2)}, u32[]{:S(2)}) %all-to-all-start.5) | async-done | bytes 131104 | tf_op jit(solution)/shard_map/all_to_all | solution.py:27
  115.2 3.5 %shard_map.100 = (f32[64,384]{1,0:T(8,128)}, bf16[2,1536,384]{2,1,0:T(8,128)(2,1)}) custom-call(f32[256,128]{1,0:T(8,128)S(1)} %bitcast.18, f32[128,128]{1,0:T(8,128)S(1)} %shard_map.95.inverse_ref, f32[1536,128]{1,0:T(8,128)S(1)} %copy-done.2, bf16[2,1536,384]{2,1,0:T(8,128)(2,1)S(1)} %shard_map.92.merged_ref), custom_call_target="tpu_custom_call" | custom-call | flops 1000 | bytes 1000 | tf_op jit(solution)/shard_map/pallas_call | solution.py:50
  (73 shorter events, 25.0 us)
Async XLA Ops:
  2.9 27.0 %collective-permute-start.1 = (bf16[3072,384]{1,0:T(8,128)(2,1)}, bf16[3072,384]{1,0:T(8,128)(2,1)}, u32[]{:S(2)}, u32[]{:S(2)}) collective-permute-start(bf16[3072,384]{1,0:T(8,128)(2,1)} %weight_ref.1), channel_id=1, source_target_pairs={{0,1},{1,0},{2,3},{3,2},{4,5},{5,4},{6,7},{7,6},{8,9},{9,8},{10,11... | collective-permute-start | bytes 7077896 | tf_op jit(solution)/shard_map/ppermute | solution.py:23
  6.1 9.8 %all-to-all-start = ((f32[8,64,128]{2,1,0:T(8,128)}), f32[8,64,128]{2,1,0:T(8,128)S(1)}, u32[]{:S(2)}, u32[]{:S(2)}) async-start(f32[8,64,128]{2,1,0:T(8,128)} %shard_map.84), calls=%async_computation | async-start | bytes 524288 | tf_op jit(solution)/shard_map/all_to_all | solution.py:27
  9.5 19.0 %collective-permute-start = (bf16[1024,384]{1,0:T(8,128)(2,1)}, bf16[1024,384]{1,0:T(8,128)(2,1)}, u32[]{:S(2)}, u32[]{:S(2)}) collective-permute-start(bf16[1024,384]{1,0:T(8,128)(2,1)} %bitcast.20), channel_id=1, source_target_pairs={{0,1},{1,0},{2,3},{3,2},{4,5},{5,4},{6,7},{7,6},{8,9},{9,8},{10,11... | collective-permute-start | bytes 2359304 | tf_op jit(solution)/shard_map/ppermute | solution.py:23
  19.4 16.8 %collective-permute-start.5 = (bf16[1536,128]{1,0:T(8,128)(2,1)S(1)}, bf16[1536,128]{1,0:T(8,128)(2,1)}, u32[]{:S(2)}, u32[]{:S(2)}) collective-permute-start(bf16[1536,128]{1,0:T(8,128)(2,1)S(1)} %get-tuple-element.70.act0_ref.refs_0_), channel_id=1, source_target_pairs={{0,6},{2,0},{4,2},{6,4},{1,7},{3,1},{5,3},{7,5},{8,14},{10,8},{12,... | collective-permute-start | bytes 1179656 | tf_op jit(solution)/shard_map/ppermute | solution.py:23
  20.3 15.9 %collective-permute-start.6 = (bf16[1536,128]{1,0:T(8,128)(2,1)S(1)}, bf16[1536,128]{1,0:T(8,128)(2,1)}, u32[]{:S(2)}, u32[]{:S(2)}) collective-permute-start(bf16[1536,128]{1,0:T(8,128)(2,1)S(1)} %get-tuple-element.78.act1_ref.refs_8_), channel_id=1, source_target_pairs={{0,2},{2,4},{4,6},{6,0},{1,3},{3,5},{5,7},{7,1},{8,10},{10,12},{12... | collective-permute-start | bytes 1179656 | tf_op jit(solution)/shard_map/ppermute | solution.py:23
  21.7 13.8 %all-to-all-start.1 = ((f32[16,48,128]{2,1,0:T(8,128)}), f32[16,48,128]{2,1,0:T(8,128)S(1)}, u32[]{:S(2)}, u32[]{:S(2)}) async-start(f32[16,48,128]{2,1,0:T(8,128)} %bitcast.28), calls=%async_computation.1 | async-start | bytes 786432 | tf_op jit(solution)/shard_map/all_to_all | solution.py:27
  27.1 28.2 %collective-permute-start.4 = (bf16[1536,128]{1,0:T(8,128)(2,1)S(1)}, bf16[1536,128]{1,0:T(8,128)(2,1)}, u32[]{:S(2)}, u32[]{:S(2)}) collective-permute-start(bf16[1536,128]{1,0:T(8,128)(2,1)S(1)} %get-tuple-element.70.act0_ref.refs_0_), channel_id=1, source_target_pairs={{0,2},{2,4},{4,6},{6,0},{1,3},{3,5},{5,7},{7,1},{8,10},{10,12},{12... | collective-permute-start | bytes 1179656 | tf_op jit(solution)/shard_map/ppermute | solution.py:23
  28.5 31.2 %collective-permute-start.8 = (bf16[1536,128]{1,0:T(8,128)(2,1)S(1)}, bf16[1536,128]{1,0:T(8,128)(2,1)}, u32[]{:S(2)}, u32[]{:S(2)}) collective-permute-start(bf16[1536,128]{1,0:T(8,128)(2,1)S(1)} %get-tuple-element.78.act1_ref.refs_8_), channel_id=1, source_target_pairs={{0,6},{2,0},{4,2},{6,4},{1,7},{3,1},{5,3},{7,5},{8,14},{10,8},{12,... | collective-permute-start | bytes 1179656 | tf_op jit(solution)/shard_map/ppermute | solution.py:23
  36.2 23.6 %collective-permute-start.7 = (bf16[1536,128]{1,0:T(8,128)(2,1)}, bf16[1536,128]{1,0:T(8,128)(2,1)}, u32[]{:S(2)}, u32[]{:S(2)}) collective-permute-start(bf16[1536,128]{1,0:T(8,128)(2,1)} %collective-permute-done.5.refs_4_), channel_id=1, source_target_pairs={{0,6},{2,0},{4,2},{6,4},{1,7},{3,1},{5,3},{7,5},{8,14},{10,8},{12,... | collective-permute-start | bytes 1179656 | tf_op jit(solution)/shard_map/ppermute | solution.py:23
  37.6 22.1 %collective-permute-start.9 = (bf16[1536,128]{1,0:T(8,128)(2,1)}, bf16[1536,128]{1,0:T(8,128)(2,1)}, u32[]{:S(2)}, u32[]{:S(2)}) collective-permute-start(bf16[1536,128]{1,0:T(8,128)(2,1)} %collective-permute-done.6.refs_10_), channel_id=1, source_target_pairs={{0,2},{2,4},{4,6},{6,0},{1,3},{3,5},{5,7},{7,1},{8,10},{10,12},{12... | collective-permute-start | bytes 1179656 | tf_op jit(solution)/shard_map/ppermute | solution.py:23
  37.6 16.9 %all-to-all-start.2 = ((f32[8,48,128]{2,1,0:T(8,128)}), f32[8,48,128]{2,1,0:T(8,128)S(1)}, u32[]{:S(2)}, u32[]{:S(2)}) async-start(f32[8,48,128]{2,1,0:T(8,128)} %shard_map.89), calls=%async_computation.2 | async-start | bytes 393216 | tf_op jit(solution)/shard_map/all_to_all | solution.py:27
  45.8 14.6 %collective-permute-start.13 = (bf16[1536,128]{1,0:T(8,128)(2,1)S(1)}, bf16[1536,128]{1,0:T(8,128)(2,1)}, u32[]{:S(2)}, u32[]{:S(2)}) collective-permute-start(bf16[1536,128]{1,0:T(8,128)(2,1)S(1)} %get-tuple-element.78.act1_ref.refs_8_), channel_id=1, source_target_pairs={{0,1},{1,0},{2,3},{3,2},{4,5},{5,4},{6,7},{7,6},{8,9},{9,8},{10,11... | collective-permute-start | bytes 1179656 | tf_op jit(solution)/shard_map/ppermute | solution.py:23
  59.8 7.0 %collective-permute-start.11 = (bf16[1536,128]{1,0:T(8,128)(2,1)}, bf16[1536,128]{1,0:T(8,128)(2,1)S(1)}, u32[]{:S(2)}, u32[]{:S(2)}) collective-permute-start(bf16[1536,128]{1,0:T(8,128)(2,1)} %collective-permute-done.5.refs_4_), channel_id=1, source_target_pairs={{0,1},{1,0},{2,3},{3,2},{4,5},{5,4},{6,7},{7,6},{8,9},{9,8},{10,11... | collective-permute-start | bytes 1179656 | tf_op jit(solution)/shard_map/ppermute | solution.py:23
  60.3 6.6 %collective-permute-start.12 = (bf16[1536,128]{1,0:T(8,128)(2,1)}, bf16[1536,128]{1,0:T(8,128)(2,1)S(1)}, u32[]{:S(2)}, u32[]{:S(2)}) collective-permute-start(bf16[1536,128]{1,0:T(8,128)(2,1)} %collective-permute-done.7.refs_6_), channel_id=1, source_target_pairs={{0,1},{1,0},{2,3},{3,2},{4,5},{5,4},{6,7},{7,6},{8,9},{9,8},{10,11... | collective-permute-start | bytes 1179656 | tf_op jit(solution)/shard_map/ppermute | solution.py:23
  60.4 6.5 %collective-permute-start.14 = (bf16[1536,128]{1,0:T(8,128)(2,1)}, bf16[1536,128]{1,0:T(8,128)(2,1)S(1)}, u32[]{:S(2)}, u32[]{:S(2)}) collective-permute-start(bf16[1536,128]{1,0:T(8,128)(2,1)} %collective-permute-done.6.refs_10_), channel_id=1, source_target_pairs={{0,1},{1,0},{2,3},{3,2},{4,5},{5,4},{6,7},{7,6},{8,9},{9,8},{10,11... | collective-permute-start | bytes 1179656 | tf_op jit(solution)/shard_map/ppermute | solution.py:23
  61.1 5.9 %collective-permute-start.15 = (bf16[1536,128]{1,0:T(8,128)(2,1)}, bf16[1536,128]{1,0:T(8,128)(2,1)S(1)}, u32[]{:S(2)}, u32[]{:S(2)}) collective-permute-start(bf16[1536,128]{1,0:T(8,128)(2,1)} %collective-permute-done.8.refs_12_), channel_id=1, source_target_pairs={{0,1},{1,0},{2,3},{3,2},{4,5},{5,4},{6,7},{7,6},{8,9},{9,8},{10,11... | collective-permute-start | bytes 1179656 | tf_op jit(solution)/shard_map/ppermute | solution.py:23
  61.9 6.8 %collective-permute-start.16 = (bf16[1536,128]{1,0:T(8,128)(2,1)}, bf16[1536,128]{1,0:T(8,128)(2,1)}, u32[]{:S(2)}, u32[]{:S(2)}) collective-permute-start(bf16[1536,128]{1,0:T(8,128)(2,1)} %collective-permute-done.9.refs_14_), channel_id=1, source_target_pairs={{0,1},{1,0},{2,3},{3,2},{4,5},{5,4},{6,7},{7,6},{8,9},{9,8},{10,11... | collective-permute-start | bytes 1179656 | tf_op jit(solution)/shard_map/ppermute | solution.py:23
  62.2 15.8 %all-to-all-start.3 = ((f32[16,48,128]{2,1,0:T(8,128)}), f32[16,48,128]{2,1,0:T(8,128)S(1)}, u32[]{:S(2)}, u32[]{:S(2)}) async-start(f32[16,48,128]{2,1,0:T(8,128)} %shard_map.91), calls=%async_computation.3 | async-start | bytes 786432 | tf_op jit(solution)/shard_map/all_to_all | solution.py:27
  75.3 20.3 %collective-permute-start.17 = (bf16[3072,128]{1,0:T(8,128)(2,1)}, bf16[3072,128]{1,0:T(8,128)(2,1)}, u32[]{:S(2)}, u32[]{:S(2)}) collective-permute-start(bf16[3072,128]{1,0:T(8,128)(2,1)} %get-tuple-element.82), channel_id=1, source_target_pairs={{0,2},{2,4},{4,6},{6,0},{1,3},{3,5},{5,7},{7,1},{8,10},{10,12},{12... | collective-permute-start | bytes 2359304 | tf_op jit(solution)/shard_map/ppermute | solution.py:23
  76.7 18.9 %collective-permute-start.18 = (bf16[3072,128]{1,0:T(8,128)(2,1)}, bf16[3072,128]{1,0:T(8,128)(2,1)}, u32[]{:S(2)}, u32[]{:S(2)}) collective-permute-start(bf16[3072,128]{1,0:T(8,128)(2,1)} %get-tuple-element.83), channel_id=1, source_target_pairs={{0,6},{2,0},{4,2},{6,4},{1,7},{3,1},{5,3},{7,5},{8,14},{10,8},{12,... | collective-permute-start | bytes 2359304 | tf_op jit(solution)/shard_map/ppermute | solution.py:23
  82.2 18.4 %all-to-all-start.4 = ((f32[32,8,128]{2,1,0:T(8,128)}), f32[32,8,128]{2,1,0:T(8,128)S(1)}, u32[]{:S(2)}, u32[]{:S(2)}) async-start(f32[32,8,128]{2,1,0:T(8,128)} %bitcast.10), calls=%async_computation.4 | async-start | bytes 262144 | tf_op jit(solution)/shard_map/all_to_all | solution.py:27
  97.9 11.9 %collective-permute-start.20 = (bf16[1536,128]{1,0:T(8,128)(2,1)}, bf16[1536,128]{1,0:T(8,128)(2,1)}, u32[]{:S(2)}, u32[]{:S(2)}) collective-permute-start(bf16[1536,128]{1,0:T(8,128)(2,1)} %get-tuple-element.90), channel_id=1, source_target_pairs={{0,2},{2,4},{4,6},{6,0},{1,3},{3,5},{5,7},{7,1},{8,10},{10,12},{12... | collective-permute-start | bytes 1179656 | tf_op jit(solution)/shard_map/ppermute | solution.py:23
  98.6 11.3 %collective-permute-start.21 = (bf16[1536,128]{1,0:T(8,128)(2,1)}, bf16[1536,128]{1,0:T(8,128)(2,1)}, u32[]{:S(2)}, u32[]{:S(2)}) collective-permute-start(bf16[1536,128]{1,0:T(8,128)(2,1)} %get-tuple-element.91), channel_id=1, source_target_pairs={{0,6},{2,0},{4,2},{6,4},{1,7},{3,1},{5,3},{7,5},{8,14},{10,8},{12,... | collective-permute-start | bytes 1179656 | tf_op jit(solution)/shard_map/ppermute | solution.py:23
  101.3 14.0 %all-to-all-start.5 = ((f32[32,8,128]{2,1,0:T(8,128)}), f32[32,8,128]{2,1,0:T(8,128)S(1)}, u32[]{:S(2)}, u32[]{:S(2)}) async-start(f32[32,8,128]{2,1,0:T(8,128)} %shard_map.99), calls=%async_computation.5 | async-start | bytes 262144 | tf_op jit(solution)/shard_map/all_to_all | solution.py:27
  (15 other events, 127.0 us)

commit v5 on v4

--- a/solution.py
+++ b/solution.py
@@ -12,6 +12,7 @@
 NX, NY, NZ, NC = 4, 4, 8, 2
 DP, MP, PLANE = ("z", "x"), ("y", "c"), ("x", "y")
 N_DP = NZ * NX
+BACK = list(range(N_DP))[::-1]
 HALF, COLS, RANK, BLOCK, D = 1536, 384, 64, 128, 3072
 PART = HALF // 2
 TILE = 512
@@ -23,8 +24,9 @@
     return lax.ppermute(value, axis, [(i, (i + shift) % size) for i in range(size)])
 
 
-def exchange(value, axes):
-    return lax.all_to_all(value, axes, 0, 0, tiled=True)
+def exchange(value, axes, order=None):
+    groups = None if order is None else [order]
+    return lax.all_to_all(value, axes, 0, 0, axis_index_groups=groups, tiled=True)
 
 
 def call(kernel, outs, flops, grid=None, pins=(), near=(), prefetch=False, **kwargs):
@@ -501,12 +503,12 @@
     (p,) = after([p], merged)
     p_other = side(p)
 
-    plus, minus = after([plus, minus], merged)
+    plus, minus = after([plus, minus], *sides)
     got_plus, got_minus = ring(plus, "y", NY, 1), ring(minus, "y", NY, 3)
 
     s_send = s_rows(place, p, merged, jnp.zeros((256, 128), F32), 0)
     s_send = s_rows(place, p_other, merged, s_send, 1)
-    s = exchange(s_send.reshape(N_DP, 8, 128), DP)
+    s = exchange(s_send.reshape(N_DP, 8, 128), DP, BACK)
     p, p_other = after([p, p_other], s_send)
     inverse = inverse_rows(p, p_other)
     (up,) = after([up], inverse)
@@ -515,7 +517,7 @@
     got_up, got_down = ring(up, "y", NY, 1), ring(down, "y", NY, 3)
     input_grad = add_three(mine, got_plus, got_minus, got_up, got_down)
     basis, packed = basis_rows(place, p, p_other, inverse)
-    s = exchange(sum_spread(s, N_DP), DP).reshape(256, 128)
+    s = exchange(sum_spread(s, N_DP), DP, BACK).reshape(256, 128)
     (inverse,) = after([inverse], basis, input_grad)
     q_factor, feedback_new = last(s, inverse, packed, merged)
     return (

time: 120 us -> 120 us (level)
  starting transfers between devices: 57.9 us -> 61.9 us
  waiting for transfers between devices: 12.5 us -> 8.98 us
    all_to_all x6, starting transfers between devices: 31.6 us -> 38.6 us  [exchange(): lax.all_to_all(value, axes, 0, 0, axis_index_groups=groups, tiled=True)]
    ppermute x22, waiting for transfers between devices: 5.44 us -> 1.13 us  [ring(): lax.ppermute(value, axis, [(i, (i + shift) % size) for i in range(size)])]
    ppermute x22, starting transfers between devices: 26.3 us -> 23.4 us  [ring(): lax.ppermute(value, axis, [(i, (i + shift) % size) for i in range(size)])]
    unnamed x22 -> x24, local copies, waits for them, and re-layouts: 2.63 us -> 2.58 us
  transfers between devices with their start and end apart: 28 -> 28, of which waited for: 8 -> 7; matrix products, arithmetic and copies ran while one was open for 0% -> 0% of each run, Pallas kernels for 33% -> 33%
where the time goes in v5:
time: 120 us; the launch traced here: 119 us
  starting transfers between devices  61.9 us (52%)
  Pallas kernels  44.7 us (37%)
  waiting for transfers between devices  8.98 us (7%)
  local copies, waits for them, and re-layouts  2.59 us (2%)
    pallas_call x17, Pallas kernels, call(): made(*(held(v, where[n]) if n in where else v for n, v in enumerate(args)))  44.7 us
    all_to_all x6, starting transfers between devices, exchange(): lax.all_to_all(value, axes, 0, 0, axis_index_groups=groups, tiled=True)  38.6 us
    ppermute x22, starting transfers between devices, ring(): lax.ppermute(value, axis, [(i, (i + shift) % size) for i in range(size)])  23.4 us
    all_to_all x6, waiting for transfers between devices, exchange(): lax.all_to_all(value, axes, 0, 0, axis_index_groups=groups, tiled=True)  7.85 us
    unnamed x24, local copies, waits for them, and re-layouts  2.58 us
  transfers between devices with their start and end apart: 28, of which 7 were waited for; matrix products, arithmetic and copies ran while one was open for 0% of the time, Pallas kernels for 33%

profile of v5, /device:TPU:1, one launch (start us, length us, event | category | flops | bytes accessed | tf_op | source)
XLA Modules:
  0.0 119.1 jit_solution(118253573144009200)
XLA Ops:
  0.6 2.2 %shard_map.84 = f32[8,64,128]{2,1,0:T(8,128)} custom-call(bf16[1024,384]{1,0:T(8,128)(2,1)} %bitcast.19, f32[64,384]{1,0:T(8,128)} %bitcast.30), custom_call_target="tpu_custom_call" | custom-call | flops 1000 | bytes 1000 | tf_op jit(solution)/shard_map/pallas_call | solution.py:52
  2.9 3.2 %collective-permute-start.1 = (bf16[3072,384]{1,0:T(8,128)(2,1)}, bf16[3072,384]{1,0:T(8,128)(2,1)}, u32[]{:S(2)}, u32[]{:S(2)}) collective-permute-start(bf16[3072,384]{1,0:T(8,128)(2,1)} %weight_ref.1), channel_id=1, source_target_pairs={{0,1},{1,0},{2,3},{3,2},{4,5},{5,4},{6,7},{7,6},{8,9},{9,8},{10,11... | collective-permute-start | bytes 7077896 | tf_op jit(solution)/shard_map/ppermute | solution.py:24
  6.1 3.4 %all-to-all-start = ((f32[8,64,128]{2,1,0:T(8,128)}), f32[8,64,128]{2,1,0:T(8,128)S(1)}, u32[]{:S(2)}, u32[]{:S(2)}) async-start(f32[8,64,128]{2,1,0:T(8,128)} %shard_map.84), calls=%async_computation | async-start | bytes 524288 | tf_op jit(solution)/shard_map/all_to_all | solution.py:29
  9.7 3.9 %shard_map.86 = (f32[1536,128]{1,0:T(8,128)}, bf16[1536,128]{1,0:T(8,128)(2,1)S(1)}, bf16[1536,128]{1,0:T(8,128)(2,1)S(1)}) custom-call(bf16[2,1536,384]{2,1,0:T(8,128)(2,1)} %bitcast.26, f32[64,384]{1,0:T(8,128)} %bitcast.31, bf16[128,3072]{1,0:T(8,128)(2,1)} %bitcast.24, bf16[128,3072]{1,0:T(8,128)(2,1)} %bitcast.25), custom_call_target="tpu_custom_call" | custom-call | flops 1000 | bytes 1000 | tf_op jit(solution)/shard_map/pallas_call | solution.py:52
  13.6 2.3 %all-to-all-done.t_ref = f32[8,64,128]{2,1,0:T(8,128)S(1)} async-done(((f32[8,64,128]{2,1,0:T(8,128)}), f32[8,64,128]{2,1,0:T(8,128)S(1)}, u32[]{:S(2)}, u32[]{:S(2)}) %all-to-all-start) | async-done | bytes 262176 | tf_op jit(solution)/shard_map/all_to_all | solution.py:29
  15.9 2.3 %shard_map.87 = (f32[768,128]{1,0:T(8,128)S(1)}, f32[768,128]{1,0:T(8,128)S(1)}) custom-call(s32[2]{0:T(128)S(1)} %pad_add_fusion.place_ref, f32[8,64,128]{2,1,0:T(8,128)S(1)} %all-to-all-done.t_ref, bf16[1536,128]{1,0:T(8,128)(2,1)S(1)} %get-tuple-element.83.act0_ref.refs_0_, bf16[1536,128]{1,0:T(8,128)(2,1)S(1)} %get-tuple-element.84.act1_ref.refs_8_, ...), custom_call_target="tpu_custom_call" | custom-call | flops 1000 | bytes 1000 | tf_op jit(solution)/shard_map/pallas_call | solution.py:52
  21.7 5.5 %all-to-all-start.1 = ((f32[16,48,128]{2,1,0:T(8,128)}), f32[16,48,128]{2,1,0:T(8,128)S(1)}, u32[]{:S(2)}, u32[]{:S(2)}) async-start(f32[16,48,128]{2,1,0:T(8,128)} %bitcast.28), calls=%async_computation.1 | async-start | bytes 786432 | tf_op jit(solution)/shard_map/all_to_all | solution.py:29
  29.9 4.3 %shard_map.85 = (bf16[3072,128]{1,0:T(8,128)(2,1)}, bf16[3072,128]{1,0:T(8,128)(2,1)}, bf16[3072,128]{1,0:T(8,128)(2,1)}, bf16[1536,128]{1,0:T(8,128)(2,1)}) custom-call(s32[2]{0:T(128)S(1)} %pad_add_fusion.place_ref, bf16[1024,384]{1,0:T(8,128)(2,1)} %bitcast.21, bf16[3072,384]{1,0:T(8,128)(2,1)S(1)} %copy-done, ...), custom_call_target="tpu_custom_call" | custom-call | flops 1000 | bytes 1000 | tf_op jit(solution)/shard_map/pallas_call | solution.py:52
  36.2 1.5 %collective-permute-start.6 = (bf16[1536,128]{1,0:T(8,128)(2,1)}, bf16[1536,128]{1,0:T(8,128)(2,1)}, u32[]{:S(2)}, u32[]{:S(2)}) collective-permute-start(bf16[1536,128]{1,0:T(8,128)(2,1)} %collective-permute-done.4.refs_4_), channel_id=1, source_target_pairs={{0,6},{2,0},{4,2},{6,4},{1,7},{3,1},{5,3},{7,5},{8,14},{10,8},{12,... | collective-permute-start | bytes 1179656 | tf_op jit(solution)/shard_map/ppermute | solution.py:24
  37.6 8.2 %all-to-all-start.2 = ((f32[8,48,128]{2,1,0:T(8,128)}), f32[8,48,128]{2,1,0:T(8,128)S(1)}, u32[]{:S(2)}, u32[]{:S(2)}) async-start(f32[8,48,128]{2,1,0:T(8,128)} %shard_map.89), calls=%async_computation.2 | async-start | bytes 393216 | tf_op jit(solution)/shard_map/all_to_all | solution.py:29
  45.8 4.4 %shard_map.90 = (bf16[3072,128]{1,0:T(8,128)(2,1)}, bf16[3072,128]{1,0:T(8,128)(2,1)}, bf16[3072,128]{1,0:T(8,128)(2,1)}, bf16[1536,128]{1,0:T(8,128)(2,1)}) custom-call(s32[2]{0:T(128)S(1)} %pad_add_fusion.place_ref, bf16[1024,384]{1,0:T(8,128)(2,1)} %bitcast.22, ...), custom_call_target="tpu_custom_call", output_to_operand_aliasing={{0}: (5, {}), {1}: (6, {}), {2}: (7, {})} | custom-call | flops 1000 | bytes 1000 | tf_op jit(solution)/shard_map/pallas_call | solution.py:52
  50.2 4.3 %all-to-all-done.2.in_ref = f32[8,48,128]{2,1,0:T(8,128)S(1)} async-done(((f32[8,48,128]{2,1,0:T(8,128)}), f32[8,48,128]{2,1,0:T(8,128)S(1)}, u32[]{:S(2)}, u32[]{:S(2)}) %all-to-all-start.2) | async-done | bytes 196640 | tf_op jit(solution)/shard_map/all_to_all | solution.py:29
  55.3 4.5 %collective-permute-start.9 = (bf16[1536,128]{1,0:T(8,128)(2,1)}, bf16[1536,128]{1,0:T(8,128)(2,1)S(1)}, u32[]{:S(2)}, u32[]{:S(2)}) collective-permute-start(bf16[1536,128]{1,0:T(8,128)(2,1)} %collective-permute-done.3.refs_2_), channel_id=1, source_target_pairs={{0,1},{1,0},{2,3},{3,2},{4,5},{5,4},{6,7},{7,6},{8,9},{9,8},{10,11... | collective-permute-start | bytes 1179656 | tf_op jit(solution)/shard_map/ppermute | solution.py:24
  63.8 4.7 %all-to-all-start.3 = ((f32[16,48,128]{2,1,0:T(8,128)}), f32[16,48,128]{2,1,0:T(8,128)S(1)}, u32[]{:S(2)}, u32[]{:S(2)}) async-start(f32[16,48,128]{2,1,0:T(8,128)} %shard_map.91), calls=%async_computation.3 | async-start | bytes 786432 | tf_op jit(solution)/shard_map/all_to_all | solution.py:29
  72.1 6.6 %shard_map.92.merged_ref = bf16[2,1536,384]{2,1,0:T(8,128)(2,1)S(1)} custom-call(s32[2]{0:T(128)S(1)} %pad_add_fusion.place_ref, bf16[1024,384]{1,0:T(8,128)(2,1)} %bitcast.23, bf16[2,1536,384]{2,1,0:T(8,128)(2,1)} %bitcast.27, bf16[1536,128]{1,0:T(8,128)(2,1)} %copy-done.3, bf16[1536,128]{1,0:T(8,128)(2,1)} %copy-done.11, ...), custom_call_target="tpu_custom_call" | custom-call | flops 15000000512 | bytes 1000 | tf_op jit(solution)/shard_map/pallas_call | solution.py:52
  81.1 1.8 %shard_map.94 = f32[256,128]{1,0:T(8,128)} custom-call(s32[2]{0:T(128)S(1)} %pad_add_fusion.place_ref, f32[768,128]{1,0:T(8,128)S(1)} %collective-permute-done.19.p_ref.other_ref, bf16[2,1536,384]{2,1,0:T(8,128)(2,1)S(1)} %shard_map.92.merged_ref, f32[256,128]{1,0:T(8,128)S(1)} %shard_map.93.before_ref), custom_call_target="tpu_custom_call" | custom-call | flops 1000 | bytes 1000 | tf_op jit(solution)/shard_map/pallas_call | solution.py:52
  82.9 7.7 %all-to-all-start.4 = ((f32[32,8,128]{2,1,0:T(8,128)}), f32[32,8,128]{2,1,0:T(8,128)S(1)}, u32[]{:S(2)}, u32[]{:S(2)}) async-start(f32[32,8,128]{2,1,0:T(8,128)} %bitcast.10), calls=%async_computation.4 | async-start | bytes 262144 | tf_op jit(solution)/shard_map/all_to_all | solution.py:29
  90.6 3.6 %shard_map.95.inverse_ref = f32[128,128]{1,0:T(8,128)S(1)} custom-call(f32[768,128]{1,0:T(8,128)S(1)} %bitcast.16, f32[768,128]{1,0:T(8,128)S(1)} %collective-permute-done.19.p_ref.other_ref), custom_call_target="tpu_custom_call" | custom-call | flops 1000 | bytes 1000 | tf_op jit(solution)/shard_map/pallas_call | solution.py:52
  94.2 2.3 %shard_map.96 = (bf16[1536,128]{1,0:T(8,128)(2,1)}, bf16[1536,128]{1,0:T(8,128)(2,1)}) custom-call(bf16[1536,128]{1,0:T(8,128)(2,1)} %get-tuple-element.88.a_ref, bf16[3072,128]{1,0:T(8,128)(2,1)} %collective-permute-done.15.b_ref.plus_ref, bf16[1536,128]{1,0:T(8,128)(2,1)} %get-tuple-element.89.c_ref, bf16[3072,128]{1,0:T(8,128)(2,1)} %collective-permute-done.16.d_ref.minus_ref), custom_call_target="tpu_custom_call" | custom-call | flops 1000 | bytes 1000 | tf_op jit(solution)/shard_map/pallas_call | solution.py:52
  96.6 2.7 %collective-permute-start.21 = (bf16[1536,128]{1,0:T(8,128)(2,1)}, bf16[1536,128]{1,0:T(8,128)(2,1)}, u32[]{:S(2)}, u32[]{:S(2)}) collective-permute-start(bf16[1536,128]{1,0:T(8,128)(2,1)} %get-tuple-element.91), channel_id=1, source_target_pairs={{0,6},{2,0},{4,2},{6,4},{1,7},{3,1},{5,3},{7,5},{8,14},{10,8},{12,... | collective-permute-start | bytes 1179656 | tf_op jit(solution)/shard_map/ppermute | solution.py:24
  99.9 9.2 %all-to-all-start.5 = ((f32[32,8,128]{2,1,0:T(8,128)}), f32[32,8,128]{2,1,0:T(8,128)S(1)}, u32[]{:S(2)}, u32[]{:S(2)}) async-start(f32[32,8,128]{2,1,0:T(8,128)} %shard_map.99), calls=%async_computation.5 | async-start | bytes 262144 | tf_op jit(solution)/shard_map/all_to_all | solution.py:29
  109.2 2.8 %shard_map.98 = (f32[64,3072]{1,0:T(8,128)}, f32[1536,128]{1,0:T(8,128)S(1)}) custom-call(s32[2]{0:T(128)S(1)} %pad_add_fusion.place_ref, f32[768,128]{1,0:T(8,128)S(1)} %bitcast.17, f32[768,128]{1,0:T(8,128)S(1)} %collective-permute-done.19.p_ref.other_ref, f32[128,128]{1,0:T(8,128)S(1)} %shard_map.95.inverse_ref), custom_call_target="tpu_custom_call" | custom-call | flops 1000 | bytes 1000 | tf_op jit(solution)/shard_map/pallas_call | solution.py:52
  112.9 2.7 %shard_map.97 = bf16[128,3072]{1,0:T(8,128)(2,1)} custom-call(bf16[3072,128]{1,0:T(8,128)(2,1)} %get-tuple-element.66.mine_ref, bf16[3072,128]{1,0:T(8,128)(2,1)} %collective-permute-done.15.b_ref.plus_ref, bf16[3072,128]{1,0:T(8,128)(2,1)} %collective-permute-done.16.d_ref.minus_ref, bf16[1536,128]{1,0:T(8,128)(2,1)} %collective-permute-done.20.up_ref, ...), custom_call_target="tpu_custom_call" | custom-call | flops 1000 | bytes 1000 | tf_op jit(solution)/shard_map/pallas_call | solution.py:52
  115.6 3.5 %shard_map.100 = (f32[64,384]{1,0:T(8,128)}, bf16[2,1536,384]{2,1,0:T(8,128)(2,1)}) custom-call(f32[256,128]{1,0:T(8,128)S(1)} %bitcast.18, f32[128,128]{1,0:T(8,128)S(1)} %shard_map.95.inverse_ref, f32[1536,128]{1,0:T(8,128)S(1)} %copy-done.2, bf16[2,1536,384]{2,1,0:T(8,128)(2,1)S(1)} %shard_map.92.merged_ref), custom_call_target="tpu_custom_call" | custom-call | flops 1000 | bytes 1000 | tf_op jit(solution)/shard_map/pallas_call | solution.py:52
  (75 shorter events, 20.7 us)
Async XLA Ops:
  2.9 27.0 %collective-permute-start.1 = (bf16[3072,384]{1,0:T(8,128)(2,1)}, bf16[3072,384]{1,0:T(8,128)(2,1)}, u32[]{:S(2)}, u32[]{:S(2)}) collective-permute-start(bf16[3072,384]{1,0:T(8,128)(2,1)} %weight_ref.1), channel_id=1, source_target_pairs={{0,1},{1,0},{2,3},{3,2},{4,5},{5,4},{6,7},{7,6},{8,9},{9,8},{10,11... | collective-permute-start | bytes 7077896 | tf_op jit(solution)/shard_map/ppermute | solution.py:24
  6.1 9.8 %all-to-all-start = ((f32[8,64,128]{2,1,0:T(8,128)}), f32[8,64,128]{2,1,0:T(8,128)S(1)}, u32[]{:S(2)}, u32[]{:S(2)}) async-start(f32[8,64,128]{2,1,0:T(8,128)} %shard_map.84), calls=%async_computation | async-start | bytes 524288 | tf_op jit(solution)/shard_map/all_to_all | solution.py:29
  9.5 19.0 %collective-permute-start = (bf16[1024,384]{1,0:T(8,128)(2,1)}, bf16[1024,384]{1,0:T(8,128)(2,1)}, u32[]{:S(2)}, u32[]{:S(2)}) collective-permute-start(bf16[1024,384]{1,0:T(8,128)(2,1)} %bitcast.20), channel_id=1, source_target_pairs={{0,1},{1,0},{2,3},{3,2},{4,5},{5,4},{6,7},{7,6},{8,9},{9,8},{10,11... | collective-permute-start | bytes 2359304 | tf_op jit(solution)/shard_map/ppermute | solution.py:24
  19.4 16.8 %collective-permute-start.4 = (bf16[1536,128]{1,0:T(8,128)(2,1)S(1)}, bf16[1536,128]{1,0:T(8,128)(2,1)}, u32[]{:S(2)}, u32[]{:S(2)}) collective-permute-start(bf16[1536,128]{1,0:T(8,128)(2,1)S(1)} %get-tuple-element.83.act0_ref.refs_0_), channel_id=1, source_target_pairs={{0,6},{2,0},{4,2},{6,4},{1,7},{3,1},{5,3},{7,5},{8,14},{10,8},{12,... | collective-permute-start | bytes 1179656 | tf_op jit(solution)/shard_map/ppermute | solution.py:24
  20.3 15.9 %collective-permute-start.5 = (bf16[1536,128]{1,0:T(8,128)(2,1)S(1)}, bf16[1536,128]{1,0:T(8,128)(2,1)}, u32[]{:S(2)}, u32[]{:S(2)}) collective-permute-start(bf16[1536,128]{1,0:T(8,128)(2,1)S(1)} %get-tuple-element.84.act1_ref.refs_8_), channel_id=1, source_target_pairs={{0,2},{2,4},{4,6},{6,0},{1,3},{3,5},{5,7},{7,1},{8,10},{10,12},{12... | collective-permute-start | bytes 1179656 | tf_op jit(solution)/shard_map/ppermute | solution.py:24
  21.7 13.8 %all-to-all-start.1 = ((f32[16,48,128]{2,1,0:T(8,128)}), f32[16,48,128]{2,1,0:T(8,128)S(1)}, u32[]{:S(2)}, u32[]{:S(2)}) async-start(f32[16,48,128]{2,1,0:T(8,128)} %bitcast.28), calls=%async_computation.1 | async-start | bytes 786432 | tf_op jit(solution)/shard_map/all_to_all | solution.py:29
  27.1 28.2 %collective-permute-start.3 = (bf16[1536,128]{1,0:T(8,128)(2,1)S(1)}, bf16[1536,128]{1,0:T(8,128)(2,1)}, u32[]{:S(2)}, u32[]{:S(2)}) collective-permute-start(bf16[1536,128]{1,0:T(8,128)(2,1)S(1)} %get-tuple-element.83.act0_ref.refs_0_), channel_id=1, source_target_pairs={{0,2},{2,4},{4,6},{6,0},{1,3},{3,5},{5,7},{7,1},{8,10},{10,12},{12... | collective-permute-start | bytes 1179656 | tf_op jit(solution)/shard_map/ppermute | solution.py:24
  28.5 26.8 %collective-permute-start.7 = (bf16[1536,128]{1,0:T(8,128)(2,1)S(1)}, bf16[1536,128]{1,0:T(8,128)(2,1)}, u32[]{:S(2)}, u32[]{:S(2)}) collective-permute-start(bf16[1536,128]{1,0:T(8,128)(2,1)S(1)} %get-tuple-element.84.act1_ref.refs_8_), channel_id=1, source_target_pairs={{0,6},{2,0},{4,2},{6,4},{1,7},{3,1},{5,3},{7,5},{8,14},{10,8},{12,... | collective-permute-start | bytes 1179656 | tf_op jit(solution)/shard_map/ppermute | solution.py:24
  36.2 19.2 %collective-permute-start.6 = (bf16[1536,128]{1,0:T(8,128)(2,1)}, bf16[1536,128]{1,0:T(8,128)(2,1)}, u32[]{:S(2)}, u32[]{:S(2)}) collective-permute-start(bf16[1536,128]{1,0:T(8,128)(2,1)} %collective-permute-done.4.refs_4_), channel_id=1, source_target_pairs={{0,6},{2,0},{4,2},{6,4},{1,7},{3,1},{5,3},{7,5},{8,14},{10,8},{12,... | collective-permute-start | bytes 1179656 | tf_op jit(solution)/shard_map/ppermute | solution.py:24
  37.6 17.7 %collective-permute-start.8 = (bf16[1536,128]{1,0:T(8,128)(2,1)}, bf16[1536,128]{1,0:T(8,128)(2,1)}, u32[]{:S(2)}, u32[]{:S(2)}) collective-permute-start(bf16[1536,128]{1,0:T(8,128)(2,1)} %collective-permute-done.5.refs_10_), channel_id=1, source_target_pairs={{0,2},{2,4},{4,6},{6,0},{1,3},{3,5},{5,7},{7,1},{8,10},{10,12},{12... | collective-permute-start | bytes 1179656 | tf_op jit(solution)/shard_map/ppermute | solution.py:24
  37.6 16.9 %all-to-all-start.2 = ((f32[8,48,128]{2,1,0:T(8,128)}), f32[8,48,128]{2,1,0:T(8,128)S(1)}, u32[]{:S(2)}, u32[]{:S(2)}) async-start(f32[8,48,128]{2,1,0:T(8,128)} %shard_map.89), calls=%async_computation.2 | async-start | bytes 393216 | tf_op jit(solution)/shard_map/all_to_all | solution.py:29
  55.3 6.1 %collective-permute-start.9 = (bf16[1536,128]{1,0:T(8,128)(2,1)}, bf16[1536,128]{1,0:T(8,128)(2,1)S(1)}, u32[]{:S(2)}, u32[]{:S(2)}) collective-permute-start(bf16[1536,128]{1,0:T(8,128)(2,1)} %collective-permute-done.3.refs_2_), channel_id=1, source_target_pairs={{0,1},{1,0},{2,3},{3,2},{4,5},{5,4},{6,7},{7,6},{8,9},{9,8},{10,11... | collective-permute-start | bytes 1179656 | tf_op jit(solution)/shard_map/ppermute | solution.py:24
  60.3 8.1 %collective-permute-start.12 = (bf16[1536,128]{1,0:T(8,128)(2,1)}, bf16[1536,128]{1,0:T(8,128)(2,1)S(1)}, u32[]{:S(2)}, u32[]{:S(2)}) collective-permute-start(bf16[1536,128]{1,0:T(8,128)(2,1)} %collective-permute-done.5.refs_10_), channel_id=1, source_target_pairs={{0,1},{1,0},{2,3},{3,2},{4,5},{5,4},{6,7},{7,6},{8,9},{9,8},{10,11... | collective-permute-start | bytes 1179656 | tf_op jit(solution)/shard_map/ppermute | solution.py:24
  60.4 8.1 %collective-permute-start.13 = (bf16[1536,128]{1,0:T(8,128)(2,1)}, bf16[1536,128]{1,0:T(8,128)(2,1)S(1)}, u32[]{:S(2)}, u32[]{:S(2)}) collective-permute-start(bf16[1536,128]{1,0:T(8,128)(2,1)} %collective-permute-done.7.refs_12_), channel_id=1, source_target_pairs={{0,1},{1,0},{2,3},{3,2},{4,5},{5,4},{6,7},{7,6},{8,9},{9,8},{10,11... | collective-permute-start | bytes 1179656 | tf_op jit(solution)/shard_map/ppermute | solution.py:24
  61.4 7.1 %collective-permute-start.14 = (bf16[1536,128]{1,0:T(8,128)(2,1)}, bf16[1536,128]{1,0:T(8,128)(2,1)S(1)}, u32[]{:S(2)}, u32[]{:S(2)}) collective-permute-start(bf16[1536,128]{1,0:T(8,128)(2,1)} %collective-permute-done.8.refs_14_), channel_id=1, source_target_pairs={{0,1},{1,0},{2,3},{3,2},{4,5},{5,4},{6,7},{7,6},{8,9},{9,8},{10,11... | collective-permute-start | bytes 1179656 | tf_op jit(solution)/shard_map/ppermute | solution.py:24
  62.0 9.3 %collective-permute-start.17 = (bf16[1536,128]{1,0:T(8,128)(2,1)S(1)}, bf16[1536,128]{1,0:T(8,128)(2,1)S(1)}, u32[]{:S(2)}, u32[]{:S(2)}) collective-permute-start(bf16[1536,128]{1,0:T(8,128)(2,1)S(1)} %get-tuple-element.83.act0_ref.refs_0_), channel_id=1, source_target_pairs={{0,1},{1,0},{2,3},{3,2},{4,5},{5,4},{6,7},{7,6},{8,9},{9,8},{10,11... | collective-permute-start | bytes 1179656 | tf_op jit(solution)/shard_map/ppermute | solution.py:24
  63.4 8.6 %collective-permute-start.18 = (bf16[1536,128]{1,0:T(8,128)(2,1)S(1)}, bf16[1536,128]{1,0:T(8,128)(2,1)}, u32[]{:S(2)}, u32[]{:S(2)}) collective-permute-start(bf16[1536,128]{1,0:T(8,128)(2,1)S(1)} %get-tuple-element.84.act1_ref.refs_8_), channel_id=1, source_target_pairs={{0,1},{1,0},{2,3},{3,2},{4,5},{5,4},{6,7},{7,6},{8,9},{9,8},{10,11... | collective-permute-start | bytes 1179656 | tf_op jit(solution)/shard_map/ppermute | solution.py:24
  63.8 14.8 %all-to-all-start.3 = ((f32[16,48,128]{2,1,0:T(8,128)}), f32[16,48,128]{2,1,0:T(8,128)S(1)}, u32[]{:S(2)}, u32[]{:S(2)}) async-start(f32[16,48,128]{2,1,0:T(8,128)} %shard_map.91), calls=%async_computation.3 | async-start | bytes 786432 | tf_op jit(solution)/shard_map/all_to_all | solution.py:29
  68.5 25.7 %collective-permute-start.15 = (bf16[3072,128]{1,0:T(8,128)(2,1)}, bf16[3072,128]{1,0:T(8,128)(2,1)}, u32[]{:S(2)}, u32[]{:S(2)}) collective-permute-start(bf16[3072,128]{1,0:T(8,128)(2,1)} %get-tuple-element.80), channel_id=1, source_target_pairs={{0,2},{2,4},{4,6},{6,0},{1,3},{3,5},{5,7},{7,1},{8,10},{10,12},{12... | collective-permute-start | bytes 2359304 | tf_op jit(solution)/shard_map/ppermute | solution.py:24
  70.0 24.2 %collective-permute-start.16 = (bf16[3072,128]{1,0:T(8,128)(2,1)}, bf16[3072,128]{1,0:T(8,128)(2,1)}, u32[]{:S(2)}, u32[]{:S(2)}) collective-permute-start(bf16[3072,128]{1,0:T(8,128)(2,1)} %get-tuple-element.81), channel_id=1, source_target_pairs={{0,6},{2,0},{4,2},{6,4},{1,7},{3,1},{5,3},{7,5},{8,14},{10,8},{12,... | collective-permute-start | bytes 2359304 | tf_op jit(solution)/shard_map/ppermute | solution.py:24
  82.9 16.3 %all-to-all-start.4 = ((f32[32,8,128]{2,1,0:T(8,128)}), f32[32,8,128]{2,1,0:T(8,128)S(1)}, u32[]{:S(2)}, u32[]{:S(2)}) async-start(f32[32,8,128]{2,1,0:T(8,128)} %bitcast.10), calls=%async_computation.4 | async-start | bytes 262144 | tf_op jit(solution)/shard_map/all_to_all | solution.py:29
  96.6 16.3 %collective-permute-start.20 = (bf16[1536,128]{1,0:T(8,128)(2,1)}, bf16[1536,128]{1,0:T(8,128)(2,1)}, u32[]{:S(2)}, u32[]{:S(2)}) collective-permute-start(bf16[1536,128]{1,0:T(8,128)(2,1)} %get-tuple-element.90), channel_id=1, source_target_pairs={{0,2},{2,4},{4,6},{6,0},{1,3},{3,5},{5,7},{7,1},{8,10},{10,12},{12... | collective-permute-start | bytes 1179656 | tf_op jit(solution)/shard_map/ppermute | solution.py:24
  96.6 16.3 %collective-permute-start.21 = (bf16[1536,128]{1,0:T(8,128)(2,1)}, bf16[1536,128]{1,0:T(8,128)(2,1)}, u32[]{:S(2)}, u32[]{:S(2)}) collective-permute-start(bf16[1536,128]{1,0:T(8,128)(2,1)} %get-tuple-element.91), channel_id=1, source_target_pairs={{0,6},{2,0},{4,2},{6,4},{1,7},{3,1},{5,3},{7,5},{8,14},{10,8},{12,... | collective-permute-start | bytes 1179656 | tf_op jit(solution)/shard_map/ppermute | solution.py:24
  99.9 15.7 %all-to-all-start.5 = ((f32[32,8,128]{2,1,0:T(8,128)}), f32[32,8,128]{2,1,0:T(8,128)S(1)}, u32[]{:S(2)}, u32[]{:S(2)}) async-start(f32[32,8,128]{2,1,0:T(8,128)} %shard_map.99), calls=%async_computation.5 | async-start | bytes 262144 | tf_op jit(solution)/shard_map/all_to_all | solution.py:29
  (16 other events, 138.4 us)
